TPU v7x, 32 devices: a whole 2x2x4 slice. The times are simulated.
32 devices in a mesh: batch: 8 (over z, x), mod: 4 (over y, core).
Axes of the slice: x: 2, y: 2, z: 4, core: 2. Of those that a mesh axis runs over, the one named last changes fastest.
Arguments:
- text: bfloat16 [32, 256, 2048], P(('batch', 'mod')), may hold values from -6 to 6
- patches: bfloat16 [32, 256, 1664], P(('batch', 'mod')), may hold values from -6 to 6
- text_lengths: int32 [32], P('batch'), may hold values from 1 to 256, as said below
- patch_mask: int32 [32, 256], P('batch'), may hold values from 0 to 1, as said below
- cotangent: bfloat16 [32, 256, 2048], P(('batch', 'mod')), may hold values from -6 to 6
- gains: bfloat16 [3, 2048], P(None, ('batch', 'mod')), may hold values from 0.5 to 1.5
- w_qkv: bfloat16 [3, 2048, 2048], P(None, 'batch', 'mod'), may hold values from -0.125 to 0.125
- w_so: bfloat16 [2048, 2048], P('mod', 'batch'), may hold values from -1 to 1
- w_cq: bfloat16 [2048, 2048], P('batch', 'mod'), may hold values from -0.125 to 0.125
- w_ckv: bfloat16 [2, 2048, 2048], P(None, 'batch', 'mod'), may hold values from -0.125 to 0.125
- w_co: bfloat16 [2048, 2048], P('mod', 'batch'), may hold values from -1 to 1
- w_patch: bfloat16 [1664, 2048], P(('batch', 'mod')), may hold values from -0.15625 to 0.15625
- w_gu: bfloat16 [2, 2048, 5120], P(None, 'batch', 'mod'), may hold values from -0.125 to 0.125
- w_down: bfloat16 [5120, 2048], P('mod', 'batch'), may hold values from -0.078125 to 0.078125
Outputs:
- result: float32 [32, 256, 2048], P(('batch', 'mod'))
- d_text: float32 [32, 256, 2048], P(('batch', 'mod'))
- d_gains: float32 [3, 2048], P(None, ('batch', 'mod'))
- d_qkv: float32 [3, 2048, 2048], P(None, 'batch', 'mod')
- d_so: float32 [2048, 2048], P('mod', 'batch')
- d_cq: float32 [2048, 2048], P('batch', 'mod')
- d_ckv: float32 [2, 2048, 2048], P(None, 'batch', 'mod')
- d_co: float32 [2048, 2048], P('mod', 'batch')
- d_patch: float32 [1664, 2048], P(('batch', 'mod'))
- d_gu: float32 [2, 2048, 5120], P(None, 'batch', 'mod')
- d_down: float32 [5120, 2048], P('mod', 'batch')
Inputs may be any that keep to these rules, and one draw needn't show every extreme that they name: text_lengths[b] counts the valid text slots of item b, which come first; in every draw some item has all 256. `patch_mask`: 1 marks a patch that text may attend to; patch 0 of every item is 1.
All inputs are finite; a program needn't handle non-finite values.
Results may differ from a plain program's by a relative error of at most 0.024.
Values may be sent and summed in bfloat16 or wider, within the bound.
A program may use at most 320 MiB of HBM per device.

v0:
```python
import jax
import jax.numpy as jnp
from jax import lax
from jax.sharding import PartitionSpec as P

HD = 128


def rms_norm(values, gain):
    factor = lax.rsqrt(jnp.mean(values * values, axis=-1, keepdims=True) + 1e-06)
    return values * factor * gain


def norm_back(values, gain, grad_in):
    _, pullback = jax.vjp(rms_norm, values, gain)
    return pullback(grad_in)


def gelu_mix(gate, upward):
    return jax.nn.gelu(gate, approximate=True) * upward


def fetch_self(w_qkv, w_so):
    return (
        lax.all_gather(w_qkv, "batch", axis=1, tiled=True),
        lax.all_gather(w_so, "batch", axis=1, tiled=True),
    )


def fetch_cross(w_cq, w_ckv, w_co):
    return (
        lax.all_gather(w_cq, "batch", axis=0, tiled=True),
        lax.all_gather(w_ckv, "batch", axis=1, tiled=True),
        lax.all_gather(w_co, "batch", axis=1, tiled=True),
    )


def fetch_ffn(w_gu, w_down):
    return (
        lax.all_gather(w_gu, "batch", axis=1, tiled=True),
        lax.all_gather(w_down, "batch", axis=1, tiled=True),
    )


def rows_gather(normed):
    return lax.all_gather(normed.astype(jnp.bfloat16), "mod", axis=0, tiled=True)


def rows_sum(partial_out):
    return lax.psum_scatter(partial_out, "mod", scatter_dimension=0, tiled=True)


def grads_gather(grad_branch):
    return lax.all_gather(grad_branch.astype(jnp.bfloat16), "mod", axis=0, tiled=True)


def back_sum(partial_grad):
    return lax.psum_scatter(partial_grad, "mod", scatter_dimension=0, tiled=True)


def scores_of(query, keys, allowed):
    item_count, query_rows, columns = query.shape
    head_count = columns // HD
    query_heads = query.reshape(item_count, query_rows, head_count, HD)
    key_heads = keys.reshape(item_count, keys.shape[1], head_count, HD)
    raw_scores = jnp.einsum(
        "bqhe,bkhe->bhqk", query_heads, key_heads, preferred_element_type=jnp.float32
    ) * HD ** (-0.5)
    return jnp.where(allowed[:, None], raw_scores, -1e30)


def attend_forward(query, keys, values, allowed):
    item_count, query_rows, columns = query.shape
    head_count = columns // HD
    scores = scores_of(query, keys, allowed)
    row_max = jnp.max(scores, axis=-1, keepdims=True)
    weights = jnp.exp(scores - row_max)
    row_total = jnp.sum(weights, axis=-1, keepdims=True)
    probs = (weights / row_total).astype(jnp.bfloat16)
    value_heads = values.reshape(item_count, values.shape[1], head_count, HD)
    context = jnp.einsum("bhqk,bkhe->bqhe", probs, value_heads, preferred_element_type=jnp.float32)
    return (
        context.reshape(item_count, query_rows, columns).astype(jnp.bfloat16),
        row_max + jnp.log(row_total),
    )


def attend_backward(query, keys, values, allowed, log_total, grad_context):
    item_count, query_rows, columns = query.shape
    key_rows = keys.shape[1]
    head_count = columns // HD
    scale = HD ** (-0.5)
    probs = jnp.exp(scores_of(query, keys, allowed) - log_total)
    grad_heads = grad_context.reshape(item_count, query_rows, head_count, HD)
    query_heads = query.reshape(item_count, query_rows, head_count, HD)
    key_heads = keys.reshape(item_count, key_rows, head_count, HD)
    value_heads = values.reshape(item_count, key_rows, head_count, HD)
    grad_values = jnp.einsum(
        "bhqk,bqhe->bkhe",
        probs.astype(jnp.bfloat16),
        grad_heads,
        preferred_element_type=jnp.float32,
    )
    grad_probs = jnp.einsum(
        "bqhe,bkhe->bhqk", grad_heads, value_heads, preferred_element_type=jnp.float32
    )
    grad_scores = probs * (grad_probs - jnp.sum(probs * grad_probs, axis=-1, keepdims=True))
    grad_scores = grad_scores.astype(jnp.bfloat16)
    grad_query = (
        jnp.einsum("bhqk,bkhe->bqhe", grad_scores, key_heads, preferred_element_type=jnp.float32)
        * scale
    )
    grad_keys = (
        jnp.einsum("bhqk,bqhe->bkhe", grad_scores, query_heads, preferred_element_type=jnp.float32)
        * scale
    )
    return (
        grad_query.reshape(item_count, query_rows, columns).astype(jnp.bfloat16),
        grad_keys.reshape(item_count, key_rows, columns).astype(jnp.bfloat16),
        grad_values.reshape(item_count, key_rows, columns).astype(jnp.bfloat16),
    )


def local(
    text,
    patches,
    text_lengths,
    patch_mask,
    cotangent,
    gains,
    w_qkv,
    w_so,
    w_cq,
    w_ckv,
    w_co,
    w_patch,
    w_gu,
    w_down,
):
    own_items = text.shape[0]
    text_rows = text.shape[1]
    first_item = lax.axis_index("mod") * own_items
    own_lengths = lax.dynamic_slice_in_dim(text_lengths, first_item, own_items)
    positions = jnp.arange(text_rows)
    causal = (positions[None, None, :] <= positions[None, :, None]) & (
        positions[None, None, :] < text_lengths[:, None, None]
    )
    cross_allowed = (patch_mask > 0)[:, None, :]
    proj_weight, gain_all = (
        lax.all_gather(w_patch, ("batch", "mod"), axis=0, tiled=True),
        lax.all_gather(gains, ("batch", "mod"), axis=1, tiled=True),
    )
    gain_all = gain_all.astype(jnp.float32)
    x_zero = text.astype(jnp.float32)
    self_qkv, self_out = fetch_self(w_qkv, w_so)
    act_one = rows_gather(rms_norm(x_zero, gain_all[0]))
    qkv = jnp.einsum("gtd,jdc->jgtc", act_one, self_qkv, preferred_element_type=jnp.float32).astype(
        jnp.bfloat16
    )
    self_ctx, self_log = attend_forward(qkv[0], qkv[1], qkv[2], causal)
    x_one = x_zero + rows_sum(
        jnp.einsum("gtc,cd->gtd", self_ctx, self_out, preferred_element_type=jnp.float32)
    )
    cross_query_w, cross_kv_w, cross_out_w = fetch_cross(w_cq, w_ckv, w_co)
    act_two = rows_gather(rms_norm(x_one, gain_all[1]))
    cross_query = jnp.einsum(
        "gtd,dc->gtc", act_two, cross_query_w, preferred_element_type=jnp.float32
    ).astype(jnp.bfloat16)
    own_proj = jnp.einsum(
        "bpe,ed->bpd", patches, proj_weight, preferred_element_type=jnp.float32
    ).astype(jnp.bfloat16)
    proj_all = lax.all_gather(own_proj, "mod", axis=0, tiled=True)
    cross_kv = jnp.einsum(
        "gpd,jdc->jgpc", proj_all, cross_kv_w, preferred_element_type=jnp.float32
    ).astype(jnp.bfloat16)
    cross_ctx, cross_log = attend_forward(cross_query, cross_kv[0], cross_kv[1], cross_allowed)
    x_two = x_one + rows_sum(
        jnp.einsum("gtc,cd->gtd", cross_ctx, cross_out_w, preferred_element_type=jnp.float32)
    )
    gate_up_w, down_w = fetch_ffn(w_gu, w_down)
    act_three = rows_gather(rms_norm(x_two, gain_all[2]))
    gate_up = jnp.einsum("gtd,jdf->jgtf", act_three, gate_up_w, preferred_element_type=jnp.float32)
    hidden = gelu_mix(gate_up[0], gate_up[1]).astype(jnp.bfloat16)
    result = x_two + rows_sum(
        jnp.einsum("gtf,fd->gtd", hidden, down_w, preferred_element_type=jnp.float32)
    )
    valid = (positions[None, :] < own_lengths[:, None]).astype(jnp.float32)
    grad_result = cotangent.astype(jnp.float32) * valid[..., None]
    gate_up_w, down_w = fetch_ffn(w_gu, w_down)
    grad_branch = grads_gather(grad_result)
    grad_down = jnp.einsum("gtf,gtd->fd", hidden, grad_branch, preferred_element_type=jnp.float32)
    grad_hidden = jnp.einsum("gtd,fd->gtf", grad_branch, down_w, preferred_element_type=jnp.float32)
    _, mix_pull = jax.vjp(gelu_mix, gate_up[0], gate_up[1])
    grad_gate, grad_upward = mix_pull(grad_hidden)
    grad_mix = jnp.stack([grad_gate, grad_upward]).astype(jnp.bfloat16)
    grad_gate_up = jnp.einsum(
        "gtd,jgtf->jdf", act_three, grad_mix, preferred_element_type=jnp.float32
    )
    grad_act = back_sum(
        jnp.einsum("jgtf,jdf->gtd", grad_mix, gate_up_w, preferred_element_type=jnp.float32)
    )
    grad_inner, gain_grad_three = norm_back(x_two, gain_all[2], grad_act)
    grad_two = grad_result + grad_inner
    ffn_grads = (
        lax.psum_scatter(
            grad_gate_up.astype(jnp.bfloat16), "batch", scatter_dimension=1, tiled=True
        ).astype(jnp.float32),
        lax.psum_scatter(
            grad_down.astype(jnp.bfloat16), "batch", scatter_dimension=1, tiled=True
        ).astype(jnp.float32),
    )
    cross_query_w, cross_kv_w, cross_out_w = fetch_cross(w_cq, w_ckv, w_co)
    grad_branch = grads_gather(grad_two)
    grad_co_w = jnp.einsum(
        "gtc,gtd->cd", cross_ctx, grad_branch, preferred_element_type=jnp.float32
    )
    grad_ctx = jnp.einsum(
        "gtd,cd->gtc", grad_branch, cross_out_w, preferred_element_type=jnp.float32
    ).astype(jnp.bfloat16)
    grad_cq_act, grad_ck_act, grad_cv_act = attend_backward(
        cross_query, cross_kv[0], cross_kv[1], cross_allowed, cross_log, grad_ctx
    )
    grad_cq_w = jnp.einsum("gtd,gtc->dc", act_two, grad_cq_act, preferred_element_type=jnp.float32)
    grad_kv_act = jnp.stack([grad_ck_act, grad_cv_act])
    grad_ckv_w = jnp.einsum(
        "gpd,jgpc->jdc", proj_all, grad_kv_act, preferred_element_type=jnp.float32
    )
    grad_proj_part = jnp.einsum(
        "jgpc,jdc->gpd", grad_kv_act, cross_kv_w, preferred_element_type=jnp.float32
    )
    grad_proj = lax.psum_scatter(
        grad_proj_part.astype(jnp.bfloat16), "mod", scatter_dimension=0, tiled=True
    )
    grad_patch_w = jnp.einsum("bpe,bpd->ed", patches, grad_proj, preferred_element_type=jnp.float32)
    grad_act = back_sum(
        jnp.einsum("gtc,dc->gtd", grad_cq_act, cross_query_w, preferred_element_type=jnp.float32)
    )
    grad_inner, gain_grad_two = norm_back(x_one, gain_all[1], grad_act)
    grad_one = grad_two + grad_inner
    cross_grads = (
        lax.psum_scatter(
            grad_cq_w.astype(jnp.bfloat16), "batch", scatter_dimension=0, tiled=True
        ).astype(jnp.float32),
        lax.psum_scatter(
            grad_ckv_w.astype(jnp.bfloat16), "batch", scatter_dimension=1, tiled=True
        ).astype(jnp.float32),
        lax.psum_scatter(
            grad_co_w.astype(jnp.bfloat16), "batch", scatter_dimension=1, tiled=True
        ).astype(jnp.float32),
    )
    self_qkv, self_out = fetch_self(w_qkv, w_so)
    grad_branch = grads_gather(grad_one)
    grad_so_w = jnp.einsum("gtc,gtd->cd", self_ctx, grad_branch, preferred_element_type=jnp.float32)
    grad_ctx = jnp.einsum(
        "gtd,cd->gtc", grad_branch, self_out, preferred_element_type=jnp.float32
    ).astype(jnp.bfloat16)
    grad_q_act, grad_k_act, grad_v_act = attend_backward(
        qkv[0], qkv[1], qkv[2], causal, self_log, grad_ctx
    )
    grad_qkv_act = jnp.stack([grad_q_act, grad_k_act, grad_v_act])
    grad_qkv_w = jnp.einsum(
        "gtd,jgtc->jdc", act_one, grad_qkv_act, preferred_element_type=jnp.float32
    )
    grad_act = back_sum(
        jnp.einsum("jgtc,jdc->gtd", grad_qkv_act, self_qkv, preferred_element_type=jnp.float32)
    )
    grad_inner, gain_grad_one = norm_back(x_zero, gain_all[0], grad_act)
    grad_zero = grad_one + grad_inner
    self_grads = (
        lax.psum_scatter(
            grad_qkv_w.astype(jnp.bfloat16), "batch", scatter_dimension=1, tiled=True
        ).astype(jnp.float32),
        lax.psum_scatter(
            grad_so_w.astype(jnp.bfloat16), "batch", scatter_dimension=1, tiled=True
        ).astype(jnp.float32),
    )
    gain_grads = jnp.stack([gain_grad_one, gain_grad_two, gain_grad_three])
    small_grads = (
        lax.psum_scatter(grad_patch_w, ("batch", "mod"), scatter_dimension=0, tiled=True),
        lax.psum_scatter(gain_grads, ("batch", "mod"), scatter_dimension=1, tiled=True),
    )
    return (
        result,
        grad_zero,
        small_grads[1],
        self_grads[0],
        self_grads[1],
        cross_grads[0],
        cross_grads[1],
        cross_grads[2],
        small_grads[0],
        ffn_grads[0],
        ffn_grads[1],
    )


def solution(mesh):
    placed = (
        P(("batch", "mod"), None, None),
        P(("batch", "mod"), None, None),
        P("batch"),
        P("batch", None),
        P(("batch", "mod"), None, None),
        P(None, ("batch", "mod")),
        P(None, "batch", "mod"),
        P("mod", "batch"),
        P("batch", "mod"),
        P(None, "batch", "mod"),
        P("mod", "batch"),
        P(("batch", "mod"), None),
        P(None, "batch", "mod"),
        P("mod", "batch"),
    )
    return jax.shard_map(
        local,
        mesh=mesh,
        in_specs=placed,
        out_specs=(
            P(("batch", "mod"), None, None),
            P(("batch", "mod"), None, None),
            P(None, ("batch", "mod")),
            P(None, "batch", "mod"),
            P("mod", "batch"),
            P("batch", "mod"),
            P(None, "batch", "mod"),
            P("mod", "batch"),
            P(("batch", "mod"), None),
            P(None, "batch", "mod"),
            P("mod", "batch"),
        ),
        check_vma=False,
    )
```

profile of v0, /device:TPU:0, one launch (start us, length us, event | category | flops | bytes accessed | tf_op | source)
XLA Modules:
  0.0 2608.2 jit_solution(9127698767051760024)
XLA Ops:
  8.9 43.5 %all-gather.1 = bf16[32,64,3]{1,2,0:T(4,128)(2,1)S(1)} all-gather(bf16[1,64,3]{1,2,0:T(4,128)(2,1)} %bitcast.305), channel_id=1, replica_groups=mesh['batch'=8,'mod'=4] {'batch','mod'}, dimensions={0}, use_global_device_ids=true | all-gather | bytes 12672 | tf_op jit(solution)/shard_map/all_gather | solution.py:151
  58.1 28.3 %all-gather.19.cloned.1.call-done = bf16[4,256,2048]{2,1,0:T(8,128)(2,1)} async-done(((bf16[1,256,2048]{2,1,0:T(8,128)(2,1)}), bf16[4,256,2048]{2,1,0:T(8,128)(2,1)}) %all-gather.19.cloned.1.call-update) | async-done | bytes 4194320 | tf_op jit(solution)/shard_map/all_gather | solution.py:46
  86.4 101.2 %all-gather.21.cloned.1.call-done = bf16[3,2048,512]{2,1,0:T(8,128)(2,1)} async-done(((bf16[3,256,512]{2,1,0:T(8,128)(2,1)}), bf16[3,2048,512]{2,1,0:T(8,128)(2,1)}) %all-gather.21.cloned.1.call-update) | async-done | bytes 6291472 | tf_op jit(solution)/shard_map/all_gather | solution.py:25
  187.6 10.0 convert_bitcast_fusion
  206.4 32.5 %all-gather.23.cloned.1.call-done = bf16[512,2048]{1,0:T(8,128)(2,1)} async-done(((bf16[512,256]{1,0:T(8,128)(2,1)}), bf16[512,2048]{1,0:T(8,128)(2,1)}) %all-gather.23.cloned.1.call-update) | async-done | bytes 2097168 | tf_op jit(solution)/shard_map/all_gather | solution.py:26
  238.9 7.3 fusion.71
  246.9 66.6 %all-gather.47.cloned.1.call-done = bf16[32,52,2048]{2,1,0:T(8,128)(2,1)} async-done(((bf16[1,52,2048]{2,1,0:T(8,128)(2,1)}), bf16[32,52,2048]{2,1,0:T(8,128)(2,1)}) %all-gather.47.cloned.1.call-update) | async-done | bytes 6815760 | tf_op jit(solution)/shard_map/all_gather | solution.py:150
  313.4 8.8 reshape.304
  322.2 7.5 convolution_convert_fusion
  330.8 55.3 %reduce-scatter.19.cloned.1.call-done = f32[1,256,2048]{2,1,0:T(8,128)} async-done(((f32[4,256,2048]{2,1,0:T(8,128)}), f32[1,256,2048]{2,1,0:T(8,128)}) %reduce-scatter.19.cloned.1.call-update) | async-done | bytes 2097168 | tf_op jit(solution)/shard_map/reduce_scatter | solution.py:50
  390.3 71.6 %all-gather.25.cloned.1.call-done = bf16[2,2048,512]{2,1,0:T(8,128)(2,1)} async-done(((bf16[2,256,512]{2,1,0:T(8,128)(2,1)}), bf16[2,2048,512]{2,1,0:T(8,128)(2,1)}) %all-gather.25.cloned.1.call-update) | async-done | bytes 4194320 | tf_op jit(solution)/shard_map/all_gather | solution.py:33
  461.8 35.0 %all-gather.45.cloned.1.call-done = bf16[1024,2048]{1,0:T(8,128)(2,1)} async-done(((bf16[256,2048]{1,0:T(8,128)(2,1)}), bf16[1024,2048]{1,0:T(8,128)(2,1)}) %all-gather.45.cloned.1.call-update) | async-done | bytes 4194320 | tf_op jit(solution)/shard_map/all_gather | solution.py:172
  496.8 7.9 convert_bitcast_fusion.1
  510.8 37.7 %all-gather.29.cloned.1.call-done = bf16[2048,512]{1,0:T(8,128)(2,1)} async-done(((bf16[256,512]{1,0:T(8,128)(2,1)}), bf16[2048,512]{1,0:T(8,128)(2,1)}) %all-gather.29.cloned.1.call-update) | async-done | bytes 2097168 | tf_op jit(solution)/shard_map/all_gather | solution.py:32
  548.5 35.2 %all-gather.27.cloned.1.call-done = bf16[4,256,2048]{2,1,0:T(8,128)(2,1)} async-done(((bf16[1,256,2048]{2,1,0:T(8,128)(2,1)}), bf16[4,256,2048]{2,1,0:T(8,128)(2,1)}) %all-gather.27.cloned.1.call-update) | async-done | bytes 4194320 | tf_op jit(solution)/shard_map/all_gather | solution.py:46
  598.9 38.0 %all-gather.31.cloned.1.call-done = bf16[512,2048]{1,0:T(8,128)(2,1)} async-done(((bf16[512,256]{1,0:T(8,128)(2,1)}), bf16[512,2048]{1,0:T(8,128)(2,1)}) %all-gather.31.cloned.1.call-update) | async-done | bytes 2097168 | tf_op jit(solution)/shard_map/all_gather | solution.py:34
  636.9 7.6 fusion.63
  645.2 69.4 %reduce-scatter.21.cloned.1.call-done = f32[1,256,2048]{2,1,0:T(8,128)} async-done(((f32[4,256,2048]{2,1,0:T(8,128)}), f32[1,256,2048]{2,1,0:T(8,128)}) %reduce-scatter.21.cloned.1.call-update) | async-done | bytes 2097168 | tf_op jit(solution)/shard_map/reduce_scatter | solution.py:50
  723.9 143.7 %all-gather.35.cloned.1.call-done = bf16[2,2048,1280]{2,1,0:T(8,128)(2,1)} async-done(((bf16[2,256,1280]{2,1,0:T(8,128)(2,1)}), bf16[2,2048,1280]{2,1,0:T(8,128)(2,1)}) %all-gather.35.cloned.1.call-update) | async-done | bytes 10485776 | tf_op jit(solution)/shard_map/all_gather | solution.py:40
  867.5 34.8 %all-gather.33.cloned.1.call-done = bf16[4,256,2048]{2,1,0:T(8,128)(2,1)} async-done(((bf16[1,256,2048]{2,1,0:T(8,128)(2,1)}), bf16[4,256,2048]{2,1,0:T(8,128)(2,1)}) %all-gather.33.cloned.1.call-update) | async-done | bytes 4194320 | tf_op jit(solution)/shard_map/all_gather | solution.py:46
  902.4 17.3 fusion.5
  919.7 19.2 all-gather.39.cloned.1.call-done
  938.9 89.1 %all-gather.37.cloned.1.call-done = bf16[1280,2048]{1,0:T(8,128)(2,1)} async-done(((bf16[1280,256]{1,0:T(8,128)(2,1)}), bf16[1280,2048]{1,0:T(8,128)(2,1)}) %all-gather.37.cloned.1.call-update) | async-done | bytes 5242896 | tf_op jit(solution)/shard_map/all_gather | solution.py:41
  1028.0 15.6 fusion.43
  1046.0 15.9 fusion.27
  1062.0 11.2 fusion.22
  1073.3 58.8 %reduce-scatter.25.cloned.1.call-done = f32[1,256,2048]{2,1,0:T(8,128)} async-done(((f32[4,256,2048]{2,1,0:T(8,128)}), f32[1,256,2048]{2,1,0:T(8,128)}) %reduce-scatter.25.cloned.1.call-update) | async-done | bytes 2097168 | tf_op jit(solution)/shard_map/reduce_scatter | solution.py:58
  1134.8 71.6 %reduce-scatter.23.cloned.1.call-done = f32[1,256,2048]{2,1,0:T(8,128)} async-done(((f32[4,256,2048]{2,1,0:T(8,128)}), f32[1,256,2048]{2,1,0:T(8,128)}) %reduce-scatter.23.cloned.1.call-update) | async-done | bytes 2097168 | tf_op jit(solution)/shard_map/reduce_scatter | solution.py:50
  1206.4 6.3 fusion.117
  1212.8 34.6 %all-gather.41.cloned.1.call-done = bf16[4,256,2048]{2,1,0:T(8,128)(2,1)} async-done(((bf16[1,256,2048]{2,1,0:T(8,128)(2,1)}), bf16[4,256,2048]{2,1,0:T(8,128)(2,1)}) %all-gather.41.cloned.1.call-update) | async-done | bytes 4194320 | tf_op jit(solution)/shard_map/all_gather | solution.py:54
  1283.2 58.9 %reduce-scatter.27.cloned.1.call-done = f32[1,256,2048]{2,1,0:T(8,128)} async-done(((f32[4,256,2048]{2,1,0:T(8,128)}), f32[1,256,2048]{2,1,0:T(8,128)}) %reduce-scatter.27.cloned.1.call-update) | async-done | bytes 2097168 | tf_op jit(solution)/shard_map/reduce_scatter | solution.py:58
  1347.4 10.8 bitcast_convert_fusion.2
  1358.2 16.8 fusion.4
  1388.6 9.0 fusion.39
  1397.7 8.3 convolution_bitcast_fusion
  1406.2 19.7 all-gather.43.cloned.1.call-done
  1458.1 11.4 fusion.8
  1471.1 11.2 fusion.24
  1482.4 50.1 %reduce-scatter.45.cloned.1.call-done = bf16[1280,256]{1,0:T(8,128)(2,1)} async-done(((bf16[1280,2048]{1,0:T(8,128)(2,1)}), bf16[1280,256]{1,0:T(8,128)(2,1)}) %reduce-scatter.45.cloned.1.call-update) | async-done | bytes 655376 | tf_op jit(solution)/shard_map/reduce_scatter | solution.py:208
  1534.7 179.6 %reduce-scatter.43.cloned.1.call-done = bf16[2,256,1280]{1,2,0:T(8,128)(2,1)} async-done(((bf16[2,2048,1280]{1,2,0:T(8,128)(2,1)}), bf16[2,256,1280]{1,2,0:T(8,128)(2,1)}) %reduce-scatter.43.cloned.1.call-update) | async-done | bytes 1310736 | tf_op jit(solution)/shard_map/reduce_scatter | solution.py:205
  1717.1 68.0 %reduce-scatter.39.cloned.1.call-done = bf16[512,256]{1,0:T(8,128)(2,1)} async-done(((bf16[512,2048]{1,0:T(8,128)(2,1)}), bf16[512,256]{1,0:T(8,128)(2,1)}) %reduce-scatter.39.cloned.1.call-update) | async-done | bytes 262160 | tf_op jit(solution)/shard_map/reduce_scatter | solution.py:247
  1786.8 68.5 %reduce-scatter.35.cloned.1.call-done = bf16[256,512]{1,0:T(8,128)(2,1)} async-done(((bf16[2048,512]{1,0:T(8,128)(2,1)}), bf16[256,512]{1,0:T(8,128)(2,1)}) %reduce-scatter.35.cloned.1.call-update) | async-done | bytes 262160 | tf_op jit(solution)/shard_map/reduce_scatter | solution.py:241
  1857.1 89.2 %reduce-scatter.37.cloned.1.call-done = bf16[2,256,512]{1,2,0:T(8,128)(2,1)} async-done(((bf16[2,2048,512]{1,2,0:T(8,128)(2,1)}), bf16[2,256,512]{1,2,0:T(8,128)(2,1)}) %reduce-scatter.37.cloned.1.call-update) | async-done | bytes 524304 | tf_op jit(solution)/shard_map/reduce_scatter | solution.py:244
  1948.5 245.6 %all-reduce.3.cloned.1.call-done = f32[1664,2048]{0,1:T(8,128)} async-done(((f32[1664,2048]{0,1:T(8,128)}), f32[1664,2048]{0,1:T(8,128)}) %all-reduce.3.cloned.1.call-update) | async-done | bytes 13631504
  2197.1 68.8 %reduce-scatter.33.cloned.1.call-done = bf16[512,256]{1,0:T(8,128)(2,1)} async-done(((bf16[512,2048]{1,0:T(8,128)(2,1)}), bf16[512,256]{1,0:T(8,128)(2,1)}) %reduce-scatter.33.cloned.1.call-update) | async-done | bytes 262160 | tf_op jit(solution)/shard_map/reduce_scatter | solution.py:273
  2267.7 119.6 %reduce-scatter.31.cloned.1.call-done = bf16[3,256,512]{1,2,0:T(8,128)(2,1)} async-done(((bf16[3,2048,512]{1,2,0:T(8,128)(2,1)}), bf16[3,256,512]{1,2,0:T(8,128)(2,1)}) %reduce-scatter.31.cloned.1.call-update) | async-done | bytes 786448 | tf_op jit(solution)/shard_map/reduce_scatter | solution.py:270
  2389.9 71.0 %reduce-scatter.29.cloned.1.call-done = f32[1,256,2048]{2,1,0:T(8,128)} async-done(((f32[4,256,2048]{2,1,0:T(8,128)}), f32[1,256,2048]{2,1,0:T(8,128)}) %reduce-scatter.29.cloned.1.call-update) | async-done | bytes 2097168 | tf_op jit(solution)/shard_map/reduce_scatter | solution.py:58
  2468.7 130.9 %reduce-scatter.47.cloned.1.call-done = f32[64,3]{1,0:T(8,128)} async-done(((f32[2048,3]{1,0:T(8,128)}), f32[64,3]{1,0:T(8,128)}) %reduce-scatter.47.cloned.1.call-update) | async-done | bytes 784
  (231 shorter events, 173.8 us)
Async XLA Ops:
  7.2 315.1 %copy-start = (bf16[1,256,1664]{2,1,0:T(8,128)(2,1)S(1)}, bf16[1,256,1664]{2,1,0:T(8,128)(2,1)}, u32[]{:S(2)}) copy-start(bf16[1,256,1664]{2,1,0:T(8,128)(2,1)} %param.15) | copy-start | bytes 2555908
  7.2 50.6 %copy-start.39 = (s32[4]{0:T(128)S(1)}, s32[4]{0:T(128)}, u32[]{:S(2)}) copy-start(s32[4]{0:T(128)} %param.16) | copy-start | bytes 52
  7.2 79.2 %all-gather.19.cloned.1.call-start = ((), (), s32[]{:S(2)}) async-start(), calls=%async_computation.15 | async-start | bytes 5242880 | tf_op jit(solution)/shard_map/all_gather | solution.py:46
  8.8 43.6 %copy-start.34 = (f32[256]{0:T(256)}, f32[256]{0:T(256)S(1)}, u32[]{:S(2)}) copy-start(f32[256]{0:T(256)S(1)} %fusion.59) | copy-start | bytes 3076
  8.8 178.8 %copy-start.32 = (f32[256]{0:T(256)}, f32[256]{0:T(256)S(1)}, u32[]{:S(2)}) copy-start(f32[256]{0:T(256)S(1)} %fusion.106) | copy-start | bytes 3076
  55.6 132.0 %all-gather.21.cloned.1.call-start = ((), (), s32[]{:S(2)}) async-start(), calls=%async_computation.16 | async-start | bytes 7077888 | tf_op jit(solution)/shard_map/all_gather | solution.py:25
  56.4 182.6 %all-gather.23.cloned.1.call-start = ((), (), s32[]{:S(2)}) async-start(), calls=%async_computation.17 | async-start | bytes 2359296 | tf_op jit(solution)/shard_map/all_gather | solution.py:26
  57.1 256.3 %all-gather.47.cloned.1.call-start = ((), (), s32[]{:S(2)}) async-start(), calls=%async_computation.43 | async-start | bytes 7569408 | tf_op jit(solution)/shard_map/all_gather | solution.py:150
  57.7 328.5 %reduce-scatter.19.cloned.1.call-start = ((), (), s32[]{:S(2)}) async-start(), calls=%async_computation.18 | async-start | bytes 10485760 | tf_op jit(solution)/shard_map/reduce_scatter | solution.py:50
  206.4 39.8 %copy-start.40 = (bf16[4,4,128,256]{3,2,1,0:T(8,128)(2,1)}, bf16[4,4,128,256]{3,2,1,0:T(8,128)(2,1)S(1)}, u32[]{:S(2)}) copy-start(bf16[4,4,128,256]{3,2,1,0:T(8,128)(2,1)S(1)} %fusion.81) | copy-start | bytes 3145732
  246.2 215.6 %all-gather.25.cloned.1.call-start = ((), (), s32[]{:S(2)}) async-start(), calls=%async_computation.19 | async-start | bytes 4718592 | tf_op jit(solution)/shard_map/all_gather | solution.py:33
  246.8 250.0 %all-gather.45.cloned.1.call-start = ((), (), s32[]{:S(2)}) async-start(), calls=%async_computation.42 | async-start | bytes 5242880 | tf_op jit(solution)/shard_map/all_gather | solution.py:172
  329.8 218.7 %all-gather.29.cloned.1.call-start = ((), (), s32[]{:S(2)}) async-start(), calls=%async_computation.21 | async-start | bytes 2359296 | tf_op jit(solution)/shard_map/all_gather | solution.py:32
  330.5 59.7 %copy-start.36 = (s32[4,256]{1,0:T(4,128)S(1)}, s32[4,256]{1,0:T(4,128)}, u32[]{:S(2)}) copy-start(s32[4,256]{1,0:T(4,128)} %param.17) | copy-start | bytes 12292
  330.6 253.2 %all-gather.27.cloned.1.call-start = ((), (), s32[]{:S(2)}) async-start(), calls=%async_computation.20 | async-start | bytes 5242880 | tf_op jit(solution)/shard_map/all_gather | solution.py:46
  389.6 247.3 %all-gather.31.cloned.1.call-start = ((), (), s32[]{:S(2)}) async-start(), calls=%async_computation.22 | async-start | bytes 2359296 | tf_op jit(solution)/shard_map/all_gather | solution.py:34
  390.2 324.4 %reduce-scatter.21.cloned.1.call-start = ((), (), s32[]{:S(2)}) async-start(), calls=%async_computation.23 | async-start | bytes 10485760 | tf_op jit(solution)/shard_map/reduce_scatter | solution.py:50
  592.1 4.8 copy-start.17
  644.6 223.0 %all-gather.35.cloned.1.call-start = ((), (), s32[]{:S(2)}) async-start(), calls=%async_computation.25 | async-start | bytes 11796480 | tf_op jit(solution)/shard_map/all_gather | solution.py:40
  645.1 257.2 %all-gather.33.cloned.1.call-start = ((), (), s32[]{:S(2)}) async-start(), calls=%async_computation.24 | async-start | bytes 5242880 | tf_op jit(solution)/shard_map/all_gather | solution.py:46
  719.1 219.8 %all-gather.39.cloned.1.call-start = ((), (), s32[]{:S(2)}) async-start(), calls=%async_computation.28 | async-start | bytes 5242880 | tf_op jit(solution)/shard_map/all_gather | solution.py:54
  722.8 305.2 %all-gather.37.cloned.1.call-start = ((), (), s32[]{:S(2)}) async-start(), calls=%async_computation.26 | async-start | bytes 5898240 | tf_op jit(solution)/shard_map/all_gather | solution.py:41
  723.4 408.6 %reduce-scatter.25.cloned.1.call-start = ((), (), s32[]{:S(2)}) async-start(), calls=%async_computation.29 | async-start | bytes 10485760 | tf_op jit(solution)/shard_map/reduce_scatter | solution.py:58
  1062.0 144.4 %reduce-scatter.23.cloned.1.call-start = ((), (), s32[]{:S(2)}) async-start(), calls=%async_computation.27 | async-start | bytes 10485760 | tf_op jit(solution)/shard_map/reduce_scatter | solution.py:50
  1073.2 174.2 %all-gather.41.cloned.1.call-start = ((), (), s32[]{:S(2)}) async-start(), calls=%async_computation.30 | async-start | bytes 5242880 | tf_op jit(solution)/shard_map/all_gather | solution.py:54
  1212.7 129.4 %reduce-scatter.27.cloned.1.call-start = ((), (), s32[]{:S(2)}) async-start(), calls=%async_computation.31 | async-start | bytes 10485760 | tf_op jit(solution)/shard_map/reduce_scatter | solution.py:58
  1270.2 127.5 %reduce-scatter.41.cloned.1.call-start = ((), (), s32[]{:S(2)}) async-start(), calls=%async_computation.39 | async-start | bytes 5242880 | tf_op jit(solution)/shard_map/reduce_scatter | solution.py:231
  1283.1 142.7 %all-gather.43.cloned.1.call-start = ((), (), s32[]{:S(2)}) async-start(), calls=%async_computation.32 | async-start | bytes 5242880 | tf_op jit(solution)/shard_map/all_gather | solution.py:54
  1347.3 185.1 %reduce-scatter.45.cloned.1.call-start = ((), (), s32[]{:S(2)}) async-start(), calls=%async_computation.41 | async-start | bytes 5898240 | tf_op jit(solution)/shard_map/reduce_scatter | solution.py:208
  1358.2 356.1 %reduce-scatter.43.cloned.1.call-start = ((), (), s32[]{:S(2)}) async-start(), calls=%async_computation.40 | async-start | bytes 11796480 | tf_op jit(solution)/shard_map/reduce_scatter | solution.py:205
  1375.0 7.4 copy-start.22
  1375.0 410.0 %reduce-scatter.39.cloned.1.call-start = ((), (), s32[]{:S(2)}) async-start(), calls=%async_computation.38 | async-start | bytes 2359296 | tf_op jit(solution)/shard_map/reduce_scatter | solution.py:247
  1382.2 6.4 copy-start.24
  1382.2 473.1 %reduce-scatter.35.cloned.1.call-start = ((), (), s32[]{:S(2)}) async-start(), calls=%async_computation.36 | async-start | bytes 2359296 | tf_op jit(solution)/shard_map/reduce_scatter | solution.py:241
  1388.5 557.8 %reduce-scatter.37.cloned.1.call-start = ((), (), s32[]{:S(2)}) async-start(), calls=%async_computation.37 | async-start | bytes 4718592 | tf_op jit(solution)/shard_map/reduce_scatter | solution.py:244
  1397.6 796.4 %all-reduce.3.cloned.1.call-start = ((), (), s32[]{:S(2)}) async-start(), calls=%async_computation.45 | async-start | bytes 27262976
  1406.1 19.8 copy-start.41
  1406.1 25.9 copy-start.27
  1406.1 25.9 copy-start.31
  1406.1 859.8 %reduce-scatter.33.cloned.1.call-start = ((), (), s32[]{:S(2)}) async-start(), calls=%async_computation.35 | async-start | bytes 2359296 | tf_op jit(solution)/shard_map/reduce_scatter | solution.py:273
  1431.7 955.6 %reduce-scatter.31.cloned.1.call-start = ((), (), s32[]{:S(2)}) async-start(), calls=%async_computation.34 | async-start | bytes 7077888 | tf_op jit(solution)/shard_map/reduce_scatter | solution.py:270
  1437.8 6.4 copy-start.16
  1469.6 991.3 %reduce-scatter.29.cloned.1.call-start = ((), (), s32[]{:S(2)}) async-start(), calls=%async_computation.33 | async-start | bytes 10485760 | tf_op jit(solution)/shard_map/reduce_scatter | solution.py:58
  1482.3 1117.2 %reduce-scatter.47.cloned.1.call-start = ((), (), s32[]{:S(2)}) async-start(), calls=%async_computation.44 | async-start | bytes 1081344
  1857.1 603.8 %copy-start.7 = (bf16[1,256,2048]{2,1,0:T(8,128)(2,1)S(1)}, bf16[1,256,2048]{2,1,0:T(8,128)(2,1)}, u32[]{:S(2)}) copy-start(bf16[1,256,2048]{2,1,0:T(8,128)(2,1)} %param.14) | copy-start | bytes 3145732
  1857.1 603.8 %copy-start.29 = (f32[1,2048]{1,0:T(1,128)S(1)}, f32[1,2048]{1,0:T(1,128)}, u32[]{:S(2)}) copy-start(f32[1,2048]{1,0:T(1,128)} %copy-done.28) | copy-start | bytes 24580
  1857.1 603.8 %copy-start.33 = (f32[256]{0:T(256)S(1)}, f32[256]{0:T(256)}, u32[]{:S(2)}) copy-start(f32[256]{0:T(256)} %copy-done.32) | copy-start | bytes 3076
  2196.0 267.1 %copy-start.35 = (f32[256]{0:T(256)S(1)}, f32[256]{0:T(256)}, u32[]{:S(2)}) copy-start(f32[256]{0:T(256)} %copy-done.34) | copy-start | bytes 3076
  (28 other events, 56.3 us)
Sparse Core Ops, SparseCore 0:
  55.7 30.5 all-gather.18
  88.5 99.0 all-gather.20
  189.6 49.2 all-gather.22
  241.7 71.7 all-gather.46
  315.9 70.2 reduce-scatter.18
  388.4 73.3 all-gather.24
  464.0 32.7 all-gather.44
  499.2 49.2 all-gather.28
  550.7 32.9 all-gather.26
  585.8 51.0 all-gather.30
  644.7 69.8 reduce-scatter.20
  716.6 150.8 all-gather.34
  869.7 32.6 all-gather.32
  904.3 34.4 all-gather.38
  940.8 87.1 all-gather.36
  1062.1 69.8 reduce-scatter.24
  1134.6 71.6 reduce-scatter.22
  1212.8 34.4 all-gather.40
  1270.3 71.7 reduce-scatter.26
  1344.6 44.5 reduce-scatter.40
  1391.3 34.4 all-gather.42
  1429.4 102.9 reduce-scatter.44
  1536.1 178.1 reduce-scatter.42
  1717.7 67.3 reduce-scatter.38
  1788.6 66.6 reduce-scatter.34
  1858.8 87.4 reduce-scatter.36
  1953.4 240.6 all-reduce.2
  2198.0 67.8 reduce-scatter.32
  2270.0 117.3 reduce-scatter.30
  2389.9 70.8 reduce-scatter.28
  2464.7 134.7 reduce-scatter.46
where the time goes:
time: 2620 us; the launch traced here: 2610 us
  waiting for transfers between devices  2200 us (84%)
  matrix products  244 us (9%)
  local copies, waits for them, and re-layouts  60.6 us (2%)
  other arithmetic  45 us (2%)
  blocking collectives  43.5 us (2%)
    unnamed x33, waiting for transfers between devices  382 us
    reduce_scatter x3, waiting for transfers between devices, rows_sum(): return lax.psum_scatter(partial_out, 'mod', scatter_dimension=0, tiled=True)  196 us
    reduce_scatter x3, waiting for transfers between devices, back_sum(): lax.psum_scatter(partial_grad, 'mod', scatter_dimension=0, tiled=True)  189 us
    reduce_scatter x1, waiting for transfers between devices, local(): lax.psum_scatter(grad_gate_up.astype(jnp.bfloat16), 'batch', scatter_dime...  180 us
    all_gather x1, waiting for transfers between devices, fetch_ffn(): lax.all_gather(w_gu, 'batch', axis=1, tiled=True)  144 us
    reduce_scatter x1, waiting for transfers between devices, local(): lax.psum_scatter(grad_qkv_w.astype(jnp.bfloat16), 'batch', scatter_dimens...  120 us
    all_gather x1, waiting for transfers between devices, fetch_self(): lax.all_gather(w_qkv, 'batch', axis=1, tiled=True)  101 us
    all_gather x3, waiting for transfers between devices, rows_gather(): lax.all_gather(normed.astype(jnp.bfloat16), 'mod', axis=0, tiled=True)  98.3 us
  transfers between devices with their start and end apart: 31, of which 30 were waited for; matrix products, arithmetic and copies ran while one was open for 10% of the time, Pallas kernels for 0%

commit v1 on v0

v1 whole, which is shorter than its diff:
```python
import jax
import jax.numpy as jnp
from jax import lax
from jax.sharding import PartitionSpec as P

HD = 128
F32 = jnp.float32
BF = jnp.bfloat16


def rms_norm(values, gain):
    factor = lax.rsqrt(jnp.mean(values * values, axis=-1, keepdims=True) + 1e-06)
    return values * factor * gain


def norm_back(values, gain, grad_in):
    _, pullback = jax.vjp(rms_norm, values, gain)
    return pullback(grad_in)


def gelu_mix(gate, upward):
    return jax.nn.gelu(gate, approximate=True) * upward


def tie(value, deps):
    if not deps:
        return value
    return lax.optimization_barrier((value, tuple(deps)))[0]


def dot(spec, a, b):
    return jnp.einsum(spec, a, b, preferred_element_type=F32)


class Batch:
    def __init__(self, size):
        self.size = size
        self.n_out = size // 2
        here = lax.axis_index("batch")
        self.outer, self.inner = here // 2, here % 2
        self.last_z = []
        self.last_x = []

    def source(self, position):
        s, j = position // 2, position % 2
        return (self.outer - s + self.n_out) % self.n_out * 2 + (self.inner + j) % 2

    def shifts(self):
        n = self.n_out
        order = []
        for d in range(1, n // 2 + 1):
            order.append(d)
            if n - d != d:
                order.append(n - d)
        return order

    def along_z(self, value, s):
        n = self.n_out
        pairs = [(o * 2 + i, (o + s) % n * 2 + i) for o in range(n) for i in range(2)]
        return lax.ppermute(value, "batch", pairs)

    def along_x(self, value):
        return lax.ppermute(value, "batch", [(b, b ^ 1) for b in range(self.size)])

    def reorder(self, value, axis):
        width = value.shape[axis] // self.size
        return jnp.concatenate(
            [
                lax.dynamic_slice_in_dim(value, self.source(p) * width, width, axis)
                for p in range(self.size)
            ],
            axis=axis,
        )

    def fetch(self, shard, deps=()):
        shard = tie(shard, deps)
        z = {0: shard}
        for s in self.shifts():
            z[s] = self.along_z(shard, s)
        out = []
        for s in range(self.n_out):
            out += [z[s], self.along_x(z[s])]
        return out

    def reduce(self, blocks_x, blocks_own, deps=()):
        got = self.along_x(tie(blocks_x.astype(BF), deps))
        total = blocks_own.astype(F32) + got.astype(F32)
        send = total.astype(BF)
        result = total[0]
        for s in self.shifts():
            result = result + self.along_z(send[s], self.n_out - s).astype(F32)
        return result


def scores_of(query, keys, allowed):
    item_count, query_rows, columns = query.shape
    head_count = columns // HD
    query_heads = query.reshape(item_count, query_rows, head_count, HD)
    key_heads = keys.reshape(item_count, keys.shape[1], head_count, HD)
    raw_scores = dot("bqhe,bkhe->bhqk", query_heads, key_heads) * HD ** (-0.5)
    return jnp.where(allowed[:, None], raw_scores, -1e30)


def attend_forward(query, keys, values, allowed):
    item_count, query_rows, columns = query.shape
    head_count = columns // HD
    scores = scores_of(query, keys, allowed)
    row_max = jnp.max(scores, axis=-1, keepdims=True)
    weights = jnp.exp(scores - row_max)
    row_total = jnp.sum(weights, axis=-1, keepdims=True)
    probs = (weights / row_total).astype(BF)
    value_heads = values.reshape(item_count, values.shape[1], head_count, HD)
    context = dot("bhqk,bkhe->bqhe", probs, value_heads)
    return (
        context.reshape(item_count, query_rows, columns).astype(BF),
        row_max + jnp.log(row_total),
    )


def attend_backward(query, keys, values, allowed, log_total, grad_context):
    item_count, query_rows, columns = query.shape
    key_rows = keys.shape[1]
    head_count = columns // HD
    scale = HD ** (-0.5)
    probs = jnp.exp(scores_of(query, keys, allowed) - log_total)
    grad_heads = grad_context.reshape(item_count, query_rows, head_count, HD)
    query_heads = query.reshape(item_count, query_rows, head_count, HD)
    key_heads = keys.reshape(item_count, key_rows, head_count, HD)
    value_heads = values.reshape(item_count, key_rows, head_count, HD)
    grad_values = dot("bhqk,bqhe->bkhe", probs.astype(BF), grad_heads)
    grad_probs = dot("bqhe,bkhe->bhqk", grad_heads, value_heads)
    grad_scores = probs * (grad_probs - jnp.sum(probs * grad_probs, axis=-1, keepdims=True))
    grad_scores = grad_scores.astype(BF)
    grad_query = dot("bhqk,bkhe->bqhe", grad_scores, key_heads) * scale
    grad_keys = dot("bhqk,bqhe->bkhe", grad_scores, query_heads) * scale
    return (
        grad_query.reshape(item_count, query_rows, columns).astype(BF),
        grad_keys.reshape(item_count, key_rows, columns).astype(BF),
        grad_values.reshape(item_count, key_rows, columns).astype(BF),
    )


def mod_gather(value, axis=0):
    return lax.all_gather(value, "mod", axis=axis, tiled=True)


def mod_sum(partial):
    return lax.psum_scatter(partial.astype(BF), "mod", scatter_dimension=0, tiled=True).astype(F32)


def local(n_batch, n_mod, text, patches, text_lengths, patch_mask, cotangent, gains,
          w_qkv, w_so, w_cq, w_ckv, w_co, w_patch, w_gu, w_down):
    own_items, text_rows, width = text.shape
    heads_w = w_qkv.shape[2]
    mod = lax.axis_index("mod")
    ex = Batch(n_batch)
    nb, no = n_batch, n_batch // 2
    own_lengths = lax.dynamic_slice_in_dim(text_lengths, mod * own_items, own_items)
    positions = jnp.arange(text_rows)
    causal = (positions[None, None, :] <= positions[None, :, None]) & (
        positions[None, None, :] < text_lengths[:, None, None]
    )
    cross_allowed = (patch_mask > 0)[:, None, :]

    text_all = mod_gather(ex.reorder(text, 2))
    gain_parts = ex.fetch(gains)
    qkv_parts = ex.fetch(w_qkv)
    gain_cols = mod_gather(jnp.stack(gain_parts)[None], 0)
    gain_all = jnp.transpose(gain_cols, (2, 1, 0, 3)).reshape(3, width).astype(F32)
    x_zero = ex.reorder(text, 2).astype(F32)
    patch_all = mod_gather(patches)
    col_w = width // n_mod
    patch_rows = mod_gather(w_patch)
    patch_own = lax.dynamic_slice_in_dim(patch_rows, mod * col_w, col_w, 1)

    so_parts = ex.fetch(w_so.T, [qkv_parts[-1]])
    patch_parts = ex.fetch(patch_own, [qkv_parts[-1]])
    act_one = rms_norm(text_all.astype(F32), gain_all[0]).astype(BF)
    self_qkv = jnp.concatenate(qkv_parts, axis=1)
    qkv = dot("gtd,jdc->jgtc", act_one, self_qkv).astype(BF)
    self_ctx, self_log = attend_forward(qkv[0], qkv[1], qkv[2], causal)
    self_out = jnp.concatenate(so_parts, axis=0)
    x_one = x_zero + mod_sum(dot("gtc,dc->gtd", self_ctx, self_out))

    pr = w_patch.shape[0] * n_mod
    proj_w = jnp.zeros((pr * nb, col_w), BF)
    for p in range(nb):
        proj_w = lax.dynamic_update_slice_in_dim(proj_w, patch_parts[p], ex.source(p) * pr, 0)
    proj_cols = dot("gpe,ec->gpc", patch_all, proj_w).astype(BF)
    proj_all = ex.reorder(mod_gather(proj_cols, 2), 2)
    ckv_parts = ex.fetch(w_ckv, [so_parts[-1], patch_parts[-1]])
    cq_parts = ex.fetch(w_cq, [so_parts[-1], patch_parts[-1]])
    co_parts = ex.fetch(w_co.T, [ckv_parts[-1], cq_parts[-1]])
    gate_parts = ex.fetch(w_gu[0], [ckv_parts[-1], cq_parts[-1]])
    up_parts = ex.fetch(w_gu[1], [gate_parts[-1]])
    down_parts = ex.fetch(w_down.T, [up_parts[-1]])

    cross_query_w = jnp.concatenate(cq_parts, axis=0)
    cross_kv_w = jnp.concatenate(ckv_parts, axis=1)
    cross_out_w = jnp.concatenate(co_parts, axis=0)
    cross_kv = dot("gpd,jdc->jgpc", proj_all, cross_kv_w).astype(BF)
    act_two = mod_gather(rms_norm(x_one, gain_all[1]).astype(BF))
    cross_query = dot("gtd,dc->gtc", act_two, cross_query_w).astype(BF)
    cross_ctx, cross_log = attend_forward(cross_query, cross_kv[0], cross_kv[1], cross_allowed)
    x_two = x_one + mod_sum(dot("gtc,dc->gtd", cross_ctx, cross_out_w))

    act_three = mod_gather(rms_norm(x_two, gain_all[2]).astype(BF))
    gate_w = jnp.concatenate(gate_parts, axis=0)
    up_w = jnp.concatenate(up_parts, axis=0)
    gate = dot("gtd,df->gtf", act_three, gate_w)
    upward = dot("gtd,df->gtf", act_three, up_w)
    hidden = gelu_mix(gate, upward).astype(BF)

    valid = (positions[None, :] < own_lengths[:, None]).astype(F32)
    grad_result = ex.reorder(cotangent, 2).astype(F32) * valid[..., None]
    grad_branch = mod_gather(grad_result.astype(BF))

    def own_and_x(acts, grads, spec):
        a = acts.reshape(acts.shape[:2] + (no, 2, width // nb))
        return dot(spec, a[:, :, :, 1], grads).astype(BF), dot(spec, a[:, :, :, 0], grads)

    def reduced(acts, grads, spec="gtsd,gtc->sdc", deps=()):
        theirs, mine = own_and_x(acts, grads, spec)
        return ex.reduce(theirs, mine, deps)

    grad_down = reduced(grad_branch, hidden)
    down_w = jnp.concatenate(down_parts, axis=0)
    result = x_two + mod_sum(dot("gtf,df->gtd", hidden, down_w))
    grad_hidden = dot("gtd,df->gtf", grad_branch, down_w)
    _, mix_pull = jax.vjp(gelu_mix, gate, upward)
    grad_gate, grad_upward = mix_pull(grad_hidden)
    grad_gate = grad_gate.astype(BF)
    grad_upward = grad_upward.astype(BF)
    grad_act = mod_sum(dot("gtf,df->gtd", grad_gate, gate_w) + dot("gtf,df->gtd", grad_upward, up_w))
    grad_gate_w = reduced(act_three, grad_gate)
    grad_up_w = reduced(act_three, grad_upward)
    grad_inner, gain_grad_three = norm_back(x_two, gain_all[2], grad_act)
    grad_two = grad_result + grad_inner

    grad_branch = mod_gather(grad_two.astype(BF))
    grad_co_w = reduced(grad_branch, cross_ctx)
    grad_ctx = dot("gtd,dc->gtc", grad_branch, cross_out_w).astype(BF)
    grad_cq_act, grad_ck_act, grad_cv_act = attend_backward(
        cross_query, cross_kv[0], cross_kv[1], cross_allowed, cross_log, grad_ctx
    )
    grad_act = mod_sum(dot("gtc,dc->gtd", grad_cq_act, cross_query_w))
    grad_kv_act = jnp.stack([grad_ck_act, grad_cv_act])
    grad_proj_part = dot("jgpc,jdc->gpd", grad_kv_act, cross_kv_w).astype(BF)
    grad_proj_part = ex.reorder(grad_proj_part, 2)
    grad_proj = lax.psum_scatter(
        jnp.stack(jnp.split(grad_proj_part, n_mod, axis=2)), "mod", scatter_dimension=0, tiled=True
    )[0]
    grad_cq_w = reduced(act_two, grad_cq_act)
    grad_ckv_w = jnp.stack([reduced(proj_all, grad_ck_act), reduced(proj_all, grad_cv_act)])
    grad_inner, gain_grad_two = norm_back(x_one, gain_all[1], grad_act)
    grad_one = grad_two + grad_inner

    grad_branch = mod_gather(grad_one.astype(BF))
    grad_so_w = reduced(grad_branch, self_ctx)
    grad_ctx = dot("gtd,dc->gtc", grad_branch, self_out).astype(BF)
    grad_patch_all = dot("gpe,gpc->ec", patch_all, grad_proj).astype(BF)
    by_source = [lax.dynamic_slice_in_dim(grad_patch_all, ex.source(p) * pr, pr, 0) for p in range(nb)]
    grad_patch_cols = ex.reduce(jnp.stack(by_source[1::2]), jnp.stack(by_source[0::2]))
    grad_patch_w = lax.all_to_all(
        grad_patch_cols.reshape(n_mod, pr // n_mod, col_w), "mod", 0, 0, tiled=True
    )
    grad_patch_w = jnp.transpose(grad_patch_w, (1, 0, 2)).reshape(pr // n_mod, width)

    grad_q_act, grad_k_act, grad_v_act = attend_backward(
        qkv[0], qkv[1], qkv[2], causal, self_log, grad_ctx
    )
    grad_qkv_act = jnp.stack([grad_q_act, grad_k_act, grad_v_act])
    grad_act = mod_sum(dot("jgtc,jdc->gtd", grad_qkv_act, self_qkv))
    grad_qkv_w = jnp.stack([reduced(act_one, g) for g in (grad_q_act, grad_k_act, grad_v_act)])
    grad_inner, gain_grad_one = norm_back(x_zero, gain_all[0], grad_act)
    grad_zero = grad_one + grad_inner

    gain_grads = jnp.stack([gain_grad_one, gain_grad_two, gain_grad_three])
    gg = gain_grads.reshape(3, no, 2, width // nb)
    got = ex.along_x(gg[:, :, 1])
    gg = gg[:, :, 0] + got
    gsum = gg[:, 0]
    for s in ex.shifts():
        gsum = gsum + ex.along_z(gg[:, s], no - s)
    gsum = jnp.sum(mod_gather(gsum[None], 0), axis=0)
    gw = width // (nb * n_mod)
    gain_out = lax.dynamic_slice_in_dim(gsum, mod * gw, gw, 1)
    return (
        ex.reorder(result, 2),
        ex.reorder(grad_zero, 2),
        gain_out,
        grad_qkv_w,
        grad_so_w.T,
        grad_cq_w,
        grad_ckv_w,
        grad_co_w.T,
        grad_patch_w,
        jnp.stack([grad_gate_w, grad_up_w]),
        grad_down.T,
    )


def solution(mesh):
    placed = (
        P(("batch", "mod"), None, None),
        P(("batch", "mod"), None, None),
        P("batch"),
        P("batch", None),
        P(("batch", "mod"), None, None),
        P(None, ("batch", "mod")),
        P(None, "batch", "mod"),
        P("mod", "batch"),
        P("batch", "mod"),
        P(None, "batch", "mod"),
        P("mod", "batch"),
        P(("batch", "mod"), None),
        P(None, "batch", "mod"),
        P("mod", "batch"),
    )

    def run(*args):
        return local(mesh.shape["batch"], mesh.shape["mod"], *args)

    return jax.shard_map(
        run,
        mesh=mesh,
        in_specs=placed,
        out_specs=(
            P(("batch", "mod"), None, None),
            P(("batch", "mod"), None, None),
            P(None, ("batch", "mod")),
            P(None, "batch", "mod"),
            P("mod", "batch"),
            P("batch", "mod"),
            P(None, "batch", "mod"),
            P("mod", "batch"),
            P(("batch", "mod"), None),
            P(None, "batch", "mod"),
            P("mod", "batch"),
        ),
        check_vma=False,
    )
```

time: 2620 us -> 1530 us (0.58)
  waiting for transfers between devices: 2200 us -> 672 us
  starting transfers between devices: 2.52 us -> 266 us
  local copies, waits for them, and re-layouts: 60.6 us -> 255 us
    reduce_scatter x14 -> x7, waiting for transfers between devices: 1030 us -> 52.5 us  [the longest x6 52.5 us: mod_sum(): lax.psum_scatter(partial.astype(BF), 'mod', scatter_dimension=0, tiled=True)]
    all_gather x15 -> x8, waiting for transfers between devices: 787 us -> 34.6 us  [mod_gather(): return lax.all_gather(value, 'mod', axis=axis, tiled=True)]
    ppermute x0 -> x122, waiting for transfers between devices: none -> 579 us  [the longest x69 340 us: along_z(): return lax.ppermute(value, 'batch', pairs)]
    unnamed x33 -> x15, waiting for transfers between devices: 382 us -> 0.25 us
    ppermute x0 -> x122, starting transfers between devices: none -> 261 us  [the longest x69 202 us: along_z(): return lax.ppermute(value, 'batch', pairs)]
    unnamed x98 -> x305, local copies, waits for them, and re-layouts: 37.9 us -> 108 us
    all_gather x0 -> x6, local copies, waits for them, and re-layouts: none -> 37.4 us  [mod_gather(): return lax.all_gather(value, 'mod', axis=axis, tiled=True)]
    dynamic_update_slice x0 -> x8, local copies, waits for them, and re-layouts: none -> 28.8 us  [local(): lax.dynamic_update_slice_in_dim(proj_w, patch_parts[p], ex.source(p) * pr...]
  transfers between devices with their start and end apart: 31 -> 138, of which waited for: 30 -> 58; matrix products, arithmetic and copies ran while one was open for 10% -> 28% of each run, Pallas kernels for 0% -> 0%
where the time goes in v1:
time: 1530 us; the launch traced here: 1520 us
  waiting for transfers between devices  672 us (44%)
  starting transfers between devices  266 us (17%)
  local copies, waits for them, and re-layouts  255 us (17%)
  matrix products  228 us (15%)
  other arithmetic  62.6 us (4%)
  blocking collectives  19.7 us (1%)
  between operations  16.1 us (1%)
    ppermute x69, waiting for transfers between devices, along_z(): return lax.ppermute(value, 'batch', pairs)  340 us
    ppermute x53, waiting for transfers between devices, along_x(): return lax.ppermute(value, 'batch', [(b, b ^ 1) for b in range(self.size)])  239 us
    dot_general x52, matrix products, dot(): return jnp.einsum(spec, a, b, preferred_element_type=F32)  228 us
    ppermute x69, starting transfers between devices, along_z(): return lax.ppermute(value, 'batch', pairs)  202 us
    unnamed x305, local copies, waits for them, and re-layouts  108 us
    ppermute x53, starting transfers between devices, along_x(): return lax.ppermute(value, 'batch', [(b, b ^ 1) for b in range(self.size)])  58.7 us
    reduce_scatter x6, waiting for transfers between devices, mod_sum(): lax.psum_scatter(partial.astype(BF), 'mod', scatter_dimension=0, tiled=True)  52.5 us
    all_gather x6, local copies, waits for them, and re-layouts, mod_gather(): return lax.all_gather(value, 'mod', axis=axis, tiled=True)  37.4 us
  transfers between devices with their start and end apart: 138, of which 58 were waited for; matrix products, arithmetic and copies ran while one was open for 28% of the time, Pallas kernels for 0%

profile of v1, /device:TPU:0, one launch (start us, length us, event | category | flops | bytes accessed | tf_op | source)
XLA Modules:
  0.0 1520.0 jit_solution(1140911036341101944)
XLA Ops:
  36.3 23.6 %collective-permute-done.5 = bf16[3,256,512]{1,2,0:T(8,128)(2,1)S(1)} collective-permute-done((bf16[3,256,512]{1,2,0:T(8,128)(2,1)S(1)}, bf16[3,256,512]{1,2,0:T(8,128)(2,1)S(1)}, u32[]{:S(2)}, u32[]{:S(2)}) %collective-permute-start.5) | collective-permute-done | bytes 786464 | tf_op jit(solution)/shard_map/ppermute | solution.py:60
  67.7 26.1 %collective-permute-done.3 = bf16[3,256,512]{1,2,0:T(8,128)(2,1)} collective-permute-done((bf16[3,256,512]{1,2,0:T(8,128)(2,1)S(1)}, bf16[3,256,512]{1,2,0:T(8,128)(2,1)}, u32[]{:S(2)}, u32[]{:S(2)}) %collective-permute-start.3) | collective-permute-done | bytes 786464 | tf_op jit(solution)/shard_map/ppermute | solution.py:60
  147.0 10.3 convert_bitcast_fusion
  169.7 9.3 all-gather.2
  191.5 8.3 collective-permute-done.33
  260.9 7.6 collective-permute-done.38
  270.9 6.6 collective-permute-done.40
  291.3 25.6 %collective-permute-done.26 = bf16[2,256,512]{1,2,0:T(8,128)(2,1)S(1)} collective-permute-done((bf16[2,256,512]{1,2,0:T(8,128)(2,1)S(1)}, bf16[2,256,512]{1,2,0:T(8,128)(2,1)S(1)}, u32[]{:S(2)}, u32[]{:S(2)}) %collective-permute-start.26) | collective-permute-done | bytes 524320 | tf_op jit(solution)/shard_map/ppermute | solution.py:60
  318.6 8.3 collective-permute-done.29
  416.6 18.7 %collective-permute-done.54 = bf16[256,1280]{1,0:T(8,128)(2,1)S(1)} collective-permute-done((bf16[256,1280]{1,0:T(8,128)(2,1)}, bf16[256,1280]{1,0:T(8,128)(2,1)S(1)}, u32[]{:S(2)}, u32[]{:S(2)}) %collective-permute-start.54) | collective-permute-done | bytes 655392 | tf_op jit(solution)/shard_map/ppermute | solution.py:60
  443.6 23.3 %collective-permute-done.52 = bf16[256,1280]{1,0:T(8,128)(2,1)} collective-permute-done((bf16[256,1280]{1,0:T(8,128)(2,1)}, bf16[256,1280]{1,0:T(8,128)(2,1)}, u32[]{:S(2)}, u32[]{:S(2)}) %collective-permute-start.52) | collective-permute-done | bytes 655392 | tf_op jit(solution)/shard_map/ppermute | solution.py:60
  491.7 12.2 collective-permute-done.57
  504.5 24.7 %collective-permute-done.59 = bf16[256,1280]{1,0:T(8,128)(2,1)S(1)} collective-permute-done((bf16[256,1280]{1,0:T(8,128)(2,1)}, bf16[256,1280]{1,0:T(8,128)(2,1)S(1)}, u32[]{:S(2)}, u32[]{:S(2)}) %collective-permute-start.59) | collective-permute-done | bytes 655392 | tf_op jit(solution)/shard_map/ppermute | solution.py:60
  556.4 23.8 %collective-permute-done.66 = bf16[256,1280]{1,0:T(8,128)(2,1)S(1)} collective-permute-done((bf16[256,1280]{1,0:T(8,128)(2,1)S(1)}, bf16[256,1280]{1,0:T(8,128)(2,1)S(1)}, u32[]{:S(2)}, u32[]{:S(2)}) %collective-permute-start.66) | collective-permute-done | bytes 655392 | tf_op jit(solution)/shard_map/ppermute | solution.py:60
  585.9 12.1 collective-permute-done.67
  599.7 10.2 collective-permute-done.69
  610.8 10.4 fusion.14
  621.2 10.5 fusion.20
  631.8 14.6 fusion.13
  646.4 7.8 fusion.18
  654.2 9.5 add_convert_fusion
  664.0 52.5 %reduce-scatter.14.cloned.1.call-done = bf16[1,256,2048]{2,1,0:T(8,128)(2,1)} async-done(((bf16[4,256,2048]{2,1,0:T(8,128)(2,1)}), bf16[1,256,2048]{2,1,0:T(8,128)(2,1)}) %reduce-scatter.14.cloned.1.call-update) | async-done | bytes 1048592 | tf_op jit(solution)/shard_map/reduce_scatter | solution.py:148
  721.2 34.6 %all-gather.25.cloned.1.call-done = bf16[4,256,2048]{2,1,0:T(8,128)(2,1)} async-done(((bf16[1,256,2048]{2,1,0:T(8,128)(2,1)}), bf16[4,256,2048]{2,1,0:T(8,128)(2,1)}) %all-gather.25.cloned.1.call-update) | async-done | bytes 4194320 | tf_op jit(solution)/shard_map/all_gather | solution.py:144
  776.4 10.1 fusion.31
  831.8 7.9 bitcast_convert_fusion
  863.3 12.2 collective-permute-done.114
  875.5 6.3 fusion.215
  886.6 45.1 %collective-permute-done.118 = bf16[4,256,1280]{2,1,0:T(8,128)(2,1)} collective-permute-done((bf16[4,256,1280]{2,1,0:T(8,128)(2,1)}, bf16[4,256,1280]{2,1,0:T(8,128)(2,1)}, u32[]{:S(2)}, u32[]{:S(2)}) %collective-permute-start.118) | collective-permute-done | bytes 2621472 | tf_op jit(solution)/shard_map/ppermute | solution.py:63
  940.0 47.0 %collective-permute-done.110 = bf16[4,256,1280]{2,1,0:T(8,128)(2,1)S(1)} collective-permute-done((bf16[4,256,1280]{2,1,0:T(8,128)(2,1)S(1)}, bf16[4,256,1280]{2,1,0:T(8,128)(2,1)S(1)}, u32[]{:S(2)}, u32[]{:S(2)}) %collective-permute-start.110) | collective-permute-done | bytes 2621472 | tf_op jit(solution)/shard_map/ppermute | solution.py:63
  998.1 7.2 collective-permute-done.119
  1023.1 38.5 %collective-permute-done.113 = bf16[256,1280]{1,0:T(8,128)(2,1)} collective-permute-done((bf16[256,1280]{1,0:T(8,128)(2,1)}, bf16[256,1280]{1,0:T(8,128)(2,1)}, u32[]{:S(2)}, u32[]{:S(2)}) %collective-permute-start.113) | collective-permute-done | bytes 655392 | tf_op jit(solution)/shard_map/ppermute | solution.py:60
  1087.9 6.4 copy.452
  1099.5 6.7 collective-permute-done.90
  1111.2 15.8 %collective-permute-start.93 = (bf16[256,512]{1,0:T(8,128)(2,1)}, bf16[256,512]{1,0:T(8,128)(2,1)}, u32[]{:S(2)}, u32[]{:S(2)}) collective-permute-start(bf16[256,512]{1,0:T(8,128)(2,1)} %get-tuple-element.156), channel_id=1, source_target_pairs={{0,16},{4,20},{8,24},{12,28},{16,0},{20,4},{24,8},{28,12},{1,17},{... | collective-permute-start | bytes 786440 | tf_op jit(solution)/shard_map/ppermute | solution.py:60
  1131.3 15.9 %collective-permute-start.101 = (bf16[256,512]{1,0:T(8,128)(2,1)S(1)}, bf16[256,512]{1,0:T(8,128)(2,1)S(1)}, u32[]{:S(2)}, u32[]{:S(2)}) collective-permute-start(bf16[256,512]{1,0:T(8,128)(2,1)S(1)} %get-tuple-element.153), channel_id=1, source_target_pairs={{0,16},{4,20},{8,24},{12,28},{16,0},{20,4},{24,8},{28,12},{1,17},{... | collective-permute-start | bytes 786440 | tf_op jit(solution)/shard_map/ppermute | solution.py:60
  1151.2 13.9 collective-permute-start.100
  1177.5 14.5 collective-permute-start.97
  1197.6 23.4 %collective-permute-done.97 = bf16[256,512]{1,0:T(8,128)(2,1)S(1)} collective-permute-done((bf16[256,512]{1,0:T(8,128)(2,1)S(1)}, bf16[256,512]{1,0:T(8,128)(2,1)S(1)}, u32[]{:S(2)}, u32[]{:S(2)}) %collective-permute-start.97) | collective-permute-done | bytes 262176 | tf_op jit(solution)/shard_map/ppermute | solution.py:60
  1252.0 10.7 bitcast_convert_fusion.1
  1279.0 6.7 collective-permute-done.106
  1296.4 9.8 collective-permute-done.109
  1347.4 9.2 collective-permute-done.82
  1366.1 12.9 collective-permute-done.86
  1386.6 14.9 collective-permute-done.78
  1409.0 13.6 collective-permute-done.74
  1443.9 15.1 collective-permute-done.81
  1464.9 15.1 collective-permute-done.77
  1495.3 6.7 collective-permute-start.73
  (752 shorter events, 727.7 us)
Async XLA Ops:
  7.2 129.1 %all-gather.13.cloned.1.call-start = ((), (), s32[]{:S(2)}) async-start(), calls=%async_computation.8 | async-start | bytes 5242880 | tf_op jit(solution)/shard_map/all_gather | solution.py:144
  15.9 217.1 %all-gather.15.cloned.1.call-start = ((), (), s32[]{:S(2)}) async-start(), calls=%async_computation.10 | async-start | bytes 4259840 | tf_op jit(solution)/shard_map/all_gather | solution.py:144
  25.3 213.5 %reduce-scatter.8.cloned.1.call-start = ((), (), s32[]{:S(2)}) async-start(), calls=%async_computation.9 | async-start | bytes 5242880 | tf_op jit(solution)/shard_map/reduce_scatter | solution.py:148
  29.0 64.8 %collective-permute-start.3 = (bf16[3,256,512]{1,2,0:T(8,128)(2,1)S(1)}, bf16[3,256,512]{1,2,0:T(8,128)(2,1)}, u32[]{:S(2)}, u32[]{:S(2)}) collective-permute-start(bf16[3,256,512]{1,2,0:T(8,128)(2,1)S(1)} %copy.376), channel_id=1, source_target_pairs={{0,16},{4,20},{8,24},{12,28},{16,0},{20,4},{24,8},{28,12},{1,17},{... | collective-permute-start | bytes 2359304 | tf_op jit(solution)/shard_map/ppermute | solution.py:60
  32.6 61.8 %collective-permute-start = (bf16[3,256,512]{1,2,0:T(8,128)(2,1)S(1)}, bf16[3,256,512]{1,2,0:T(8,128)(2,1)}, u32[]{:S(2)}, u32[]{:S(2)}) collective-permute-start(bf16[3,256,512]{1,2,0:T(8,128)(2,1)S(1)} %copy.376), channel_id=1, source_target_pairs={{0,4},{4,0},{8,12},{12,8},{16,20},{20,16},{24,28},{28,24},{1,5},{5... | collective-permute-start | bytes 2359304 | tf_op jit(solution)/shard_map/ppermute | solution.py:63
  168.8 192.6 %all-gather.17.cloned.1.call-start = ((), (), s32[]{:S(2)}) async-start(), calls=%async_computation.11 | async-start | bytes 5242880 | tf_op jit(solution)/shard_map/all_gather | solution.py:144
  238.7 135.7 %all-gather.19.cloned.1.call-start = ((), (), s32[]{:S(2)}) async-start(), calls=%async_computation.12 | async-start | bytes 5242880 | tf_op jit(solution)/shard_map/all_gather | solution.py:144
  242.2 234.7 %reduce-scatter.10.cloned.1.call-start = ((), (), s32[]{:S(2)}) async-start(), calls=%async_computation.13 | async-start | bytes 5242880 | tf_op jit(solution)/shard_map/reduce_scatter | solution.py:148
  287.2 46.5 %collective-permute-start.25 = (bf16[2,256,512]{1,2,0:T(8,128)(2,1)S(1)}, bf16[2,256,512]{1,2,0:T(8,128)(2,1)S(1)}, u32[]{:S(2)}, u32[]{:S(2)}) collective-permute-start(bf16[2,256,512]{1,2,0:T(8,128)(2,1)S(1)} %collective-permute-done.24), channel_id=1, source_target_pairs={{0,4},{4,0},{8,12},{12,8},{16,20},{20,16},{24,28},{28,24},{1,5},{5... | collective-permute-start | bytes 1572872 | tf_op jit(solution)/shard_map/ppermute | solution.py:63
  395.6 215.2 %all-gather.23.cloned.1.call-start = ((), (), s32[]{:S(2)}) async-start(), calls=%async_computation.16 | async-start | bytes 5242880 | tf_op jit(solution)/shard_map/all_gather | solution.py:144
  404.7 216.5 %all-gather.21.cloned.1.call-start = ((), (), s32[]{:S(2)}) async-start(), calls=%async_computation.14 | async-start | bytes 5242880 | tf_op jit(solution)/shard_map/all_gather | solution.py:144
  411.1 55.8 %collective-permute-start.52 = (bf16[256,1280]{1,0:T(8,128)(2,1)}, bf16[256,1280]{1,0:T(8,128)(2,1)}, u32[]{:S(2)}, u32[]{:S(2)}) collective-permute-start(bf16[256,1280]{1,0:T(8,128)(2,1)} %get-tuple-element.24), channel_id=1, source_target_pairs={{0,16},{4,20},{8,24},{12,28},{16,0},{20,4},{24,8},{28,12},{1,17},{... | collective-permute-start | bytes 1966088 | tf_op jit(solution)/shard_map/ppermute | solution.py:60
  412.6 55.8 %collective-permute-start.49 = (bf16[256,1280]{1,0:T(8,128)(2,1)}, bf16[256,1280]{1,0:T(8,128)(2,1)S(1)}, u32[]{:S(2)}, u32[]{:S(2)}) collective-permute-start(bf16[256,1280]{1,0:T(8,128)(2,1)} %get-tuple-element.24), channel_id=1, source_target_pairs={{0,4},{4,0},{8,12},{12,8},{16,20},{20,16},{24,28},{28,24},{1,5},{5... | collective-permute-start | bytes 1966088 | tf_op jit(solution)/shard_map/ppermute | solution.py:63
  473.9 55.9 %collective-permute-start.56 = (bf16[256,1280]{1,0:T(8,128)(2,1)}, bf16[256,1280]{1,0:T(8,128)(2,1)}, u32[]{:S(2)}, u32[]{:S(2)}) collective-permute-start(bf16[256,1280]{1,0:T(8,128)(2,1)} %get-tuple-element.25), channel_id=1, source_target_pairs={{0,4},{4,0},{8,12},{12,8},{16,20},{20,16},{24,28},{28,24},{1,5},{5... | collective-permute-start | bytes 1966088 | tf_op jit(solution)/shard_map/ppermute | solution.py:63
  480.4 236.1 %reduce-scatter.14.cloned.1.call-start = ((), (), s32[]{:S(2)}) async-start(), calls=%async_computation.17 | async-start | bytes 5242880 | tf_op jit(solution)/shard_map/reduce_scatter | solution.py:148
  480.4 48.8 %collective-permute-start.59 = (bf16[256,1280]{1,0:T(8,128)(2,1)}, bf16[256,1280]{1,0:T(8,128)(2,1)S(1)}, u32[]{:S(2)}, u32[]{:S(2)}) collective-permute-start(bf16[256,1280]{1,0:T(8,128)(2,1)} %get-tuple-element.25), channel_id=1, source_target_pairs={{0,16},{4,20},{8,24},{12,28},{16,0},{20,4},{24,8},{28,12},{1,17},{... | collective-permute-start | bytes 1966088 | tf_op jit(solution)/shard_map/ppermute | solution.py:60
  489.4 44.4 %collective-permute-start.62 = (bf16[256,1280]{1,0:T(8,128)(2,1)}, bf16[256,1280]{1,0:T(8,128)(2,1)S(1)}, u32[]{:S(2)}, u32[]{:S(2)}) collective-permute-start(bf16[256,1280]{1,0:T(8,128)(2,1)} %collective-permute-done.61), channel_id=1, source_target_pairs={{0,4},{4,0},{8,12},{12,8},{16,20},{20,16},{24,28},{28,24},{1,5},{5... | collective-permute-start | bytes 1966088 | tf_op jit(solution)/shard_map/ppermute | solution.py:63
  533.8 48.5 %collective-permute-start.63 = (bf16[256,1280]{1,0:T(8,128)(2,1)S(1)}, bf16[256,1280]{1,0:T(8,128)(2,1)S(1)}, u32[]{:S(2)}, u32[]{:S(2)}) collective-permute-start(bf16[256,1280]{1,0:T(8,128)(2,1)S(1)} %bitcast.755), channel_id=1, source_target_pairs={{0,4},{4,0},{8,12},{12,8},{16,20},{20,16},{24,28},{28,24},{1,5},{5... | collective-permute-start | bytes 1966088 | tf_op jit(solution)/shard_map/ppermute | solution.py:63
  535.6 44.6 %collective-permute-start.66 = (bf16[256,1280]{1,0:T(8,128)(2,1)S(1)}, bf16[256,1280]{1,0:T(8,128)(2,1)S(1)}, u32[]{:S(2)}, u32[]{:S(2)}) collective-permute-start(bf16[256,1280]{1,0:T(8,128)(2,1)S(1)} %bitcast.757), channel_id=1, source_target_pairs={{0,16},{4,20},{8,24},{12,28},{16,0},{20,4},{24,8},{28,12},{1,17},{... | collective-permute-start | bytes 1966088 | tf_op jit(solution)/shard_map/ppermute | solution.py:60
  663.7 92.1 %all-gather.25.cloned.1.call-start = ((), (), s32[]{:S(2)}) async-start(), calls=%async_computation.18 | async-start | bytes 5242880 | tf_op jit(solution)/shard_map/all_gather | solution.py:144
  721.2 343.7 %reduce-scatter.16.cloned.1.call-start = ((), (), s32[]{:S(2)}) async-start(), calls=%async_computation.19 | async-start | bytes 5242880 | tf_op jit(solution)/shard_map/reduce_scatter | solution.py:148
  776.3 290.8 %reduce-scatter.12.cloned.1.call-start = ((), (), s32[]{:S(2)}) async-start(), calls=%async_computation.15 | async-start | bytes 5242880 | tf_op jit(solution)/shard_map/reduce_scatter | solution.py:148
  786.5 439.2 %reduce-scatter.20.cloned.1.call-start = ((), (), s32[]{:S(2)}) async-start(), calls=%async_computation.22 | async-start | bytes 5242880 | tf_op jit(solution)/shard_map/reduce_scatter | solution.py:250
  815.5 60.0 %collective-permute-start.114 = (bf16[4,256,1280]{2,1,0:T(8,128)(2,1)}, bf16[4,256,1280]{2,1,0:T(8,128)(2,1)}, u32[]{:S(2)}, u32[]{:S(2)}) collective-permute-start(bf16[4,256,1280]{2,1,0:T(8,128)(2,1)} %bitcast_convert_fusion.3), channel_id=1, source_target_pairs={{0,4},{4,0},{8,12},{12,8},{16,20},{20,16},{24,28},{28,24},{1,5},{5... | collective-permute-start | bytes 7864328 | tf_op jit(solution)/shard_map/ppermute | solution.py:63
  820.7 111.0 %collective-permute-start.118 = (bf16[4,256,1280]{2,1,0:T(8,128)(2,1)}, bf16[4,256,1280]{2,1,0:T(8,128)(2,1)}, u32[]{:S(2)}, u32[]{:S(2)}) collective-permute-start(bf16[4,256,1280]{2,1,0:T(8,128)(2,1)} %bitcast_convert_fusion.2), channel_id=1, source_target_pairs={{0,4},{4,0},{8,12},{12,8},{16,20},{20,16},{24,28},{28,24},{1,5},{5... | collective-permute-start | bytes 7864328 | tf_op jit(solution)/shard_map/ppermute | solution.py:63
  843.0 389.3 %all-gather.27.cloned.1.call-start = ((), (), s32[]{:S(2)}) async-start(), calls=%async_computation.20 | async-start | bytes 5242880 | tf_op jit(solution)/shard_map/all_gather | solution.py:144
  862.0 125.0 %collective-permute-start.110 = (bf16[4,256,1280]{2,1,0:T(8,128)(2,1)S(1)}, bf16[4,256,1280]{2,1,0:T(8,128)(2,1)S(1)}, u32[]{:S(2)}, u32[]{:S(2)}) collective-permute-start(bf16[4,256,1280]{2,1,0:T(8,128)(2,1)S(1)} %bitcast_convert_fusion.4), channel_id=1, source_target_pairs={{0,4},{4,0},{8,12},{12,8},{16,20},{20,16},{24,28},{28,24},{1,5},{5... | collective-permute-start | bytes 7864328 | tf_op jit(solution)/shard_map/ppermute | solution.py:63
  883.0 111.6 %collective-permute-start.117 = (bf16[256,1280]{1,0:T(8,128)(2,1)S(1)}, bf16[256,1280]{1,0:T(8,128)(2,1)S(1)}, u32[]{:S(2)}, u32[]{:S(2)}) collective-permute-start(bf16[256,1280]{1,0:T(8,128)(2,1)S(1)} %get-tuple-element.127), channel_id=1, source_target_pairs={{0,16},{4,20},{8,24},{12,28},{16,0},{20,4},{24,8},{28,12},{1,17},{... | collective-permute-start | bytes 1966088 | tf_op jit(solution)/shard_map/ppermute | solution.py:60
  885.1 128.7 %collective-permute-start.116 = (bf16[256,1280]{1,0:T(8,128)(2,1)}, bf16[256,1280]{1,0:T(8,128)(2,1)}, u32[]{:S(2)}, u32[]{:S(2)}) collective-permute-start(bf16[256,1280]{1,0:T(8,128)(2,1)} %get-tuple-element.128), channel_id=1, source_target_pairs={{0,8},{4,12},{8,16},{12,20},{16,24},{20,28},{24,0},{28,4},{1,9},{5... | collective-permute-start | bytes 1966088 | tf_op jit(solution)/shard_map/ppermute | solution.py:60
  936.5 60.1 %collective-permute-start.121 = (bf16[256,1280]{1,0:T(8,128)(2,1)S(1)}, bf16[256,1280]{1,0:T(8,128)(2,1)S(1)}, u32[]{:S(2)}, u32[]{:S(2)}) collective-permute-start(bf16[256,1280]{1,0:T(8,128)(2,1)S(1)} %get-tuple-element.121), channel_id=1, source_target_pairs={{0,16},{4,20},{8,24},{12,28},{16,0},{20,4},{24,8},{28,12},{1,17},{... | collective-permute-start | bytes 1966088 | tf_op jit(solution)/shard_map/ppermute | solution.py:60
  938.5 58.1 %collective-permute-start.120 = (bf16[256,1280]{1,0:T(8,128)(2,1)S(1)}, bf16[256,1280]{1,0:T(8,128)(2,1)S(1)}, u32[]{:S(2)}, u32[]{:S(2)}) collective-permute-start(bf16[256,1280]{1,0:T(8,128)(2,1)S(1)} %get-tuple-element.122), channel_id=1, source_target_pairs={{0,8},{4,12},{8,16},{12,20},{16,24},{20,28},{24,0},{28,4},{1,9},{5... | collective-permute-start | bytes 1966088 | tf_op jit(solution)/shard_map/ppermute | solution.py:60
  996.6 65.0 %collective-permute-start.113 = (bf16[256,1280]{1,0:T(8,128)(2,1)}, bf16[256,1280]{1,0:T(8,128)(2,1)}, u32[]{:S(2)}, u32[]{:S(2)}) collective-permute-start(bf16[256,1280]{1,0:T(8,128)(2,1)} %get-tuple-element.124), channel_id=1, source_target_pairs={{0,16},{4,20},{8,24},{12,28},{16,0},{20,4},{24,8},{28,12},{1,17},{... | collective-permute-start | bytes 1966088 | tf_op jit(solution)/shard_map/ppermute | solution.py:60
  996.6 65.0 %collective-permute-start.112 = (bf16[256,1280]{1,0:T(8,128)(2,1)}, bf16[256,1280]{1,0:T(8,128)(2,1)}, u32[]{:S(2)}, u32[]{:S(2)}) collective-permute-start(bf16[256,1280]{1,0:T(8,128)(2,1)} %get-tuple-element.125), channel_id=1, source_target_pairs={{0,8},{4,12},{8,16},{12,20},{16,24},{20,28},{24,0},{28,4},{1,9},{5... | collective-permute-start | bytes 1966088 | tf_op jit(solution)/shard_map/ppermute | solution.py:60
  1005.4 56.3 %collective-permute-start.111 = (bf16[256,1280]{1,0:T(8,128)(2,1)}, bf16[256,1280]{1,0:T(8,128)(2,1)}, u32[]{:S(2)}, u32[]{:S(2)}) collective-permute-start(bf16[256,1280]{1,0:T(8,128)(2,1)} %get-tuple-element.123), channel_id=1, source_target_pairs={{0,24},{4,28},{8,0},{12,4},{16,8},{20,12},{24,16},{28,20},{1,25},{... | collective-permute-start | bytes 1966088 | tf_op jit(solution)/shard_map/ppermute | solution.py:60
  1072.1 410.4 %reduce-scatter.18.cloned.1.call-start = ((), (), s32[]{:S(2)}) async-start(), calls=%async_computation.21 | async-start | bytes 5242880 | tf_op jit(solution)/shard_map/reduce_scatter | solution.py:148
  1083.6 45.1 %collective-permute-start.98 = (bf16[4,256,512]{2,1,0:T(8,128)(2,1)}, bf16[4,256,512]{2,1,0:T(8,128)(2,1)}, u32[]{:S(2)}, u32[]{:S(2)}) collective-permute-start(bf16[4,256,512]{2,1,0:T(8,128)(2,1)} %bitcast_convert_fusion.7), channel_id=1, source_target_pairs={{0,4},{4,0},{8,12},{12,8},{16,20},{20,16},{24,28},{28,24},{1,5},{5... | collective-permute-start | bytes 3145736 | tf_op jit(solution)/shard_map/ppermute | solution.py:63
  1086.4 64.7 %collective-permute-start.94 = (bf16[4,256,512]{2,1,0:T(8,128)(2,1)}, bf16[4,256,512]{2,1,0:T(8,128)(2,1)}, u32[]{:S(2)}, u32[]{:S(2)}) collective-permute-start(bf16[4,256,512]{2,1,0:T(8,128)(2,1)} %bitcast_convert_fusion.8), channel_id=1, source_target_pairs={{0,4},{4,0},{8,12},{12,8},{16,20},{20,16},{24,28},{28,24},{1,5},{5... | collective-permute-start | bytes 3145736 | tf_op jit(solution)/shard_map/ppermute | solution.py:63
  1098.4 71.3 %collective-permute-start.102 = (bf16[4,256,512]{2,1,0:T(8,128)(2,1)S(1)}, bf16[4,256,512]{2,1,0:T(8,128)(2,1)S(1)}, u32[]{:S(2)}, u32[]{:S(2)}) collective-permute-start(bf16[4,256,512]{2,1,0:T(8,128)(2,1)S(1)} %bitcast_convert_fusion.6), channel_id=1, source_target_pairs={{0,4},{4,0},{8,12},{12,8},{16,20},{20,16},{24,28},{28,24},{1,5},{5... | collective-permute-start | bytes 3145736 | tf_op jit(solution)/shard_map/ppermute | solution.py:63
  1111.2 163.4 %collective-permute-start.93 = (bf16[256,512]{1,0:T(8,128)(2,1)}, bf16[256,512]{1,0:T(8,128)(2,1)}, u32[]{:S(2)}, u32[]{:S(2)}) collective-permute-start(bf16[256,512]{1,0:T(8,128)(2,1)} %get-tuple-element.156), channel_id=1, source_target_pairs={{0,16},{4,20},{8,24},{12,28},{16,0},{20,4},{24,8},{28,12},{1,17},{... | collective-permute-start | bytes 786440 | tf_op jit(solution)/shard_map/ppermute | solution.py:60
  1127.0 147.6 %collective-permute-start.92 = (bf16[256,512]{1,0:T(8,128)(2,1)}, bf16[256,512]{1,0:T(8,128)(2,1)}, u32[]{:S(2)}, u32[]{:S(2)}) collective-permute-start(bf16[256,512]{1,0:T(8,128)(2,1)} %get-tuple-element.157), channel_id=1, source_target_pairs={{0,8},{4,12},{8,16},{12,20},{16,24},{20,28},{24,0},{28,4},{1,9},{5... | collective-permute-start | bytes 786440 | tf_op jit(solution)/shard_map/ppermute | solution.py:60
  1131.3 46.2 %collective-permute-start.101 = (bf16[256,512]{1,0:T(8,128)(2,1)S(1)}, bf16[256,512]{1,0:T(8,128)(2,1)S(1)}, u32[]{:S(2)}, u32[]{:S(2)}) collective-permute-start(bf16[256,512]{1,0:T(8,128)(2,1)S(1)} %get-tuple-element.153), channel_id=1, source_target_pairs={{0,16},{4,20},{8,24},{12,28},{16,0},{20,4},{24,8},{28,12},{1,17},{... | collective-permute-start | bytes 786440 | tf_op jit(solution)/shard_map/ppermute | solution.py:60
  1221.0 47.2 %collective-permute-start.104 = (bf16[256,512]{1,0:T(8,128)(2,1)}, bf16[256,512]{1,0:T(8,128)(2,1)}, u32[]{:S(2)}, u32[]{:S(2)}) collective-permute-start(bf16[256,512]{1,0:T(8,128)(2,1)} %get-tuple-element.148), channel_id=1, source_target_pairs={{0,8},{4,12},{8,16},{12,20},{16,24},{20,28},{24,0},{28,4},{1,9},{5... | collective-permute-start | bytes 786440 | tf_op jit(solution)/shard_map/ppermute | solution.py:60
  1221.0 48.7 %collective-permute-start.103 = (bf16[256,512]{1,0:T(8,128)(2,1)}, bf16[256,512]{1,0:T(8,128)(2,1)}, u32[]{:S(2)}, u32[]{:S(2)}) collective-permute-start(bf16[256,512]{1,0:T(8,128)(2,1)} %get-tuple-element.146), channel_id=1, source_target_pairs={{0,24},{4,28},{8,0},{12,4},{16,8},{20,12},{24,16},{28,20},{1,25},{... | collective-permute-start | bytes 786440 | tf_op jit(solution)/shard_map/ppermute | solution.py:60
  1343.9 57.6 %collective-permute-start.78 = (bf16[4,256,512]{2,1,0:T(8,128)(2,1)S(1)}, bf16[4,256,512]{2,1,0:T(8,128)(2,1)S(1)}, u32[]{:S(2)}, u32[]{:S(2)}) collective-permute-start(bf16[4,256,512]{2,1,0:T(8,128)(2,1)S(1)} %bitcast_convert_fusion.12), channel_id=1, source_target_pairs={{0,4},{4,0},{8,12},{12,8},{16,20},{20,16},{24,28},{28,24},{1,5},{5... | collective-permute-start | bytes 3145736 | tf_op jit(solution)/shard_map/ppermute | solution.py:63
  1346.7 75.8 %collective-permute-start.74 = (bf16[4,256,512]{2,1,0:T(8,128)(2,1)S(1)}, bf16[4,256,512]{2,1,0:T(8,128)(2,1)S(1)}, u32[]{:S(2)}, u32[]{:S(2)}) collective-permute-start(bf16[4,256,512]{2,1,0:T(8,128)(2,1)S(1)} %bitcast_convert_fusion.13), channel_id=1, source_target_pairs={{0,4},{4,0},{8,12},{12,8},{16,20},{20,16},{24,28},{28,24},{1,5},{5... | collective-permute-start | bytes 3145736 | tf_op jit(solution)/shard_map/ppermute | solution.py:63
  1359.9 76.7 %collective-permute-start.85 = (bf16[256,512]{1,0:T(8,128)(2,1)}, bf16[256,512]{1,0:T(8,128)(2,1)S(1)}, u32[]{:S(2)}, u32[]{:S(2)}) collective-permute-start(bf16[256,512]{1,0:T(8,128)(2,1)} %get-tuple-element.168), channel_id=1, source_target_pairs={{0,16},{4,20},{8,24},{12,28},{16,0},{20,4},{24,8},{28,12},{1,17},{... | collective-permute-start | bytes 786440 | tf_op jit(solution)/shard_map/ppermute | solution.py:60
  1366.1 73.7 %collective-permute-start.84 = (bf16[256,512]{1,0:T(8,128)(2,1)S(1)}, bf16[256,512]{1,0:T(8,128)(2,1)S(1)}, u32[]{:S(2)}, u32[]{:S(2)}) collective-permute-start(bf16[256,512]{1,0:T(8,128)(2,1)S(1)} %get-tuple-element.169), channel_id=1, source_target_pairs={{0,8},{4,12},{8,16},{12,20},{16,24},{20,28},{24,0},{28,4},{1,9},{5... | collective-permute-start | bytes 786440 | tf_op jit(solution)/shard_map/ppermute | solution.py:60
  1380.4 50.6 %collective-permute-start.89 = (bf16[256,512]{1,0:T(8,128)(2,1)S(1)}, bf16[256,512]{1,0:T(8,128)(2,1)S(1)}, u32[]{:S(2)}, u32[]{:S(2)}) collective-permute-start(bf16[256,512]{1,0:T(8,128)(2,1)S(1)} %get-tuple-element.159), channel_id=1, source_target_pairs={{0,16},{4,20},{8,24},{12,28},{16,0},{20,4},{24,8},{28,12},{1,17},{... | collective-permute-start | bytes 786440 | tf_op jit(solution)/shard_map/ppermute | solution.py:60
  (186 other events, 2807.8 us)
Sparse Core Ops, SparseCore 0:
  16.1 37.1 all-gather.12
  54.8 30.1 all-gather.14
  168.9 46.6 reduce-scatter.7
  238.8 36.8 all-gather.16
  277.8 34.4 all-gather.18
  395.7 45.0 reduce-scatter.9
  442.9 34.4 all-gather.22
  480.5 34.7 all-gather.20
  663.9 52.6 reduce-scatter.13
  721.3 34.4 all-gather.24
  776.5 44.5 reduce-scatter.15
  823.4 44.5 reduce-scatter.11
  870.6 44.5 reduce-scatter.19
  1072.2 47.0 all-gather.26
  1262.8 45.0 reduce-scatter.17

commit v2 on v1

--- a/solution.py
+++ b/solution.py
@@ -1,6 +1,10 @@
+import functools
+
 import jax
 import jax.numpy as jnp
 from jax import lax
+from jax.experimental import pallas as pl
+from jax.experimental.pallas import tpu as pltpu
 from jax.sharding import PartitionSpec as P
 
 HD = 128
@@ -90,6 +94,582 @@
         for s in self.shifts():
             result = result + self.along_z(send[s], self.n_out - s).astype(F32)
         return result
+
+
+MESH = pl.DeviceIdType.MESH
+
+
+class Place:
+    def __init__(self, n_batch):
+        self.n_batch = n_batch
+        self.n_out = n_batch // 2
+        self.b = lax.axis_index("batch")
+        self.m = lax.axis_index("mod")
+        self.outer = self.b // 2
+        self.inner = self.b % 2
+        self.core = self.m + 1 - 2 * (self.m % 2)
+        self.far = (self.m + 2) % 4
+        self.farcore = (self.core + 2) % 4
+        self.x_peer = self.b + 1 - 2 * self.inner
+        self.shifts = []
+        for d in range(1, self.n_out // 2 + 1):
+            self.shifts += [d] if 2 * d == self.n_out else [d, self.n_out - d]
+
+    def z_peer(self, s):
+        return (self.outer + s) % self.n_out * 2 + self.inner
+
+    def z_from(self, s):
+        return (self.outer - s + self.n_out) % self.n_out * 2 + self.inner
+
+    def greet(self):
+        barrier = pltpu.get_barrier_semaphore()
+        ids = [{"batch": self.z_peer(s), "mod": self.m} for s in self.shifts]
+        ids.append({"batch": self.x_peer, "mod": self.m})
+        for j in (self.core, self.far, self.farcore):
+            ids.append({"batch": self.b, "mod": j})
+        for device in ids:
+            pl.semaphore_signal(barrier, inc=1, device_id=device, device_id_type=MESH)
+        pl.semaphore_wait(barrier, len(ids))
+
+
+def remote(src, dst, send, recv, **device):
+    return pltpu.make_async_remote_copy(
+        src_ref=src, dst_ref=dst, send_sem=send, recv_sem=recv, device_id=device, device_id_type=MESH
+    )
+
+
+class BatchGather:
+    def __init__(self, place, tensors, sems):
+        self.p = place
+        self.tensors = tensors
+        self.z_send, self.z_recv, self.x_send, self.x_recv, self.own = sems
+        self.started = 0
+        self.events = [(t, s) for t in range(len(tensors)) for s in [0] + place.shifts]
+        self.at = 0
+
+    @staticmethod
+    def semaphores(n_out, count):
+        dma = pltpu.SemaphoreType.DMA
+        return [dma((count, n_out)) for _ in range(4)] + [dma((count,))]
+
+    def z_copy(self, t, s):
+        src, block = self.tensors[t]
+        return remote(src, block(self.p.b), self.z_send.at[t, s], self.z_recv.at[t, s],
+                      batch=self.p.z_peer(s), mod=self.p.m)
+
+    def own_copy(self, t):
+        src, block = self.tensors[t]
+        return pltpu.make_async_copy(src, block(self.p.b), self.own.at[t])
+
+    def x_copy(self, t, s):
+        src, block = self.tensors[t]
+        where = block(self.p.z_from(s))
+        return remote(src if s == 0 else where, where, self.x_send.at[t, s], self.x_recv.at[t, s],
+                      batch=self.p.x_peer, mod=self.p.m)
+
+    def start(self, count=1):
+        for t in range(self.started, min(self.started + count, len(self.tensors))):
+            for s in self.p.shifts:
+                self.z_copy(t, s).start()
+            self.own_copy(t).start()
+            self.started = t + 1
+
+    def pump(self, upto):
+        while self.at < len(self.events) and self.events[self.at][0] <= upto:
+            t, s = self.events[self.at]
+            if s:
+                self.z_copy(t, s).wait_recv()
+                if s == self.p.shifts[-1]:
+                    self.start()
+            self.x_copy(t, s).start()
+            self.at += 1
+
+    def arrived(self, t, ahead=1):
+        self.pump(t + ahead)
+        self.own_copy(t).wait()
+        for s in [0] + self.p.shifts:
+            self.x_copy(t, s).wait_recv()
+
+    def sent(self):
+        for t in range(len(self.tensors)):
+            for s in self.p.shifts:
+                self.z_copy(t, s).wait_send()
+            for s in [0] + self.p.shifts:
+                self.x_copy(t, s).wait_send()
+
+
+class ModGather:
+    def __init__(self, place, block, send, recv):
+        self.p = place
+        self.block = block
+        mine = block(place.m)
+        far = block(place.far)
+        self.near = remote(mine, mine, send.at[0], recv.at[0], batch=place.b, mod=place.core)
+        self.across = remote(mine, mine, send.at[1], recv.at[1], batch=place.b, mod=place.far)
+        self.on = remote(far, far, send.at[2], recv.at[2], batch=place.b, mod=place.core)
+
+    def start(self):
+        self.across.start()
+        self.near.start()
+
+    def forward(self):
+        self.across.wait_recv()
+        self.on.start()
+
+    def finish(self):
+        self.near.wait_recv()
+        self.on.wait_recv()
+        self.near.wait_send()
+        self.across.wait_send()
+        self.on.wait_send()
+
+
+def first_kernel(n_batch, text, patches, gain_tile, patch_tile, w_qkv, w_so, w_co, w_down,
+                 text_all, patch_all, gain_all, patch_rows, qkv_all, so_t, co_t, down_t,
+                 gain_mod, gain_sum, z_send, z_recv, x_send, x_recv, own, mod_send, mod_recv, misc):
+    p = Place(n_batch)
+    rows = w_qkv.shape[1]
+    tensors = [
+        (w_qkv.at[0], lambda q: qkv_all.at[0, pl.ds(q * rows, rows)]),
+        (w_qkv.at[1], lambda q: qkv_all.at[1, pl.ds(q * rows, rows)]),
+        (gain_sum, lambda q: gain_all.at[q]),
+        (w_qkv.at[2], lambda q: qkv_all.at[2, pl.ds(q * rows, rows)]),
+    ]
+    g = BatchGather(p, tensors, (z_send, z_recv, x_send, x_recv, own))
+    copies = [
+        pltpu.make_async_copy(text, text_all.at[p.m], misc.at[0]),
+        pltpu.make_async_copy(patches, patch_all.at[p.m], misc.at[1]),
+        pltpu.make_async_copy(gain_tile, gain_mod.at[p.m], misc.at[2]),
+        pltpu.make_async_copy(patch_tile.at[p.m], patch_rows.at[p.m], misc.at[3]),
+    ]
+    for c in copies:
+        c.start()
+    p.greet()
+    gains = [
+        remote(gain_tile, gain_mod.at[p.m], mod_send.at[2, k], mod_recv.at[2, k], batch=p.b, mod=j)
+        for k, j in enumerate((p.core, p.far, p.farcore))
+    ]
+    for c in gains:
+        c.start()
+    g.start()
+    for c in copies:
+        c.wait()
+    text_g = ModGather(p, lambda j: text_all.at[j], mod_send.at[0], mod_recv.at[0])
+    patch_g = ModGather(p, lambda j: patch_all.at[j], mod_send.at[1], mod_recv.at[1])
+    text_g.start()
+    rows_c = [
+        remote(patch_tile.at[j], patch_rows.at[p.m], mod_send.at[3, k], mod_recv.at[3, k], batch=p.b, mod=j)
+        for k, j in enumerate((p.core, p.far, p.farcore))
+    ]
+    for c in rows_c:
+        c.start()
+    patch_g.start()
+    for c in gains:
+        c.wait_recv()
+    gain_sum[...] = gain_mod[0] + gain_mod[1] + gain_mod[2] + gain_mod[3]
+    so_t[...] = w_so[...].T
+    co_t[...] = w_co[...].T
+    down_t[...] = w_down[...].T
+    g.pump(0)
+    text_g.forward()
+    g.pump(1)
+    patch_g.forward()
+    for t in range(4):
+        g.arrived(t)
+    text_g.finish()
+    patch_g.finish()
+    for c in gains:
+        c.wait_send()
+    for c in rows_c:
+        c.wait_recv()
+        c.wait_send()
+    g.sent()
+
+
+def first_call(n_batch, text, patches, gain_tile, patch_tile, w_qkv, w_so, w_co, w_down):
+    n_out = n_batch // 2
+    dma = pltpu.SemaphoreType.DMA
+    j, rows, columns = w_qkv.shape
+    return pl.pallas_call(
+        functools.partial(first_kernel, n_batch),
+        out_shape=[
+            jax.ShapeDtypeStruct((4,) + text.shape, BF),
+            jax.ShapeDtypeStruct((4,) + patches.shape, BF),
+            jax.ShapeDtypeStruct((n_batch,) + gain_tile.shape, BF),
+            jax.ShapeDtypeStruct(patch_tile.shape, BF),
+            jax.ShapeDtypeStruct((j, rows * n_batch, columns), BF),
+        ]
+        + [jax.ShapeDtypeStruct(w.shape[::-1], BF) for w in (w_so, w_co, w_down)],
+        in_specs=[pl.BlockSpec(memory_space=pltpu.VMEM)] * 8,
+        out_specs=[pl.BlockSpec(memory_space=pl.ANY)] * 5 + [pl.BlockSpec(memory_space=pltpu.VMEM)] * 3,
+        scratch_shapes=[
+            pltpu.VMEM((4,) + gain_tile.shape, BF),
+            pltpu.VMEM(gain_tile.shape, BF),
+        ]
+        + BatchGather.semaphores(n_out, 4)
+        + [dma((4, 3)), dma((4, 3)), dma((4,))],
+        compiler_params=pltpu.CompilerParams(collective_id=0, has_side_effects=True),
+        cost_estimate=pl.CostEstimate(flops=10**6, bytes_accessed=300 * 10**6, transcendentals=0),
+    )(text, patches, gain_tile, patch_tile, w_qkv, w_so, w_co, w_down)
+
+
+def mm(a, b):
+    return lax.dot_general(a, b, (((1,), (0,)), ((), ())), preferred_element_type=F32)
+
+
+def mm_nt(a, b):
+    return lax.dot_general(a, b, (((1,), (1,)), ((), ())), preferred_element_type=F32)
+
+
+def mm_tn(a, b):
+    return lax.dot_general(a, b, (((0,), (0,)), ((), ())), preferred_element_type=F32)
+
+
+class Local:
+    def __init__(self, sems):
+        self.sems = sems
+        self.used = 0
+
+    def go(self, src, dst):
+        copy = pltpu.make_async_copy(src, dst, self.sems.at[self.used])
+        self.used += 1
+        copy.start()
+        return copy
+
+
+STEP = 32
+
+
+def each_rows(rows, body, step=STEP):
+    def one(r, carry):
+        body(pl.ds(pl.multiple_of(r * step, step), step))
+        return carry
+
+    lax.fori_loop(0, rows // step, one, 0)
+
+
+def each(count, body, first=0):
+    def one(k, carry):
+        body(k)
+        return carry
+
+    lax.fori_loop(first, count, one, 0)
+
+
+def cols(n, width):
+    return pl.ds(pl.multiple_of(n * width, width), width)
+
+
+def rms_of(values, gain):
+    return values * lax.rsqrt(jnp.mean(values * values, axis=-1, keepdims=True) + 1e-06) * gain
+
+
+def attend(q_ref, k_ref, v_ref, out_ref, lse_ref, j, allowed, heads):
+    for h in range(heads):
+        at = pl.ds(h * HD, HD)
+        s = mm_nt(q_ref[j, :, at], k_ref[j, :, at]) * HD ** (-0.5)
+        s = jnp.where(allowed, s, -1e30)
+        top = jnp.max(s, axis=-1, keepdims=True)
+        e = jnp.exp(s - top)
+        total = jnp.sum(e, axis=-1, keepdims=True)
+        probs = (e / total).astype(BF)
+        out_ref[j, :, at] = mm(probs, v_ref[j, :, at]).astype(BF)
+        lse_ref[j, :, pl.ds(h, 1)] = top + jnp.log(total)
+
+
+def causal_ok(key_row, rows):
+    shape = (rows, key_row.shape[1])
+    return (lax.broadcasted_iota(jnp.int32, shape, 1) <= lax.broadcasted_iota(jnp.int32, shape, 0)) & (
+        jnp.broadcast_to(key_row, shape) > 0.5
+    )
+
+
+class BranchSum:
+    def __init__(self, place, bufs, send, recv):
+        self.p = place
+        self.fs, self.cf, self.ys, self.yr, self.ns, self.cn = bufs
+        self.to_core = remote(self.fs, self.cf, send.at[0], recv.at[0], batch=place.b, mod=place.core)
+        self.to_far = remote(self.ys, self.yr, send.at[1], recv.at[1], batch=place.b, mod=place.far)
+        self.to_near = remote(self.ns, self.cn, send.at[2], recv.at[2], batch=place.b, mod=place.core)
+
+    def send(self, part, width, step=512):
+        p = self.p
+        n = width // step
+
+        def first(k):
+            self.fs[:, cols(k, step)] = part(p.farcore, cols(k, step)).astype(BF)
+
+        def second(k):
+            self.ns[:, cols(k, step)] = part(p.core, cols(k, step)).astype(BF)
+
+        def third(k):
+            at = cols(k, step)
+            self.ys[:, at] = (part(p.far, at) + self.cf[:, at].astype(F32)).astype(BF)
+
+        each(n, first)
+        self.to_core.start()
+        each(n, second)
+        self.to_near.start()
+        self.to_core.wait_recv()
+        each(n, third)
+        self.to_far.start()
+
+    def receive(self):
+        self.to_near.wait_recv()
+        self.to_far.wait_recv()
+
+    def others(self, rows):
+        return self.cn[rows, :].astype(F32) + self.yr[rows, :].astype(F32)
+
+    def sent(self):
+        self.to_core.wait_send()
+        self.to_near.wait_send()
+        self.to_far.wait_send()
+
+
+def halves(shard, whole, rows):
+    half = rows // 2
+
+    def piece(k):
+        return (shard.at[pl.ds(k * half, half)], lambda q: whole.at[pl.ds(q * rows + k * half, half)])
+
+    return [piece(0), piece(1)]
+
+
+def forward_kernel(n_batch, *refs):
+    (text_all, patch_all, gains, patch_own, key_ok, cross_ok, qkv_w,
+     w_so, w_ckv, w_cq, w_co, w_gu, w_down) = refs[:13]
+    (so_all, patch_w, ckv_all, cq_all, co_all, gu_all, down_all, act1_o, act2_o, act3_o, qkv_o, cqkv_o,
+     ctx_o, cctx_o, lse_o, clse_o, pp_o, x1_o, x2_o, gate_o, up_o, h_o) = refs[13:35]
+    (act, x, wq, wo, wp, pat, pp, qkv, ctx, lse, fs, cf, ys, yr, ns, cn, wg, gate, up, hid,
+     z_send, z_recv, x_send, x_recv, own, mod_send, mod_recv, sum_send, sum_recv, loc) = refs[35:]
+    p = Place(n_batch)
+    local = Local(loc)
+    rows, width = x.shape
+    heads = wq.shape[2] // HD
+    cq_r, pr = w_cq.shape[0], patch_own.shape[0]
+    g = BatchGather(
+        p,
+        [
+            (w_so, lambda q: so_all.at[pl.ds(q * cq_r, cq_r)]),
+            (patch_own, lambda q: patch_w.at[pl.ds(q * pr, pr)]),
+            (w_ckv.at[0], lambda q: ckv_all.at[0, pl.ds(q * cq_r, cq_r)]),
+            (w_ckv.at[1], lambda q: ckv_all.at[1, pl.ds(q * cq_r, cq_r)]),
+            (w_cq, lambda q: cq_all.at[pl.ds(q * cq_r, cq_r)]),
+            (w_co, lambda q: co_all.at[pl.ds(q * cq_r, cq_r)]),
+        ]
+        + halves(w_gu.at[0], gu_all.at[0], cq_r)
+        + halves(w_gu.at[1], gu_all.at[1], cq_r)
+        + halves(w_down, down_all, cq_r),
+        (z_send, z_recv, x_send, x_recv, own),
+    )
+    SO, PATCH, CK, CV, CQ, CO, GATE, GATE2, UP, UP2, DOWN, DOWN2 = range(12)
+    load_act = local.go(text_all, act)
+    load_q = local.go(qkv_w, wq)
+    load_pat = local.go(patch_all, pat)
+    p.greet()
+    g.start()
+    bufs = (fs, cf, ys, yr, ns, cn)
+    one = BranchSum(p, bufs, sum_send.at[0], sum_recv.at[0])
+    two = BranchSum(p, bufs, sum_send.at[1], sum_recv.at[1])
+    act_block = lambda j: act.at[j]
+    col_w = wq.shape[2]
+    pp_g = ModGather(p, lambda j: pp.at[:, :, pl.ds(pl.multiple_of(j * col_w, col_w), col_w)], mod_send.at[0], mod_recv.at[0])
+    a2_g = ModGather(p, act_block, mod_send.at[1], mod_recv.at[1])
+    a3_g = ModGather(p, act_block, mod_send.at[2], mod_recv.at[2])
+
+    load_act.wait()
+    x[...] = act[p.m].astype(F32)
+
+    def norm_one(j):
+        def body(r):
+            act[j, r, :] = rms_of(act[j, r, :].astype(F32), gains[pl.ds(0, 1), :]).astype(BF)
+
+        each_rows(rows, body)
+
+    each(4, norm_one)
+    save_act = local.go(act, act1_o)
+    load_q.wait()
+
+    def project(j):
+        for w in range(3):
+            qkv[w, j] = mm(act[j], wq[w]).astype(BF)
+
+    each(4, project)
+    save_qkv = local.go(qkv, qkv_o)
+    g.pump(SO)
+    attend_one = lambda j: attend(qkv.at[0], qkv.at[1], qkv.at[2], ctx, lse, j, causal_ok(key_ok[j, pl.ds(0, 1), :], rows), heads)
+    each(4, attend_one)
+    save_ctx = local.go(ctx, ctx_o)
+    save_lse = local.go(lse, lse_o)
+    g.arrived(SO)
+    load_o = local.go(so_all, wo)
+    save_act.wait()
+    save_qkv.wait()
+    load_o.wait()
+    part = lambda j, at: mm_nt(ctx[j], wo[at, :])
+    one.send(part, width)
+
+    def add_own(k):
+        at = cols(k, 512)
+        x[:, at] += part(p.m, at)
+
+    each(width // 512, add_own)
+    g.arrived(PATCH)
+    load_p = local.go(patch_w, wp)
+    load_p.wait()
+    load_pat.wait()
+    own_cols = pl.ds(pl.multiple_of(p.m * col_w, col_w), col_w)
+
+    def project_patch(j):
+        pp[j, :, own_cols] = mm(pat[j], wp[...]).astype(BF)
+
+    each(4, project_patch)
+    pp_g.start()
+    one.receive()
+
+    def finish_one(r):
+        x[r, :] += one.others(r)
+        act[p.m, r, :] = rms_of(x[r, :], gains[pl.ds(1, 1), :]).astype(BF)
+
+    each_rows(rows, finish_one)
+    a2_g.start()
+    save_x = local.go(x, x1_o)
+    one.sent()
+    g.pump(CV)
+    pp_g.forward()
+    g.pump(CQ)
+    a2_g.forward()
+    g.arrived(CK)
+    load_ck = local.go(ckv_all.at[0], wq.at[1])
+    pp_g.finish()
+    save_pp = local.go(pp, pp_o)
+    load_ck.wait()
+
+    def project_pp(w):
+        def body(j):
+            qkv[w, j] = mm(pp[j], wq[w]).astype(BF)
+
+        return body
+
+    each(4, project_pp(1))
+    g.arrived(CV)
+    load_cv = local.go(ckv_all.at[1], wq.at[2])
+    load_cv.wait()
+    each(4, project_pp(2))
+    g.arrived(CQ)
+    load_cq = local.go(cq_all, wq.at[0])
+    a2_g.finish()
+    save_act = local.go(act, act2_o)
+    load_cq.wait()
+
+    def project_cq(j):
+        qkv[0, j] = mm(act[j], wq[0]).astype(BF)
+
+    each(4, project_cq)
+    save_ctx.wait()
+    save_lse.wait()
+    save_qkv = local.go(qkv, cqkv_o)
+
+    def attend_two(j):
+        ok = jnp.broadcast_to(cross_ok[j, pl.ds(0, 1), :], (rows, cross_ok.shape[2])) > 0.5
+        attend(qkv.at[0], qkv.at[1], qkv.at[2], ctx, lse, j, ok, heads)
+
+    each(4, attend_two)
+    save_ctx = local.go(ctx, cctx_o)
+    save_lse = local.go(lse, clse_o)
+    g.arrived(CO)
+    load_o = local.go(co_all, wo)
+    save_act.wait()
+    save_x.wait()
+    load_o.wait()
+    two.send(part, width)
+    each(width // 512, add_own)
+    g.pump(GATE2)
+    two.receive()
+
+    def finish_two(r):
+        x[r, :] += two.others(r)
+        act[p.m, r, :] = rms_of(x[r, :], gains[pl.ds(2, 1), :]).astype(BF)
+
+    each_rows(rows, finish_two)
+    a3_g.start()
+    save_x = local.go(x, x2_o)
+    two.sent()
+    g.pump(UP)
+    a3_g.forward()
+    a3_g.finish()
+    save_act = local.go(act, act3_o)
+
+    g.arrived(GATE)
+    g.arrived(GATE2)
+    load_g = local.go(gu_all.at[0], wg)
+    load_g.wait()
+
+    def gate_one(j):
+        gate[j] = mm(act[j], wg[...])
+
+    each(4, gate_one)
+    save_gate = local.go(gate, gate_o)
+    g.arrived(UP)
+    g.arrived(UP2)
+    load_g = local.go(gu_all.at[1], wg)
+    load_g.wait()
+
+    def up_one(j):
+        u = mm(act[j], wg[...])
+        up[j] = u.astype(BF)
+        hid[j] = (jax.nn.gelu(gate[j], approximate=True) * u).astype(BF)
+
+    each(4, up_one)
+    save_up = local.go(up, up_o)
+    save_h = local.go(hid, h_o)
+    g.arrived(DOWN)
+    g.arrived(DOWN2)
+    g.sent()
+    for c in (save_act, save_x, save_gate, save_up, save_h, save_ctx, save_lse, save_qkv, save_pp):
+        c.wait()
+
+
+def forward_call(n_batch, text_all, patch_all, gains, patch_own, key_ok, cross_ok, qkv_w,
+                 w_so, w_ckv, w_cq, w_co, w_gu, w_down):
+    n_out = n_batch // 2
+    dma = pltpu.SemaphoreType.DMA
+    items, rows, width = text_all.shape
+    c, f = qkv_w.shape[2], w_gu.shape[2]
+    patch_width = patch_all.shape[2]
+    keys = patch_all.shape[1]
+    sds = jax.ShapeDtypeStruct
+    any_ = pl.BlockSpec(memory_space=pl.ANY)
+    vmem = pl.BlockSpec(memory_space=pltpu.VMEM)
+    big = (items, rows, width)
+    return pl.pallas_call(
+        functools.partial(forward_kernel, n_batch),
+        out_shape=[
+            sds((width, c), BF), sds((patch_width, c), BF), sds((2, width, c), BF), sds((width, c), BF),
+            sds((width, c), BF), sds((2, width, f), BF), sds((width, f), BF),
+            sds(big, BF), sds(big, BF), sds(big, BF),
+            sds((3, items, rows, c), BF), sds((3, items, rows, c), BF),
+            sds((items, rows, c), BF), sds((items, rows, c), BF),
+            sds((items, rows, 128), F32), sds((items, rows, 128), F32),
+            sds((items, keys, width), BF), sds((rows, width), F32), sds((rows, width), F32),
+            sds((items, rows, f), F32), sds((items, rows, f), BF), sds((items, rows, f), BF),
+        ],
+        in_specs=[any_, any_, vmem, vmem, vmem, vmem, any_] + [vmem] * 6,
+        out_specs=[any_] * 22,
+        scratch_shapes=[
+            pltpu.VMEM(big, BF), pltpu.VMEM((rows, width), F32), pltpu.VMEM((3, width, c), BF),
+            pltpu.VMEM((width, c), BF), pltpu.VMEM((patch_width, c), BF), pltpu.VMEM((items, keys, patch_width), BF),
+            pltpu.VMEM((items, keys, width), BF), pltpu.VMEM((3, items, rows, c), BF), pltpu.VMEM((items, rows, c), BF),
+            pltpu.VMEM((items, rows, 128), F32),
+        ]
+        + [pltpu.VMEM((rows, width), BF)] * 6
+        + [pltpu.VMEM((width, f), BF), pltpu.VMEM((items, rows, f), F32), pltpu.VMEM((items, rows, f), BF), pltpu.VMEM((items, rows, f), BF)]
+        + BatchGather.semaphores(n_out, 12)
+        + [dma((3, 3)), dma((3, 3)), dma((2, 3)), dma((2, 3)), dma((32,))],
+        compiler_params=pltpu.CompilerParams(collective_id=1, has_side_effects=True, vmem_limit_bytes=60 * 2**20),
+        cost_estimate=pl.CostEstimate(flops=35 * 10**9, bytes_accessed=600 * 10**6, transcendentals=0),
+    )(text_all, patch_all, gains, patch_own, key_ok, cross_ok, qkv_w, w_so, w_ckv, w_cq, w_co, w_gu, w_down)
 
 
 def scores_of(query, keys, allowed):
@@ -162,55 +742,50 @@
     )
     cross_allowed = (patch_mask > 0)[:, None, :]
 
-    text_all = mod_gather(ex.reorder(text, 2))
-    gain_parts = ex.fetch(gains)
-    qkv_parts = ex.fetch(w_qkv)
-    gain_cols = mod_gather(jnp.stack(gain_parts)[None], 0)
-    gain_all = jnp.transpose(gain_cols, (2, 1, 0, 3)).reshape(3, width).astype(F32)
+    gw = width // (nb * n_mod)
+    gain_tile = lax.dynamic_update_slice(jnp.zeros((16, gw * n_mod), BF), gains, (0, mod * gw))
+    col_w = width // n_mod
+    pr = w_patch.shape[0]
+    pr_pad = -(-pr // 16) * 16
+    patch_tile = jnp.pad(w_patch, ((0, pr_pad - pr), (0, 0))).reshape(pr_pad, n_mod, col_w)
+    patch_tile = jnp.transpose(patch_tile, (1, 0, 2))
+    text_all, patch_all, gain_raw, patch_rows, self_qkv, so_t, co_t, down_t = first_call(
+        n_batch, text[0], patches[0], gain_tile, patch_tile, w_qkv, w_so, w_co, w_down
+    )
+    gain_all = jnp.transpose(gain_raw[:, :3], (1, 0, 2)).reshape(3, width).astype(F32)
+    patch_own = patch_rows[:, :pr].reshape(n_mod * pr, col_w)
+    block, block_pad = n_mod * pr, -(-n_mod * pr // 16) * 16
+    patch_in = patch_all
+    if block_pad != block:
+        patch_own = jnp.pad(patch_own, ((0, block_pad - block), (0, 0)))
+        patch_in = jnp.pad(
+            patch_all.reshape(patch_all.shape[:2] + (nb, block)), ((0, 0), (0, 0), (0, 0), (0, block_pad - block))
+        ).reshape(patch_all.shape[:2] + (nb * block_pad,))
+    row_ok = (positions[None, :] < text_lengths[:, None]).astype(F32)
+    key_ok = jnp.broadcast_to(row_ok[:, None, :], (n_mod, 8, text_rows))
+    cross_ok = jnp.broadcast_to((patch_mask > 0).astype(F32)[:, None, :], (n_mod, 8, patch_mask.shape[1]))
+    gain_pad = jnp.pad(gain_all, ((0, 5), (0, 0)))
+    (self_out, _, cross_kv_w, cross_query_w, cross_out_w, gu_w, down_w, act_one, act_two, act_three, qkv, cqkv,
+     self_ctx, cross_ctx, self_lse, cross_lse, proj_all, x_one, x_two, gate, upward, hidden) = forward_call(
+        n_batch, text_all, patch_in, gain_pad, patch_own, key_ok, cross_ok, self_qkv,
+        so_t, w_ckv, w_cq, co_t, w_gu, down_t)
+    gain_all = ex.reorder(gain_all, 1)
     x_zero = ex.reorder(text, 2).astype(F32)
-    patch_all = mod_gather(patches)
-    col_w = width // n_mod
-    patch_rows = mod_gather(w_patch)
-    patch_own = lax.dynamic_slice_in_dim(patch_rows, mod * col_w, col_w, 1)
-
-    so_parts = ex.fetch(w_so.T, [qkv_parts[-1]])
-    patch_parts = ex.fetch(patch_own, [qkv_parts[-1]])
-    act_one = rms_norm(text_all.astype(F32), gain_all[0]).astype(BF)
-    self_qkv = jnp.concatenate(qkv_parts, axis=1)
-    qkv = dot("gtd,jdc->jgtc", act_one, self_qkv).astype(BF)
-    self_ctx, self_log = attend_forward(qkv[0], qkv[1], qkv[2], causal)
-    self_out = jnp.concatenate(so_parts, axis=0)
-    x_one = x_zero + mod_sum(dot("gtc,dc->gtd", self_ctx, self_out))
+    self_qkv = ex.reorder(self_qkv, 1)
+    self_out = ex.reorder(self_out, 0)
+    cross_kv_w = ex.reorder(cross_kv_w, 1)
+    cross_query_w = ex.reorder(cross_query_w, 0)
+    cross_out_w = ex.reorder(cross_out_w, 0)
+    gate_w, up_w = ex.reorder(gu_w[0], 0), ex.reorder(gu_w[1], 0)
+    down_w = ex.reorder(down_w, 0)
+    act_one, act_two, act_three, proj_all = [ex.reorder(v, 2) for v in (act_one, act_two, act_three, proj_all)]
+    x_one, x_two = ex.reorder(x_one[None], 2), ex.reorder(x_two[None], 2)
+    upward = upward.astype(F32)
+    cross_query, cross_kv = cqkv[0], cqkv[1:]
+    self_log = jnp.transpose(self_lse[:, :, :heads_w // HD], (0, 2, 1))[..., None]
+    cross_log = jnp.transpose(cross_lse[:, :, :heads_w // HD], (0, 2, 1))[..., None]
 
     pr = w_patch.shape[0] * n_mod
-    proj_w = jnp.zeros((pr * nb, col_w), BF)
-    for p in range(nb):
-        proj_w = lax.dynamic_update_slice_in_dim(proj_w, patch_parts[p], ex.source(p) * pr, 0)
-    proj_cols = dot("gpe,ec->gpc", patch_all, proj_w).astype(BF)
-    proj_all = ex.reorder(mod_gather(proj_cols, 2), 2)
-    ckv_parts = ex.fetch(w_ckv, [so_parts[-1], patch_parts[-1]])
-    cq_parts = ex.fetch(w_cq, [so_parts[-1], patch_parts[-1]])
-    co_parts = ex.fetch(w_co.T, [ckv_parts[-1], cq_parts[-1]])
-    gate_parts = ex.fetch(w_gu[0], [ckv_parts[-1], cq_parts[-1]])
-    up_parts = ex.fetch(w_gu[1], [gate_parts[-1]])
-    down_parts = ex.fetch(w_down.T, [up_parts[-1]])
-
-    cross_query_w = jnp.concatenate(cq_parts, axis=0)
-    cross_kv_w = jnp.concatenate(ckv_parts, axis=1)
-    cross_out_w = jnp.concatenate(co_parts, axis=0)
-    cross_kv = dot("gpd,jdc->jgpc", proj_all, cross_kv_w).astype(BF)
-    act_two = mod_gather(rms_norm(x_one, gain_all[1]).astype(BF))
-    cross_query = dot("gtd,dc->gtc", act_two, cross_query_w).astype(BF)
-    cross_ctx, cross_log = attend_forward(cross_query, cross_kv[0], cross_kv[1], cross_allowed)
-    x_two = x_one + mod_sum(dot("gtc,dc->gtd", cross_ctx, cross_out_w))
-
-    act_three = mod_gather(rms_norm(x_two, gain_all[2]).astype(BF))
-    gate_w = jnp.concatenate(gate_parts, axis=0)
-    up_w = jnp.concatenate(up_parts, axis=0)
-    gate = dot("gtd,df->gtf", act_three, gate_w)
-    upward = dot("gtd,df->gtf", act_three, up_w)
-    hidden = gelu_mix(gate, upward).astype(BF)
-
     valid = (positions[None, :] < own_lengths[:, None]).astype(F32)
     grad_result = ex.reorder(cotangent, 2).astype(F32) * valid[..., None]
     grad_branch = mod_gather(grad_result.astype(BF))
@@ -224,7 +799,6 @@
         return ex.reduce(theirs, mine, deps)
 
     grad_down = reduced(grad_branch, hidden)
-    down_w = jnp.concatenate(down_parts, axis=0)
     result = x_two + mod_sum(dot("gtf,df->gtd", hidden, down_w))
     grad_hidden = dot("gtd,df->gtf", grad_branch, down_w)
     _, mix_pull = jax.vjp(gelu_mix, gate, upward)
@@ -283,7 +857,6 @@
     for s in ex.shifts():
         gsum = gsum + ex.along_z(gg[:, s], no - s)
     gsum = jnp.sum(mod_gather(gsum[None], 0), axis=0)
-    gw = width // (nb * n_mod)
     gain_out = lax.dynamic_slice_in_dim(gsum, mod * gw, gw, 1)
     return (
         ex.reorder(result, 2),

time: 1530 us -> 1560 us (1.020)
  Pallas kernels: 0 us -> 445 us
  waiting for transfers between devices: 672 us -> 310 us
  local copies, waits for them, and re-layouts: 255 us -> 385 us
  starting transfers between devices: 266 us -> 159 us
  matrix products: 228 us -> 172 us
    pallas_call x0 -> x2, Pallas kernels: none -> 445 us  [the longest x1 337 us: forward_call(): pl.pallas_call(functools.partial(forward_kernel, n_batch), out_shape=[sds...]
    ppermute x69 -> x39, waiting for transfers between devices: 340 us -> 119 us  [along_z(): return lax.ppermute(value, 'batch', pairs)]
    unnamed x305 -> x327, local copies, waits for them, and re-layouts: 108 us -> 209 us
    ppermute x69 -> x39, starting transfers between devices: 202 us -> 140 us  [along_z(): return lax.ppermute(value, 'batch', pairs)]
    dot_general x52 -> x42, matrix products: 228 us -> 172 us  [dot(): return jnp.einsum(spec, a, b, preferred_element_type=F32)]
    reduce_scatter x6 -> x4, waiting for transfers between devices: 52.5 us -> 0.03 us  [mod_sum(): lax.psum_scatter(partial.astype(BF), 'mod', scatter_dimension=0, tiled=True)]
    ppermute x53 -> x13, waiting for transfers between devices: 239 us -> 189 us  [along_x(): return lax.ppermute(value, 'batch', [(b, b ^ 1) for b in range(self.size)])]
    ppermute x53 -> x13, starting transfers between devices: 58.7 us -> 14.1 us  [along_x(): return lax.ppermute(value, 'batch', [(b, b ^ 1) for b in range(self.size)])]
  transfers between devices with their start and end apart: 138 -> 61, of which waited for: 58 -> 24; matrix products, arithmetic and copies ran while one was open for 28% -> 33% of each run, Pallas kernels for 0% -> 29%
where the time goes in v2:
time: 1560 us; the launch traced here: 1540 us
  Pallas kernels  445 us (29%)
  local copies, waits for them, and re-layouts  385 us (25%)
  waiting for transfers between devices  310 us (20%)
  matrix products  172 us (11%)
  starting transfers between devices  159 us (10%)
  other arithmetic  52 us (3%)
  between operations  16.5 us (1%)
    pallas_call x1, Pallas kernels, forward_call(): pl.pallas_call(functools.partial(forward_kernel, n_batch), out_shape=[sds...  337 us
    unnamed x327, local copies, waits for them, and re-layouts  209 us
    ppermute x13, waiting for transfers between devices, along_x(): return lax.ppermute(value, 'batch', [(b, b ^ 1) for b in range(self.size)])  189 us
    dot_general x42, matrix products, dot(): return jnp.einsum(spec, a, b, preferred_element_type=F32)  172 us
    ppermute x39, starting transfers between devices, along_z(): return lax.ppermute(value, 'batch', pairs)  140 us
    ppermute x39, waiting for transfers between devices, along_z(): return lax.ppermute(value, 'batch', pairs)  119 us
    pallas_call x1, Pallas kernels, first_call(): pl.pallas_call(functools.partial(first_kernel, n_batch), out_shape=[jax.S...  108 us
    slice x7, local copies, waits for them, and re-layouts, own_and_x(): a[:, :, :, 0]  49.3 us
  transfers between devices with their start and end apart: 61, of which 24 were waited for; matrix products, arithmetic and copies ran while one was open for 33% of the time, Pallas kernels for 29%

profile of v2, /device:TPU:0, one launch (start us, length us, event | category | flops | bytes accessed | tf_op | source)
XLA Modules:
  0.0 1544.3 jit_solution(12374161472776028758)
XLA Ops:
  21.1 108.3 %shard_map.221 = (bf16[4,256,2048]{2,1,0:T(8,128)(2,1)}, bf16[4,256,1664]{2,1,0:T(8,128)(2,1)}, bf16[8,16,256]{2,1,0:T(8,128)(2,1)}, bf16[4,64,512]{2,1,0:T(8,12...) custom-call(bf16[256,2048]{1,0:T(8,128)(2,1)} %bitcast.712, ...), custom_call_target="tpu_custom_call" | custom-call | flops 1000000 | bytes 300000000 | tf_op jit(solution)/shard_map/pallas_call | solution.py:293
  134.3 336.6 %shard_map.222 = (bf16[2048,512]{1,0:T(8,128)(2,1)}, bf16[1664,512]{1,0:T(8,128)(2,1)}, bf16[2,2048,512]{2,1,0:T(8,128)(2,1)}, bf16[2048,512]{1,0:T(8,128)(2,1)}...) custom-call(bf16[4,256,2048]{2,1,0:T(8,128)(2,1)} %get-tuple-element, ...), custom_call_target="tpu_custom_call" | custom-call | flops 35000000512 | bytes 600000000 | tf_op jit(solution)/shard_map/pallas_call | solution.py:646
  478.5 8.6 fusion.211
  502.6 13.3 fusion.8
  521.6 9.7 add_convert_fusion
  531.3 10.3 fusion.18
  585.8 7.8 reshape.1782
  593.6 10.1 fusion.218
  603.7 10.5 copy.398
  614.2 10.4 copy.397
  624.6 7.8 reshape.1784
  632.4 10.1 fusion.216
  642.5 10.4 copy.402
  652.9 10.4 copy.401
  691.9 8.3 reshape.1785
  700.2 10.1 fusion.215
  710.3 10.4 copy.404
  720.7 10.4 copy.403
  731.1 7.8 reshape.1789
  738.9 10.1 fusion.213
  749.0 10.4 copy.408
  759.5 10.6 copy.407
  855.2 7.0 bitcast_convert_fusion
  865.8 7.4 bitcast_convert_fusion.4
  888.2 15.9 %collective-permute-done.44 = bf16[4,256,1280]{2,1,0:T(8,128)(2,1)} collective-permute-done((bf16[4,256,1280]{2,1,0:T(8,128)(2,1)}, bf16[4,256,1280]{2,1,0:T(8,128)(2,1)}, u32[]{:S(2)}, u32[]{:S(2)}) %collective-permute-start.44) | collective-permute-done | bytes 2621472 | tf_op jit(solution)/shard_map/ppermute | solution.py:67
  912.9 47.4 %collective-permute-done.40 = bf16[4,256,1280]{2,1,0:T(8,128)(2,1)} collective-permute-done((bf16[4,256,1280]{2,1,0:T(8,128)(2,1)}, bf16[4,256,1280]{2,1,0:T(8,128)(2,1)}, u32[]{:S(2)}, u32[]{:S(2)}) %collective-permute-start.40) | collective-permute-done | bytes 2621472 | tf_op jit(solution)/shard_map/ppermute | solution.py:67
  965.1 50.2 %collective-permute-done.48 = bf16[4,256,1280]{2,1,0:T(8,128)(2,1)S(1)} collective-permute-done((bf16[4,256,1280]{2,1,0:T(8,128)(2,1)S(1)}, bf16[4,256,1280]{2,1,0:T(8,128)(2,1)S(1)}, u32[]{:S(2)}, u32[]{:S(2)}) %collective-permute-start.48) | collective-permute-done | bytes 2621472 | tf_op jit(solution)/shard_map/ppermute | solution.py:67
  1034.9 12.2 collective-permute-done.41
  1052.2 37.0 %collective-permute-done.51 = bf16[256,1280]{1,0:T(8,128)(2,1)} collective-permute-done((bf16[256,1280]{1,0:T(8,128)(2,1)}, bf16[256,1280]{1,0:T(8,128)(2,1)}, u32[]{:S(2)}, u32[]{:S(2)}) %collective-permute-start.51) | collective-permute-done | bytes 655392 | tf_op jit(solution)/shard_map/ppermute | solution.py:64
  1128.7 7.4 collective-permute-done.20
  1141.0 13.5 collective-permute-start.23
  1163.5 13.5 collective-permute-start.31
  1185.7 16.7 %collective-permute-done.32 = bf16[4,256,512]{2,1,0:T(8,128)(2,1)S(1)} collective-permute-done((bf16[4,256,512]{2,1,0:T(8,128)(2,1)S(1)}, bf16[4,256,512]{2,1,0:T(8,128)(2,1)S(1)}, u32[]{:S(2)}, u32[]{:S(2)}) %collective-permute-start.32) | collective-permute-done | bytes 1048608 | tf_op jit(solution)/shard_map/ppermute | solution.py:67
  1234.2 11.1 bitcast_convert_fusion.1
  1249.9 13.6 collective-permute-start.27
  1269.6 12.9 collective-permute-done.27
  1288.5 14.0 collective-permute-start.34
  1308.6 10.7 collective-permute-start.38
  1370.4 9.3 collective-permute-done.12
  1384.5 8.2 collective-permute-start.15
  1394.1 8.0 collective-permute-done.16
  1403.4 8.2 collective-permute-start.19
  1411.6 12.9 collective-permute-done.8
  1433.4 12.2 collective-permute-done.4
  1445.6 9.0 collective-permute-start.17
  1471.3 12.6 collective-permute-done.11
  1485.3 19.7 %collective-permute-done.7 = bf16[256,512]{1,0:T(8,128)(2,1)S(1)} collective-permute-done((bf16[256,512]{1,0:T(8,128)(2,1)}, bf16[256,512]{1,0:T(8,128)(2,1)S(1)}, u32[]{:S(2)}, u32[]{:S(2)}) %collective-permute-start.7) | collective-permute-done | bytes 262176 | tf_op jit(solution)/shard_map/ppermute | solution.py:64
  1517.8 8.1 collective-permute-start.3
  (590 shorter events, 486.6 us)
Async XLA Ops:
  7.2 495.4 %all-gather.6.cloned.1.call-start = ((), (), s32[]{:S(2)}) async-start(), calls=%async_computation.7 | async-start | bytes 5242880 | tf_op jit(solution)/shard_map/all_gather | solution.py:724
  18.7 664.0 %reduce-scatter.8.cloned.1.call-start = ((), (), s32[]{:S(2)}) async-start(), calls=%async_computation.8 | async-start | bytes 5242880 | tf_op jit(solution)/shard_map/reduce_scatter | solution.py:728
  531.3 153.4 %reduce-scatter.6.cloned.1.call-start = ((), (), s32[]{:S(2)}) async-start(), calls=%async_computation.6 | async-start | bytes 5242880 | tf_op jit(solution)/shard_map/reduce_scatter | solution.py:728
  541.7 240.1 %all-gather.8.cloned.1.call-start = ((), (), s32[]{:S(2)}) async-start(), calls=%async_computation.9 | async-start | bytes 5242880 | tf_op jit(solution)/shard_map/all_gather | solution.py:724
  689.5 358.9 %reduce-scatter.10.cloned.1.call-start = ((), (), s32[]{:S(2)}) async-start(), calls=%async_computation.10 | async-start | bytes 5242880 | tf_op jit(solution)/shard_map/reduce_scatter | solution.py:728
  803.7 401.6 %reduce-scatter.14.cloned.1.call-start = ((), (), s32[]{:S(2)}) async-start(), calls=%async_computation.13 | async-start | bytes 5242880 | tf_op jit(solution)/shard_map/reduce_scatter | solution.py:824
  844.0 60.1 %collective-permute-start.44 = (bf16[4,256,1280]{2,1,0:T(8,128)(2,1)}, bf16[4,256,1280]{2,1,0:T(8,128)(2,1)}, u32[]{:S(2)}, u32[]{:S(2)}) collective-permute-start(bf16[4,256,1280]{2,1,0:T(8,128)(2,1)} %bitcast_convert_fusion.3), channel_id=1, source_target_pairs={{0,4},{4,0},{8,12},{12,8},{16,20},{20,16},{24,28},{28,24},{1,5},{5... | collective-permute-start | bytes 7864328 | tf_op jit(solution)/shard_map/ppermute | solution.py:67
  865.5 345.3 %all-gather.10.cloned.1.call-start = ((), (), s32[]{:S(2)}) async-start(), calls=%async_computation.11 | async-start | bytes 5242880 | tf_op jit(solution)/shard_map/all_gather | solution.py:724
  873.2 87.1 %collective-permute-start.40 = (bf16[4,256,1280]{2,1,0:T(8,128)(2,1)}, bf16[4,256,1280]{2,1,0:T(8,128)(2,1)}, u32[]{:S(2)}, u32[]{:S(2)}) collective-permute-start(bf16[4,256,1280]{2,1,0:T(8,128)(2,1)} %bitcast_convert_fusion.4), channel_id=1, source_target_pairs={{0,4},{4,0},{8,12},{12,8},{16,20},{20,16},{24,28},{28,24},{1,5},{5... | collective-permute-start | bytes 7864328 | tf_op jit(solution)/shard_map/ppermute | solution.py:67
  886.2 129.1 %collective-permute-start.48 = (bf16[4,256,1280]{2,1,0:T(8,128)(2,1)S(1)}, bf16[4,256,1280]{2,1,0:T(8,128)(2,1)S(1)}, u32[]{:S(2)}, u32[]{:S(2)}) collective-permute-start(bf16[4,256,1280]{2,1,0:T(8,128)(2,1)S(1)} %bitcast_convert_fusion.2), channel_id=1, source_target_pairs={{0,4},{4,0},{8,12},{12,8},{16,20},{20,16},{24,28},{28,24},{1,5},{5... | collective-permute-start | bytes 7864328 | tf_op jit(solution)/shard_map/ppermute | solution.py:67
  908.9 110.9 %collective-permute-start.47 = (bf16[256,1280]{1,0:T(8,128)(2,1)S(1)}, bf16[256,1280]{1,0:T(8,128)(2,1)S(1)}, u32[]{:S(2)}, u32[]{:S(2)}) collective-permute-start(bf16[256,1280]{1,0:T(8,128)(2,1)S(1)} %get-tuple-element.185), channel_id=1, source_target_pairs={{0,16},{4,20},{8,24},{12,28},{16,0},{20,4},{24,8},{28,12},{1,17},{... | collective-permute-start | bytes 1966088 | tf_op jit(solution)/shard_map/ppermute | solution.py:64
  909.0 116.0 %collective-permute-start.46 = (bf16[256,1280]{1,0:T(8,128)(2,1)S(1)}, bf16[256,1280]{1,0:T(8,128)(2,1)S(1)}, u32[]{:S(2)}, u32[]{:S(2)}) collective-permute-start(bf16[256,1280]{1,0:T(8,128)(2,1)S(1)} %get-tuple-element.186), channel_id=1, source_target_pairs={{0,8},{4,12},{8,16},{12,20},{16,24},{20,28},{24,0},{28,4},{1,9},{5... | collective-permute-start | bytes 1966088 | tf_op jit(solution)/shard_map/ppermute | solution.py:64
  909.6 115.5 %collective-permute-start.45 = (bf16[256,1280]{1,0:T(8,128)(2,1)S(1)}, bf16[256,1280]{1,0:T(8,128)(2,1)S(1)}, u32[]{:S(2)}, u32[]{:S(2)}) collective-permute-start(bf16[256,1280]{1,0:T(8,128)(2,1)S(1)} %get-tuple-element.184), channel_id=1, source_target_pairs={{0,24},{4,28},{8,0},{12,4},{16,8},{20,12},{24,16},{28,20},{1,25},{... | collective-permute-start | bytes 1966088 | tf_op jit(solution)/shard_map/ppermute | solution.py:64
  965.1 60.8 %collective-permute-start.43 = (bf16[256,1280]{1,0:T(8,128)(2,1)S(1)}, bf16[256,1280]{1,0:T(8,128)(2,1)S(1)}, u32[]{:S(2)}, u32[]{:S(2)}) collective-permute-start(bf16[256,1280]{1,0:T(8,128)(2,1)S(1)} %get-tuple-element.182), channel_id=1, source_target_pairs={{0,16},{4,20},{8,24},{12,28},{16,0},{20,4},{24,8},{28,12},{1,17},{... | collective-permute-start | bytes 1966088 | tf_op jit(solution)/shard_map/ppermute | solution.py:64
  1015.3 19.6 %collective-permute-start.42 = (bf16[256,1280]{1,0:T(8,128)(2,1)S(1)}, bf16[256,1280]{1,0:T(8,128)(2,1)S(1)}, u32[]{:S(2)}, u32[]{:S(2)}) collective-permute-start(bf16[256,1280]{1,0:T(8,128)(2,1)S(1)} %get-tuple-element.183), channel_id=1, source_target_pairs={{0,8},{4,12},{8,16},{12,20},{16,24},{20,28},{24,0},{28,4},{1,9},{5... | collective-permute-start | bytes 1966088 | tf_op jit(solution)/shard_map/ppermute | solution.py:64
  1019.8 27.2 %collective-permute-start.41 = (bf16[256,1280]{1,0:T(8,128)(2,1)S(1)}, bf16[256,1280]{1,0:T(8,128)(2,1)S(1)}, u32[]{:S(2)}, u32[]{:S(2)}) collective-permute-start(bf16[256,1280]{1,0:T(8,128)(2,1)S(1)} %get-tuple-element.181), channel_id=1, source_target_pairs={{0,24},{4,28},{8,0},{12,4},{16,8},{20,12},{24,16},{28,20},{1,25},{... | collective-permute-start | bytes 1966088 | tf_op jit(solution)/shard_map/ppermute | solution.py:64
  1025.0 64.2 %collective-permute-start.51 = (bf16[256,1280]{1,0:T(8,128)(2,1)}, bf16[256,1280]{1,0:T(8,128)(2,1)}, u32[]{:S(2)}, u32[]{:S(2)}) collective-permute-start(bf16[256,1280]{1,0:T(8,128)(2,1)} %get-tuple-element.179), channel_id=1, source_target_pairs={{0,16},{4,20},{8,24},{12,28},{16,0},{20,4},{24,8},{28,12},{1,17},{... | collective-permute-start | bytes 1966088 | tf_op jit(solution)/shard_map/ppermute | solution.py:64
  1025.0 64.2 %collective-permute-start.50 = (bf16[256,1280]{1,0:T(8,128)(2,1)}, bf16[256,1280]{1,0:T(8,128)(2,1)}, u32[]{:S(2)}, u32[]{:S(2)}) collective-permute-start(bf16[256,1280]{1,0:T(8,128)(2,1)} %get-tuple-element.180), channel_id=1, source_target_pairs={{0,8},{4,12},{8,16},{12,20},{16,24},{20,28},{24,0},{28,4},{1,9},{5... | collective-permute-start | bytes 1966088 | tf_op jit(solution)/shard_map/ppermute | solution.py:64
  1025.9 63.4 %collective-permute-start.49 = (bf16[256,1280]{1,0:T(8,128)(2,1)}, bf16[256,1280]{1,0:T(8,128)(2,1)}, u32[]{:S(2)}, u32[]{:S(2)}) collective-permute-start(bf16[256,1280]{1,0:T(8,128)(2,1)} %get-tuple-element.178), channel_id=1, source_target_pairs={{0,24},{4,28},{8,0},{12,4},{16,8},{20,12},{24,16},{28,20},{1,25},{... | collective-permute-start | bytes 1966088 | tf_op jit(solution)/shard_map/ppermute | solution.py:64
  1052.2 455.3 %reduce-scatter.12.cloned.1.call-start = ((), (), s32[]{:S(2)}) async-start(), calls=%async_computation.12 | async-start | bytes 5242880 | tf_op jit(solution)/shard_map/reduce_scatter | solution.py:728
  1109.8 26.4 %collective-permute-start.20 = (bf16[4,256,512]{2,1,0:T(8,128)(2,1)}, bf16[4,256,512]{2,1,0:T(8,128)(2,1)}, u32[]{:S(2)}, u32[]{:S(2)}) collective-permute-start(bf16[4,256,512]{2,1,0:T(8,128)(2,1)} %bitcast_convert_fusion.9), channel_id=1, source_target_pairs={{0,4},{4,0},{8,12},{12,8},{16,20},{20,16},{24,28},{28,24},{1,5},{5... | collective-permute-start | bytes 3145736 | tf_op jit(solution)/shard_map/ppermute | solution.py:67
  1113.2 45.5 %collective-permute-start.28 = (bf16[4,256,512]{2,1,0:T(8,128)(2,1)}, bf16[4,256,512]{2,1,0:T(8,128)(2,1)}, u32[]{:S(2)}, u32[]{:S(2)}) collective-permute-start(bf16[4,256,512]{2,1,0:T(8,128)(2,1)} %bitcast_convert_fusion.7), channel_id=1, source_target_pairs={{0,4},{4,0},{8,12},{12,8},{16,20},{20,16},{24,28},{28,24},{1,5},{5... | collective-permute-start | bytes 3145736 | tf_op jit(solution)/shard_map/ppermute | solution.py:67
  1116.4 64.7 %collective-permute-start.24 = (bf16[4,256,512]{2,1,0:T(8,128)(2,1)}, bf16[4,256,512]{2,1,0:T(8,128)(2,1)}, u32[]{:S(2)}, u32[]{:S(2)}) collective-permute-start(bf16[4,256,512]{2,1,0:T(8,128)(2,1)} %bitcast_convert_fusion.8), channel_id=1, source_target_pairs={{0,4},{4,0},{8,12},{12,8},{16,20},{20,16},{24,28},{28,24},{1,5},{5... | collective-permute-start | bytes 3145736 | tf_op jit(solution)/shard_map/ppermute | solution.py:67
  1127.8 74.7 %collective-permute-start.32 = (bf16[4,256,512]{2,1,0:T(8,128)(2,1)S(1)}, bf16[4,256,512]{2,1,0:T(8,128)(2,1)S(1)}, u32[]{:S(2)}, u32[]{:S(2)}) collective-permute-start(bf16[4,256,512]{2,1,0:T(8,128)(2,1)S(1)} %bitcast_convert_fusion.6), channel_id=1, source_target_pairs={{0,4},{4,0},{8,12},{12,8},{16,20},{20,16},{24,28},{28,24},{1,5},{5... | collective-permute-start | bytes 3145736 | tf_op jit(solution)/shard_map/ppermute | solution.py:67
  1141.0 202.5 %collective-permute-start.23 = (bf16[256,512]{1,0:T(8,128)(2,1)}, bf16[256,512]{1,0:T(8,128)(2,1)}, u32[]{:S(2)}, u32[]{:S(2)}) collective-permute-start(bf16[256,512]{1,0:T(8,128)(2,1)} %get-tuple-element.208), channel_id=1, source_target_pairs={{0,16},{4,20},{8,24},{12,28},{16,0},{20,4},{24,8},{28,12},{1,17},{... | collective-permute-start | bytes 786440 | tf_op jit(solution)/shard_map/ppermute | solution.py:64
  1163.5 86.4 %collective-permute-start.31 = (bf16[256,512]{1,0:T(8,128)(2,1)}, bf16[256,512]{1,0:T(8,128)(2,1)}, u32[]{:S(2)}, u32[]{:S(2)}) collective-permute-start(bf16[256,512]{1,0:T(8,128)(2,1)} %get-tuple-element.205), channel_id=1, source_target_pairs={{0,16},{4,20},{8,24},{12,28},{16,0},{20,4},{24,8},{28,12},{1,17},{... | collective-permute-start | bytes 786440 | tf_op jit(solution)/shard_map/ppermute | solution.py:64
  1176.9 86.6 %collective-permute-start.30 = (bf16[256,512]{1,0:T(8,128)(2,1)}, bf16[256,512]{1,0:T(8,128)(2,1)}, u32[]{:S(2)}, u32[]{:S(2)}) collective-permute-start(bf16[256,512]{1,0:T(8,128)(2,1)} %get-tuple-element.206), channel_id=1, source_target_pairs={{0,8},{4,12},{8,16},{12,20},{16,24},{20,28},{24,0},{28,4},{1,9},{5... | collective-permute-start | bytes 786440 | tf_op jit(solution)/shard_map/ppermute | solution.py:64
  1181.1 83.6 %collective-permute-start.29 = (bf16[256,512]{1,0:T(8,128)(2,1)}, bf16[256,512]{1,0:T(8,128)(2,1)}, u32[]{:S(2)}, u32[]{:S(2)}) collective-permute-start(bf16[256,512]{1,0:T(8,128)(2,1)} %get-tuple-element.204), channel_id=1, source_target_pairs={{0,24},{4,28},{8,0},{12,4},{16,8},{20,12},{24,16},{28,20},{1,25},{... | collective-permute-start | bytes 786440 | tf_op jit(solution)/shard_map/ppermute | solution.py:64
  1247.5 57.1 %collective-permute-start.36 = (bf16[4,208,512]{2,1,0:T(8,128)(2,1)S(1)}, bf16[4,208,512]{2,1,0:T(8,128)(2,1)S(1)}, u32[]{:S(2)}, u32[]{:S(2)}) collective-permute-start(bf16[4,208,512]{2,1,0:T(8,128)(2,1)S(1)} %pad_maximum_fusion.4), channel_id=1, source_target_pairs={{0,4},{4,0},{8,12},{12,8},{16,20},{20,16},{24,28},{28,24},{1,5},{5... | collective-permute-start | bytes 2555912 | tf_op jit(solution)/shard_map/ppermute | solution.py:67
  1249.9 32.6 %collective-permute-start.27 = (bf16[256,512]{1,0:T(8,128)(2,1)S(1)}, bf16[256,512]{1,0:T(8,128)(2,1)S(1)}, u32[]{:S(2)}, u32[]{:S(2)}) collective-permute-start(bf16[256,512]{1,0:T(8,128)(2,1)S(1)} %get-tuple-element.202), channel_id=1, source_target_pairs={{0,16},{4,20},{8,24},{12,28},{16,0},{20,4},{24,8},{28,12},{1,17},{... | collective-permute-start | bytes 786440 | tf_op jit(solution)/shard_map/ppermute | solution.py:64
  1264.7 23.8 %collective-permute-start.25 = (bf16[256,512]{1,0:T(8,128)(2,1)S(1)}, bf16[256,512]{1,0:T(8,128)(2,1)S(1)}, u32[]{:S(2)}, u32[]{:S(2)}) collective-permute-start(bf16[256,512]{1,0:T(8,128)(2,1)S(1)} %get-tuple-element.201), channel_id=1, source_target_pairs={{0,24},{4,28},{8,0},{12,4},{16,8},{20,12},{24,16},{28,20},{1,25},{... | collective-permute-start | bytes 786440 | tf_op jit(solution)/shard_map/ppermute | solution.py:64
  1282.5 61.0 %collective-permute-start.22 = (bf16[256,512]{1,0:T(8,128)(2,1)}, bf16[256,512]{1,0:T(8,128)(2,1)S(1)}, u32[]{:S(2)}, u32[]{:S(2)}) collective-permute-start(bf16[256,512]{1,0:T(8,128)(2,1)} %get-tuple-element.209), channel_id=1, source_target_pairs={{0,8},{4,12},{8,16},{12,20},{16,24},{20,28},{24,0},{28,4},{1,9},{5... | collective-permute-start | bytes 786440 | tf_op jit(solution)/shard_map/ppermute | solution.py:64
  1282.5 26.1 %collective-permute-start.35 = (bf16[256,512]{1,0:T(8,128)(2,1)S(1)}, bf16[256,512]{1,0:T(8,128)(2,1)S(1)}, u32[]{:S(2)}, u32[]{:S(2)}) collective-permute-start(bf16[256,512]{1,0:T(8,128)(2,1)S(1)} %get-tuple-element.199), channel_id=1, source_target_pairs={{0,16},{4,20},{8,24},{12,28},{16,0},{20,4},{24,8},{28,12},{1,17},{... | collective-permute-start | bytes 786440 | tf_op jit(solution)/shard_map/ppermute | solution.py:64
  1288.5 20.0 %collective-permute-start.34 = (bf16[256,512]{1,0:T(8,128)(2,1)S(1)}, bf16[256,512]{1,0:T(8,128)(2,1)S(1)}, u32[]{:S(2)}, u32[]{:S(2)}) collective-permute-start(bf16[256,512]{1,0:T(8,128)(2,1)S(1)} %get-tuple-element.200), channel_id=1, source_target_pairs={{0,8},{4,12},{8,16},{12,20},{16,24},{20,28},{24,0},{28,4},{1,9},{5... | collective-permute-start | bytes 786440 | tf_op jit(solution)/shard_map/ppermute | solution.py:64
  1353.3 26.4 %collective-permute-start.12 = (bf16[4,256,512]{2,1,0:T(8,128)(2,1)}, bf16[4,256,512]{2,1,0:T(8,128)(2,1)}, u32[]{:S(2)}, u32[]{:S(2)}) collective-permute-start(bf16[4,256,512]{2,1,0:T(8,128)(2,1)} %bitcast_convert_fusion.11), channel_id=1, source_target_pairs={{0,4},{4,0},{8,12},{12,8},{16,20},{20,16},{24,28},{28,24},{1,5},{5... | collective-permute-start | bytes 3145736 | tf_op jit(solution)/shard_map/ppermute | solution.py:67
  1364.5 37.6 %collective-permute-start.16 = (bf16[4,256,512]{2,1,0:T(8,128)(2,1)S(1)}, bf16[4,256,512]{2,1,0:T(8,128)(2,1)S(1)}, u32[]{:S(2)}, u32[]{:S(2)}) collective-permute-start(bf16[4,256,512]{2,1,0:T(8,128)(2,1)S(1)} %bitcast_convert_fusion.10), channel_id=1, source_target_pairs={{0,4},{4,0},{8,12},{12,8},{16,20},{20,16},{24,28},{28,24},{1,5},{5... | collective-permute-start | bytes 3145736 | tf_op jit(solution)/shard_map/ppermute | solution.py:67
  1366.9 57.6 %collective-permute-start.8 = (bf16[4,256,512]{2,1,0:T(8,128)(2,1)S(1)}, bf16[4,256,512]{2,1,0:T(8,128)(2,1)S(1)}, u32[]{:S(2)}, u32[]{:S(2)}) collective-permute-start(bf16[4,256,512]{2,1,0:T(8,128)(2,1)S(1)} %bitcast_convert_fusion.12), channel_id=1, source_target_pairs={{0,4},{4,0},{8,12},{12,8},{16,20},{20,16},{24,28},{28,24},{1,5},{5... | collective-permute-start | bytes 3145736 | tf_op jit(solution)/shard_map/ppermute | solution.py:67
  1369.2 76.4 %collective-permute-start.4 = (bf16[4,256,512]{2,1,0:T(8,128)(2,1)S(1)}, bf16[4,256,512]{2,1,0:T(8,128)(2,1)S(1)}, u32[]{:S(2)}, u32[]{:S(2)}) collective-permute-start(bf16[4,256,512]{2,1,0:T(8,128)(2,1)S(1)} %bitcast_convert_fusion.13), channel_id=1, source_target_pairs={{0,4},{4,0},{8,12},{12,8},{16,20},{20,16},{24,28},{28,24},{1,5},{5... | collective-permute-start | bytes 3145736 | tf_op jit(solution)/shard_map/ppermute | solution.py:67
  1384.5 77.8 %collective-permute-start.15 = (bf16[256,512]{1,0:T(8,128)(2,1)}, bf16[256,512]{1,0:T(8,128)(2,1)S(1)}, u32[]{:S(2)}, u32[]{:S(2)}) collective-permute-start(bf16[256,512]{1,0:T(8,128)(2,1)} %get-tuple-element.220), channel_id=1, source_target_pairs={{0,16},{4,20},{8,24},{12,28},{16,0},{20,4},{24,8},{28,12},{1,17},{... | collective-permute-start | bytes 786440 | tf_op jit(solution)/shard_map/ppermute | solution.py:64
  1392.7 72.5 %collective-permute-start.14 = (bf16[256,512]{1,0:T(8,128)(2,1)}, bf16[256,512]{1,0:T(8,128)(2,1)}, u32[]{:S(2)}, u32[]{:S(2)}) collective-permute-start(bf16[256,512]{1,0:T(8,128)(2,1)} %get-tuple-element.221), channel_id=1, source_target_pairs={{0,8},{4,12},{8,16},{12,20},{16,24},{20,28},{24,0},{28,4},{1,9},{5... | collective-permute-start | bytes 786440 | tf_op jit(solution)/shard_map/ppermute | solution.py:64
  1403.4 55.7 %collective-permute-start.19 = (bf16[256,512]{1,0:T(8,128)(2,1)S(1)}, bf16[256,512]{1,0:T(8,128)(2,1)S(1)}, u32[]{:S(2)}, u32[]{:S(2)}) collective-permute-start(bf16[256,512]{1,0:T(8,128)(2,1)S(1)} %get-tuple-element.211), channel_id=1, source_target_pairs={{0,16},{4,20},{8,24},{12,28},{16,0},{20,4},{24,8},{28,12},{1,17},{... | collective-permute-start | bytes 786440 | tf_op jit(solution)/shard_map/ppermute | solution.py:64
  1424.5 35.2 %collective-permute-start.18 = (bf16[256,512]{1,0:T(8,128)(2,1)S(1)}, bf16[256,512]{1,0:T(8,128)(2,1)S(1)}, u32[]{:S(2)}, u32[]{:S(2)}) collective-permute-start(bf16[256,512]{1,0:T(8,128)(2,1)S(1)} %get-tuple-element.212), channel_id=1, source_target_pairs={{0,8},{4,12},{8,16},{12,20},{16,24},{20,28},{24,0},{28,4},{1,9},{5... | collective-permute-start | bytes 786440 | tf_op jit(solution)/shard_map/ppermute | solution.py:64
  1459.7 24.2 %collective-permute-start.11 = (bf16[256,512]{1,0:T(8,128)(2,1)}, bf16[256,512]{1,0:T(8,128)(2,1)S(1)}, u32[]{:S(2)}, u32[]{:S(2)}) collective-permute-start(bf16[256,512]{1,0:T(8,128)(2,1)} %get-tuple-element.217), channel_id=1, source_target_pairs={{0,16},{4,20},{8,24},{12,28},{16,0},{20,4},{24,8},{28,12},{1,17},{... | collective-permute-start | bytes 786440 | tf_op jit(solution)/shard_map/ppermute | solution.py:64
  1459.7 24.4 %collective-permute-start.10 = (bf16[256,512]{1,0:T(8,128)(2,1)}, bf16[256,512]{1,0:T(8,128)(2,1)S(1)}, u32[]{:S(2)}, u32[]{:S(2)}) collective-permute-start(bf16[256,512]{1,0:T(8,128)(2,1)} %get-tuple-element.218), channel_id=1, source_target_pairs={{0,8},{4,12},{8,16},{12,20},{16,24},{20,28},{24,0},{28,4},{1,9},{5... | collective-permute-start | bytes 786440 | tf_op jit(solution)/shard_map/ppermute | solution.py:64
  1462.3 21.8 %collective-permute-start.9 = (bf16[256,512]{1,0:T(8,128)(2,1)}, bf16[256,512]{1,0:T(8,128)(2,1)S(1)}, u32[]{:S(2)}, u32[]{:S(2)}) collective-permute-start(bf16[256,512]{1,0:T(8,128)(2,1)} %get-tuple-element.216), channel_id=1, source_target_pairs={{0,24},{4,28},{8,0},{12,4},{16,8},{20,12},{24,16},{28,20},{1,25},{... | collective-permute-start | bytes 786440 | tf_op jit(solution)/shard_map/ppermute | solution.py:64
  1465.2 39.9 %collective-permute-start.7 = (bf16[256,512]{1,0:T(8,128)(2,1)}, bf16[256,512]{1,0:T(8,128)(2,1)S(1)}, u32[]{:S(2)}, u32[]{:S(2)}) collective-permute-start(bf16[256,512]{1,0:T(8,128)(2,1)} %get-tuple-element.214), channel_id=1, source_target_pairs={{0,16},{4,20},{8,24},{12,28},{16,0},{20,4},{24,8},{28,12},{1,17},{... | collective-permute-start | bytes 786440 | tf_op jit(solution)/shard_map/ppermute | solution.py:64
  1470.0 35.1 %collective-permute-start.6 = (bf16[256,512]{1,0:T(8,128)(2,1)}, bf16[256,512]{1,0:T(8,128)(2,1)S(1)}, u32[]{:S(2)}, u32[]{:S(2)}) collective-permute-start(bf16[256,512]{1,0:T(8,128)(2,1)} %get-tuple-element.215), channel_id=1, source_target_pairs={{0,8},{4,12},{8,16},{12,20},{16,24},{20,28},{24,0},{28,4},{1,9},{5... | collective-permute-start | bytes 786440 | tf_op jit(solution)/shard_map/ppermute | solution.py:64
  1483.9 21.2 %collective-permute-start.5 = (bf16[256,512]{1,0:T(8,128)(2,1)}, bf16[256,512]{1,0:T(8,128)(2,1)S(1)}, u32[]{:S(2)}, u32[]{:S(2)}) collective-permute-start(bf16[256,512]{1,0:T(8,128)(2,1)} %get-tuple-element.213), channel_id=1, source_target_pairs={{0,24},{4,28},{8,0},{12,4},{16,8},{20,12},{24,16},{28,20},{1,25},{... | collective-permute-start | bytes 786440 | tf_op jit(solution)/shard_map/ppermute | solution.py:64
  (102 other events, 1160.1 us)
Sparse Core Ops, SparseCore 0:
  18.8 60.2 all-gather.5
  531.4 42.4 reduce-scatter.7
  576.6 44.5 reduce-scatter.5
  689.6 32.0 all-gather.7
  803.9 42.0 reduce-scatter.9
  865.6 40.7 reduce-scatter.13
  1052.3 43.1 all-gather.9
  1245.4 55.3 reduce-scatter.11

commit v3 on v2

v3 whole, which is shorter than its diff:
```python
import functools

import jax
import jax.numpy as jnp
from jax import lax
from jax.experimental import pallas as pl
from jax.experimental.pallas import tpu as pltpu
from jax.sharding import PartitionSpec as P

HD = 128
F32 = jnp.float32
BF = jnp.bfloat16


VMEM_LIMIT = 62 * 2**20
MESH = pl.DeviceIdType.MESH


class Place:
    def __init__(self, n_batch):
        self.n_batch = n_batch
        self.n_out = n_batch // 2
        self.b = lax.axis_index("batch")
        self.m = lax.axis_index("mod")
        self.outer = self.b // 2
        self.inner = self.b % 2
        self.core = self.m + 1 - 2 * (self.m % 2)
        self.far = (self.m + 2) % 4
        self.farcore = (self.core + 2) % 4
        self.x_peer = self.b + 1 - 2 * self.inner
        self.shifts = []
        for d in range(1, self.n_out // 2 + 1):
            self.shifts += [d] if 2 * d == self.n_out else [d, self.n_out - d]

    def z_peer(self, s):
        return (self.outer + s) % self.n_out * 2 + self.inner

    def z_from(self, s):
        return (self.outer - s + self.n_out) % self.n_out * 2 + self.inner

    def greet(self):
        barrier = pltpu.get_barrier_semaphore()
        ids = [{"batch": self.z_peer(s), "mod": self.m} for s in self.shifts]
        ids.append({"batch": self.x_peer, "mod": self.m})
        for j in (self.core, self.far, self.farcore):
            ids.append({"batch": self.b, "mod": j})
        for device in ids:
            pl.semaphore_signal(barrier, inc=1, device_id=device, device_id_type=MESH)
        pl.semaphore_wait(barrier, len(ids))


def remote(src, dst, send, recv, **device):
    return pltpu.make_async_remote_copy(
        src_ref=src, dst_ref=dst, send_sem=send, recv_sem=recv, device_id=device, device_id_type=MESH
    )


class BatchGather:
    def __init__(self, place, tensors, sems):
        self.p = place
        self.tensors = tensors
        self.z_send, self.z_recv, self.x_send, self.x_recv, self.own = sems
        self.started = 0
        self.events = [(t, s) for t in range(len(tensors)) for s in [0] + place.shifts]
        self.at = 0

    @staticmethod
    def semaphores(n_out, count):
        dma = pltpu.SemaphoreType.DMA
        return [dma((count, n_out)) for _ in range(4)] + [dma((count,))]

    def z_copy(self, t, s):
        src, block = self.tensors[t]
        return remote(src, block(self.p.b), self.z_send.at[t, s], self.z_recv.at[t, s],
                      batch=self.p.z_peer(s), mod=self.p.m)

    def own_copy(self, t):
        src, block = self.tensors[t]
        return pltpu.make_async_copy(src, block(self.p.b), self.own.at[t])

    def x_copy(self, t, s):
        src, block = self.tensors[t]
        where = block(self.p.z_from(s))
        return remote(src if s == 0 else where, where, self.x_send.at[t, s], self.x_recv.at[t, s],
                      batch=self.p.x_peer, mod=self.p.m)

    def start(self, count=1):
        for t in range(self.started, min(self.started + count, len(self.tensors))):
            for s in self.p.shifts:
                self.z_copy(t, s).start()
            self.own_copy(t).start()
            self.started = t + 1

    def pump(self, upto):
        while self.at < len(self.events) and self.events[self.at][0] <= upto:
            t, s = self.events[self.at]
            if s:
                self.z_copy(t, s).wait_recv()
                if s == self.p.shifts[-1]:
                    self.start()
            self.x_copy(t, s).start()
            self.at += 1

    def arrived(self, t, ahead=1):
        self.pump(t + ahead)
        self.own_copy(t).wait()
        for s in [0] + self.p.shifts:
            self.x_copy(t, s).wait_recv()

    def sent(self):
        for t in range(len(self.tensors)):
            for s in self.p.shifts:
                self.z_copy(t, s).wait_send()
            for s in [0] + self.p.shifts:
                self.x_copy(t, s).wait_send()


class ModGather:
    def __init__(self, place, block, send, recv):
        self.p = place
        self.block = block
        mine = block(place.m)
        far = block(place.far)
        self.near = remote(mine, mine, send.at[0], recv.at[0], batch=place.b, mod=place.core)
        self.across = remote(mine, mine, send.at[1], recv.at[1], batch=place.b, mod=place.far)
        self.on = remote(far, far, send.at[2], recv.at[2], batch=place.b, mod=place.core)

    def start(self):
        self.across.start()
        self.near.start()

    def forward(self):
        self.across.wait_recv()
        self.on.start()

    def finish(self):
        self.near.wait_recv()
        self.on.wait_recv()
        self.near.wait_send()
        self.across.wait_send()
        self.on.wait_send()


def first_kernel(n_batch, text, patches, gain_tile, patch_tile, w_qkv, w_so, w_co, w_down, cot, valid,
                 text_all, patch_all, gain_all, patch_rows, qkv_all, dy_all, so_t, co_t, down_t,
                 dy, gain_mod, gain_sum, z_send, z_recv, x_send, x_recv, own, mod_send, mod_recv, misc):
    p = Place(n_batch)
    rows = w_qkv.shape[1]
    tensors = [
        (w_qkv.at[0], lambda q: qkv_all.at[0, pl.ds(q * rows, rows)]),
        (w_qkv.at[1], lambda q: qkv_all.at[1, pl.ds(q * rows, rows)]),
        (gain_sum, lambda q: gain_all.at[q]),
        (w_qkv.at[2], lambda q: qkv_all.at[2, pl.ds(q * rows, rows)]),
    ]
    g = BatchGather(p, tensors, (z_send, z_recv, x_send, x_recv, own))
    copies = [
        pltpu.make_async_copy(text, text_all.at[p.m], misc.at[0]),
        pltpu.make_async_copy(patches, patch_all.at[p.m], misc.at[1]),
        pltpu.make_async_copy(gain_tile, gain_mod.at[p.m], misc.at[2]),
        pltpu.make_async_copy(patch_tile.at[p.m], patch_rows.at[p.m], misc.at[3]),
        pltpu.make_async_copy(dy, dy_all.at[p.m], misc.at[4]),
    ]

    def mask_rows(r):
        dy[r, :] = (cot[r, :].astype(F32) * valid[r, pl.ds(0, 1)]).astype(BF)

    each_rows(dy.shape[0], mask_rows)
    for c in copies:
        c.start()
    p.greet()
    gains = [
        remote(gain_tile, gain_mod.at[p.m], mod_send.at[2, k], mod_recv.at[2, k], batch=p.b, mod=j)
        for k, j in enumerate((p.core, p.far, p.farcore))
    ]
    for c in gains:
        c.start()
    g.start()
    for c in copies:
        c.wait()
    text_g = ModGather(p, lambda j: text_all.at[j], mod_send.at[0], mod_recv.at[0])
    patch_g = ModGather(p, lambda j: patch_all.at[j], mod_send.at[1], mod_recv.at[1])
    dy_g = ModGather(p, lambda j: dy_all.at[j], mod_send.at[4], mod_recv.at[4])
    text_g.start()
    rows_c = [
        remote(patch_tile.at[j], patch_rows.at[p.m], mod_send.at[3, k], mod_recv.at[3, k], batch=p.b, mod=j)
        for k, j in enumerate((p.core, p.far, p.farcore))
    ]
    for c in rows_c:
        c.start()
    patch_g.start()
    for c in gains:
        c.wait_recv()
    gain_sum[...] = gain_mod[0] + gain_mod[1] + gain_mod[2] + gain_mod[3]
    so_t[...] = w_so[...].T
    co_t[...] = w_co[...].T
    down_t[...] = w_down[...].T
    g.pump(0)
    text_g.forward()
    dy_g.start()
    g.pump(1)
    patch_g.forward()
    g.pump(3)
    dy_g.forward()
    for t in range(4):
        g.arrived(t)
    text_g.finish()
    patch_g.finish()
    dy_g.finish()
    for c in gains:
        c.wait_send()
    for c in rows_c:
        c.wait_recv()
        c.wait_send()
    g.sent()


def first_call(n_batch, text, patches, gain_tile, patch_tile, w_qkv, w_so, w_co, w_down, cot, valid):
    n_out = n_batch // 2
    dma = pltpu.SemaphoreType.DMA
    j, rows, columns = w_qkv.shape
    return pl.pallas_call(
        functools.partial(first_kernel, n_batch),
        out_shape=[
            jax.ShapeDtypeStruct((4,) + text.shape, BF),
            jax.ShapeDtypeStruct((4,) + patches.shape, BF),
            jax.ShapeDtypeStruct((n_batch,) + gain_tile.shape, BF),
            jax.ShapeDtypeStruct(patch_tile.shape, BF),
            jax.ShapeDtypeStruct((j, rows * n_batch, columns), BF),
            jax.ShapeDtypeStruct((4,) + cot.shape, BF),
        ]
        + [jax.ShapeDtypeStruct(w.shape[::-1], BF) for w in (w_so, w_co, w_down)],
        in_specs=[pl.BlockSpec(memory_space=pltpu.VMEM)] * 10,
        out_specs=[pl.BlockSpec(memory_space=pl.ANY)] * 6 + [pl.BlockSpec(memory_space=pltpu.VMEM)] * 3,
        scratch_shapes=[
            pltpu.VMEM(cot.shape, BF),
            pltpu.VMEM((4,) + gain_tile.shape, BF),
            pltpu.VMEM(gain_tile.shape, BF),
        ]
        + BatchGather.semaphores(n_out, 4)
        + [dma((5, 3)), dma((5, 3)), dma((5,))],
        compiler_params=pltpu.CompilerParams(collective_id=0, has_side_effects=True),
        cost_estimate=pl.CostEstimate(flops=10**6, bytes_accessed=300 * 10**6, transcendentals=0),
    )(text, patches, gain_tile, patch_tile, w_qkv, w_so, w_co, w_down, cot, valid)


def mm(a, b):
    return lax.dot_general(a, b, (((1,), (0,)), ((), ())), preferred_element_type=F32)


def mm_nt(a, b):
    return lax.dot_general(a, b, (((1,), (1,)), ((), ())), preferred_element_type=F32)


def mm_tn(a, b):
    return lax.dot_general(a, b, (((0,), (0,)), ((), ())), preferred_element_type=F32)


class Local:
    def __init__(self, sems):
        self.sems = sems
        self.used = 0

    def go(self, src, dst):
        copy = pltpu.make_async_copy(src, dst, self.sems.at[self.used])
        self.used += 1
        copy.start()
        return copy


STEP = 32


def each_rows(rows, body, step=STEP):
    def one(r, carry):
        body(pl.ds(pl.multiple_of(r * step, step), step))
        return carry

    lax.fori_loop(0, rows // step, one, 0)


def each(count, body, first=0):
    def one(k, carry):
        body(k)
        return carry

    lax.fori_loop(first, count, one, 0)


def cols(n, width):
    return pl.ds(pl.multiple_of(n * width, width), width)


def rms_of(values, gain):
    return values * lax.rsqrt(jnp.mean(values * values, axis=-1, keepdims=True) + 1e-06) * gain


def attend(q_ref, k_ref, v_ref, out_ref, lse_ref, j, allowed, heads):
    for h in range(heads):
        at = pl.ds(h * HD, HD)
        s = mm_nt(q_ref[j, :, at], k_ref[j, :, at]) * HD ** (-0.5)
        s = jnp.where(allowed, s, -1e30)
        top = jnp.max(s, axis=-1, keepdims=True)
        e = jnp.exp(s - top)
        total = jnp.sum(e, axis=-1, keepdims=True)
        probs = (e / total).astype(BF)
        out_ref[j, :, at] = mm(probs, v_ref[j, :, at]).astype(BF)
        lse_ref[j, :, pl.ds(h, 1)] = top + jnp.log(total)


def causal_ok(key_row, rows):
    shape = (rows, key_row.shape[1])
    return (lax.broadcasted_iota(jnp.int32, shape, 1) <= lax.broadcasted_iota(jnp.int32, shape, 0)) & (
        jnp.broadcast_to(key_row, shape) > 0.5
    )


class BranchSum:
    def __init__(self, place, bufs, send, recv, step=512):
        self.p = place
        self.step = step
        self.fs, self.ns, self.cf, self.yr, self.cn = bufs
        self.to_core = remote(self.fs, self.cf, send.at[0], recv.at[0], batch=place.b, mod=place.core)
        self.to_far = remote(self.fs, self.yr, send.at[1], recv.at[1], batch=place.b, mod=place.far)
        self.to_near = remote(self.ns, self.cn, send.at[2], recv.at[2], batch=place.b, mod=place.core)

    def send(self, part):
        p, step = self.p, self.step
        n = self.fs.shape[1] // step

        def first(k):
            self.fs[:, cols(k, step)] = part(p.farcore, k).astype(BF)

        def second(k):
            self.ns[:, cols(k, step)] = part(p.core, k).astype(BF)

        def third(k):
            at = cols(k, step)
            self.fs[:, at] = (part(p.far, k) + self.cf[:, at].astype(F32)).astype(BF)

        each(n, first)
        self.to_core.start()
        each(n, second)
        self.to_near.start()
        self.to_core.wait()
        each(n, third)
        self.to_far.start()

    def receive(self):
        self.to_near.wait_recv()
        self.to_far.wait_recv()

    def others(self, rows, at=slice(None)):
        return self.cn[rows, at].astype(F32) + self.yr[rows, at].astype(F32)

    def sent(self):
        self.to_near.wait_send()
        self.to_far.wait_send()


def halves(shard, whole, rows):
    half = rows // 2

    def piece(k):
        return (shard.at[pl.ds(k * half, half)], lambda q: whole.at[pl.ds(q * rows + k * half, half)])

    return [piece(0), piece(1)]


def forward_kernel(n_batch, *refs):
    (text_all, patch_all, gains, patch_own, key_ok, cross_ok, qkv_w,
     w_so, w_ckv, w_cq, w_co, w_gu, w_down) = refs[:13]
    (so_all, patch_w, ckv_all, cq_all, co_all, gu_all, down_all, act1_o, act2_o, act3_o, qkv_o, cqkv_o,
     ctx_o, cctx_o, lse_o, clse_o, pp_o, x1_o, x2_o, gate_o, up_o, h_o) = refs[13:35]
    (act, x, wq, wo, wp, pat, pp, qkv, ctx, lse, fs, ns, cf, yr, cn, wg, gate, gate_b, up, hid,
     z_send, z_recv, x_send, x_recv, own, mod_send, mod_recv, sum_send, sum_recv, loc) = refs[35:]
    p = Place(n_batch)
    local = Local(loc)
    rows, width = x.shape
    heads = wq.shape[2] // HD
    cq_r, pr = w_cq.shape[0], patch_own.shape[0]
    g = BatchGather(
        p,
        [
            (w_so, lambda q: so_all.at[pl.ds(q * cq_r, cq_r)]),
            (patch_own, lambda q: patch_w.at[pl.ds(q * pr, pr)]),
            (w_ckv.at[0], lambda q: ckv_all.at[0, pl.ds(q * cq_r, cq_r)]),
            (w_ckv.at[1], lambda q: ckv_all.at[1, pl.ds(q * cq_r, cq_r)]),
            (w_cq, lambda q: cq_all.at[pl.ds(q * cq_r, cq_r)]),
            (w_co, lambda q: co_all.at[pl.ds(q * cq_r, cq_r)]),
        ]
        + halves(w_gu.at[0], gu_all.at[0], cq_r)
        + halves(w_gu.at[1], gu_all.at[1], cq_r)
        + halves(w_down, down_all, cq_r),
        (z_send, z_recv, x_send, x_recv, own),
    )
    SO, PATCH, CK, CV, CQ, CO, GATE, GATE2, UP, UP2, DOWN, DOWN2 = range(12)
    load_act = local.go(text_all, act)
    load_q = local.go(qkv_w, wq)
    load_pat = local.go(patch_all, pat)
    p.greet()
    g.start()
    bufs = (fs, ns, cf, yr, cn)
    one = BranchSum(p, bufs, sum_send.at[0], sum_recv.at[0])
    two = BranchSum(p, bufs, sum_send.at[1], sum_recv.at[1])
    act_block = lambda j: act.at[j]
    col_w = wq.shape[2]
    pp_g = ModGather(p, lambda j: pp.at[:, :, pl.ds(pl.multiple_of(j * col_w, col_w), col_w)], mod_send.at[0], mod_recv.at[0])
    a2_g = ModGather(p, act_block, mod_send.at[1], mod_recv.at[1])
    a3_g = ModGather(p, act_block, mod_send.at[2], mod_recv.at[2])

    load_act.wait()
    x[...] = act[p.m].astype(F32)

    def norm_one(j):
        def body(r):
            act[j, r, :] = rms_of(act[j, r, :].astype(F32), gains[pl.ds(0, 1), :]).astype(BF)

        each_rows(rows, body)

    each(4, norm_one)
    save_act = local.go(act, act1_o)
    load_q.wait()

    def project(j):
        for w in range(3):
            qkv[w, j] = mm(act[j], wq[w]).astype(BF)

    each(4, project)
    save_qkv = local.go(qkv, qkv_o)
    g.pump(SO)
    attend_one = lambda j: attend(qkv.at[0], qkv.at[1], qkv.at[2], ctx, lse, j, causal_ok(key_ok[j, pl.ds(0, 1), :], rows), heads)
    each(4, attend_one)
    save_ctx = local.go(ctx, ctx_o)
    save_lse = local.go(lse, lse_o)
    g.arrived(SO)
    load_o = local.go(so_all, wo)
    save_act.wait()
    save_qkv.wait()
    load_o.wait()
    part = lambda j, k: mm_nt(ctx[j], wo[cols(k, 512), :])
    one.send(part)

    def add_own(k):
        at = cols(k, 512)
        x[:, at] += part(p.m, k)

    each(width // 512, add_own)
    g.arrived(PATCH)
    if pr != cq_r:
        wp[...] = jnp.zeros(wp.shape, BF)
    for c in [local.go(patch_w.at[pl.ds(q * pr, pr)], wp.at[pl.ds(q * cq_r, pr)]) for q in range(n_batch)]:
        c.wait()
    load_pat.wait()
    own_cols = pl.ds(pl.multiple_of(p.m * col_w, col_w), col_w)

    def project_patch(j):
        pp[j, :, own_cols] = mm(pat[j], wp[...]).astype(BF)

    each(4, project_patch)
    pp_g.start()
    one.receive()

    def finish_one(r):
        x[r, :] += one.others(r)
        act[p.m, r, :] = rms_of(x[r, :], gains[pl.ds(1, 1), :]).astype(BF)

    each_rows(rows, finish_one)
    a2_g.start()
    save_x = local.go(x, x1_o)
    one.sent()
    g.pump(CV)
    pp_g.forward()
    g.pump(CQ)
    a2_g.forward()
    g.arrived(CK)
    load_ck = local.go(ckv_all.at[0], wq.at[1])
    pp_g.finish()
    save_pp = local.go(pp, pp_o)
    load_ck.wait()

    def project_pp(w):
        def body(j):
            qkv[w, j] = mm(pp[j], wq[w]).astype(BF)

        return body

    each(4, project_pp(1))
    g.arrived(CV)
    load_cv = local.go(ckv_all.at[1], wq.at[2])
    load_cv.wait()
    each(4, project_pp(2))
    g.arrived(CQ)
    load_cq = local.go(cq_all, wq.at[0])
    a2_g.finish()
    save_act = local.go(act, act2_o)
    load_cq.wait()

    def project_cq(j):
        qkv[0, j] = mm(act[j], wq[0]).astype(BF)

    each(4, project_cq)
    save_ctx.wait()
    save_lse.wait()
    save_qkv = local.go(qkv, cqkv_o)

    def attend_two(j):
        ok = jnp.broadcast_to(cross_ok[j, pl.ds(0, 1), :], (rows, cross_ok.shape[2])) > 0.5
        attend(qkv.at[0], qkv.at[1], qkv.at[2], ctx, lse, j, ok, heads)

    each(4, attend_two)
    save_ctx = local.go(ctx, cctx_o)
    save_lse = local.go(lse, clse_o)
    g.arrived(CO)
    load_o = local.go(co_all, wo)
    save_act.wait()
    save_x.wait()
    load_o.wait()
    two.send(part)
    each(width // 512, add_own)
    g.pump(GATE2)
    two.receive()

    def finish_two(r):
        x[r, :] += two.others(r)
        act[p.m, r, :] = rms_of(x[r, :], gains[pl.ds(2, 1), :]).astype(BF)

    each_rows(rows, finish_two)
    a3_g.start()
    save_x = local.go(x, x2_o)
    two.sent()
    g.pump(UP)
    a3_g.forward()
    a3_g.finish()
    save_act = local.go(act, act3_o)

    g.arrived(GATE)
    g.arrived(GATE2)
    load_g = local.go(gu_all.at[0], wg)
    load_g.wait()

    def gate_one(j):
        gate[j] = mm(act[j], wg[...])
        gate_b[j] = gate[j].astype(BF)

    each(4, gate_one)
    save_gate = local.go(gate_b, gate_o)
    g.arrived(UP)
    g.arrived(UP2)
    load_g = local.go(gu_all.at[1], wg)
    load_g.wait()

    def up_one(j):
        u = mm(act[j], wg[...])
        up[j] = u.astype(BF)
        hid[j] = (jax.nn.gelu(gate[j], approximate=True) * u).astype(BF)

    each(4, up_one)
    save_up = local.go(up, up_o)
    save_h = local.go(hid, h_o)
    g.arrived(DOWN)
    g.arrived(DOWN2)
    g.sent()
    for c in (save_act, save_x, save_gate, save_up, save_h, save_ctx, save_lse, save_qkv, save_pp):
        c.wait()


def forward_call(n_batch, text_all, patch_all, gains, patch_own, key_ok, cross_ok, qkv_w,
                 w_so, w_ckv, w_cq, w_co, w_gu, w_down):
    n_out = n_batch // 2
    dma = pltpu.SemaphoreType.DMA
    items, rows, width = text_all.shape
    c, f = qkv_w.shape[2], w_gu.shape[2]
    patch_width = patch_all.shape[2]
    keys = patch_all.shape[1]
    sds = jax.ShapeDtypeStruct
    any_ = pl.BlockSpec(memory_space=pl.ANY)
    vmem = pl.BlockSpec(memory_space=pltpu.VMEM)
    big = (items, rows, width)
    return pl.pallas_call(
        functools.partial(forward_kernel, n_batch),
        out_shape=[
            sds((width, c), BF), sds((n_batch * patch_own.shape[0], c), BF), sds((2, width, c), BF), sds((width, c), BF),
            sds((width, c), BF), sds((2, width, f), BF), sds((width, f), BF),
            sds(big, BF), sds(big, BF), sds(big, BF),
            sds((3, items, rows, c), BF), sds((3, items, rows, c), BF),
            sds((items, rows, c), BF), sds((items, rows, c), BF),
            sds((items, rows, 128), F32), sds((items, rows, 128), F32),
            sds((items, keys, width), BF), sds((rows, width), F32), sds((rows, width), F32),
            sds((items, rows, f), BF), sds((items, rows, f), BF), sds((items, rows, f), BF),
        ],
        in_specs=[any_, any_, vmem, vmem, vmem, vmem, any_] + [vmem] * 6,
        out_specs=[any_] * 22,
        scratch_shapes=[
            pltpu.VMEM(big, BF), pltpu.VMEM((rows, width), F32), pltpu.VMEM((3, width, c), BF),
            pltpu.VMEM((width, c), BF), pltpu.VMEM((patch_width, c), BF), pltpu.VMEM((items, keys, patch_width), BF),
            pltpu.VMEM((items, keys, width), BF), pltpu.VMEM((3, items, rows, c), BF), pltpu.VMEM((items, rows, c), BF),
            pltpu.VMEM((items, rows, 128), F32),
        ]
        + [pltpu.VMEM((rows, width), BF)] * 5
        + [pltpu.VMEM((width, f), BF), pltpu.VMEM((items, rows, f), F32), pltpu.VMEM((items, rows, f), BF), pltpu.VMEM((items, rows, f), BF), pltpu.VMEM((items, rows, f), BF)]
        + BatchGather.semaphores(n_out, 12)
        + [dma((3, 3)), dma((3, 3)), dma((2, 3)), dma((2, 3)), dma((32 + n_batch,))],
        compiler_params=pltpu.CompilerParams(collective_id=1, has_side_effects=True, vmem_limit_bytes=VMEM_LIMIT),
        cost_estimate=pl.CostEstimate(flops=35 * 10**9, bytes_accessed=600 * 10**6, transcendentals=0),
    )(text_all, patch_all, gains, patch_own, key_ok, cross_ok, qkv_w, w_so, w_ckv, w_cq, w_co, w_gu, w_down)


class GradSum:
    def __init__(self, place, pieces, mine, got, sems, loc):
        self.p = place
        self.pieces = pieces
        self.mine, self.got = mine, got
        self.x_send, self.x_recv, self.z_send, self.z_recv = sems
        self.loc = loc
        self.ready = self.started = self.done = 0
        self.window = 1

    @staticmethod
    def semaphores(n_out, count):
        dma = pltpu.SemaphoreType.DMA
        return [dma((count,)), dma((count,)), dma((count, n_out)), dma((count, n_out))]

    def x_copy(self, t):
        whole, from_x, _ = self.pieces[t]
        return remote(whole.at[:, 1 - self.p.inner], from_x, self.x_send.at[t], self.x_recv.at[t],
                      batch=self.p.x_peer, mod=self.p.m)

    def z_copy(self, t, s):
        _, from_x, from_z = self.pieces[t]
        return remote(from_x.at[(self.p.outer + s) % self.p.n_out], from_z.at[s], self.z_send.at[t, s],
                      self.z_recv.at[t, s], batch=self.p.z_peer(s), mod=self.p.m)

    def kick(self):
        while self.started < self.ready and self.started - self.done < self.window:
            self.x_copy(self.started).start()
            self.started += 1

    def add(self):
        self.ready += 1
        self.kick()

    def pump(self, count=1):
        for _ in range(min(count, self.ready - self.done)):
            t = self.done
            whole, from_x, from_z = self.pieces[t]
            n_out, rows, width = from_x.shape
            self.x_copy(t).wait_recv()
            self.done += 1
            self.kick()
            mine = self.mine.at[:, pl.ds(0, rows), pl.ds(0, width)]
            got = self.got.at[:, pl.ds(0, rows), pl.ds(0, width)]
            one = pltpu.make_async_copy(whole.at[:, self.p.inner], mine, self.loc.at[0])
            two = pltpu.make_async_copy(from_x, got, self.loc.at[1])
            one.start()
            two.start()
            one.wait()
            two.wait()
            step = 16

            def body(o):
                def add(r):
                    mine[o, r, :] = (mine[o, r, :].astype(F32) + got[o, r, :].astype(F32)).astype(BF)

                each_rows(rows, add, step)

            each(n_out, body)
            one = pltpu.make_async_copy(mine, from_x, self.loc.at[0])
            two = pltpu.make_async_copy(mine.at[self.p.outer], from_z.at[0], self.loc.at[1])
            one.start()
            two.start()
            one.wait()
            for s in self.p.shifts:
                self.z_copy(t, s).start()
            two.wait()

    def finish(self):
        self.pump(len(self.pieces))
        for t in range(len(self.pieces)):
            self.x_copy(t).wait_send()
            for s in self.p.shifts:
                self.z_copy(t, s).wait()


def attend_back(q_ref, k_ref, v_ref, do_ref, lse_ref, dq_ref, dk_ref, dv_ref, j, allowed, heads):
    scale = HD ** (-0.5)
    for h in range(heads):
        at = pl.ds(h * HD, HD)
        q, k, v, do = q_ref[j, :, at], k_ref[j, :, at], v_ref[j, :, at], do_ref[j, :, at]
        s = jnp.where(allowed, mm_nt(q, k) * scale, -1e30)
        probs = jnp.exp(s - lse_ref[j, :, pl.ds(h, 1)])
        dp = mm_nt(do, v)
        ds = (probs * (dp - jnp.sum(probs * dp, axis=-1, keepdims=True))).astype(BF)
        dv_ref[j, :, at] = mm_tn(probs.astype(BF), do).astype(BF)
        dq_ref[j, :, at] = (mm(ds, k) * scale).astype(BF)
        dk_ref[j, :, at] = (mm_tn(ds, q) * scale).astype(BF)


def gelu_parts(g):
    c = 0.7978845608028654
    t = jnp.tanh(c * (g + 0.044715 * g * g * g))
    half = 0.5 * (1.0 + t)
    return g * half, half + 0.5 * g * (1.0 - t * t) * c * (1.0 + 3 * 0.044715 * g * g)


def backward_kernel(n_batch, *refs):
    (dy_all, text, pat_all, gains, key_ok, cross_ok, qkv_w, so_all, ckv_all, cq_all, co_all, gu_all, down_all,
     act1, act2, act3, qkv_i, cqkv_i, ctx_i, cctx_i, lse_i, clse_i, pp_i, x1_i, x2_i, gate_i, up_i, h_i) = refs[:28]
    (result, d_text, gain_out, whole_f, from_x_f, from_z_f, whole_c, from_x_c, from_z_c,
     whole_p, from_x_p, from_z_p) = refs[28:40]
    (dy, act_a, act_b, gate, up, hid, w0, w1, qkv, dqkv, ctx, dctx, dpp, lse, g, da, v, fs, ns, cf, yr, cn,
     cf2, yr2, cn2, st, mine, got, dg, dgm, dgx, dgz,
     gx_send, gx_recv, gz_send, gz_recv, mod_send, mod_recv, sum_send, sum_recv, gain_send, gain_recv,
     gx, loc, loc2) = refs[40:]
    p = Place(n_batch)
    local = Local(loc)
    items, rows, width = dy.shape
    c, f = qkv_w.shape[2], gu_all.shape[2]
    half = f // 2
    n_out, blk = p.n_out, width // n_batch
    heads = c // HD
    pieces = [(whole_f.at[k], from_x_f.at[k], from_z_f.at[k]) for k in range(6)]
    pieces += [(whole_c.at[k], from_x_c.at[k], from_z_c.at[k]) for k in range(8)]
    pieces.append((whole_p, from_x_p, from_z_p))
    gs = GradSum(p, pieces, mine, got, (gx_send, gx_recv, gz_send, gz_recv), loc2)
    left = pl.ds(0, c)
    right = pl.ds(c, c)

    load_dy = local.go(dy_all, dy)
    load_h = local.go(h_i, hid)
    load_w0 = local.go(down_all, w0)
    load_v = local.go(x2_i, v)
    load_gate = local.go(gate_i, gate)
    load_up = local.go(up_i, up)
    load_w1 = local.go(gu_all.at[0], w1)
    load_a = local.go(act3, act_a)
    load_b = local.go(act2, act_b)
    p.greet()
    set_a = (fs, ns, cf, yr, cn)
    set_b = (fs, ns, cf2, yr2, cn2)
    sums = [
        BranchSum(p, bufs, sum_send.at[k], sum_recv.at[k])
        for k, bufs in enumerate((set_b, set_a, set_a, set_b, set_a))
    ]
    gathers = [ModGather(p, lambda j: dy.at[j], mod_send.at[k], mod_recv.at[k]) for k in range(2)]
    dg[...] = jnp.zeros(dg.shape, F32)

    def piece(acts, grads, first, count):
        t = gs.ready
        whole = pieces[t][0]
        used = whole.shape[2]
        chunk = max(256, 2 * blk)
        per = chunk // (2 * blk)

        def body(n):
            a = acts[:, :, cols(n, chunk)].reshape(items * rows, chunk)
            b = grads[:, :, pl.ds(first, count)].reshape(items * rows, count)
            st[pl.ds(n * per, per), :, :, pl.ds(0, count)] = mm_tn(a, b).astype(BF).reshape(per, 2, blk, count)

        each(width // chunk, body)
        copy = pltpu.make_async_copy(st.at[:, :, pl.ds(0, used), pl.ds(0, count)], whole, loc2.at[2])
        copy.start()
        copy.wait()
        gs.add()

    def norm_back(k, total, v_rows):
        def body(r):
            grad = da[r, :] + total.others(r)
            val = v_rows(r)
            factor = lax.rsqrt(jnp.mean(val * val, axis=-1, keepdims=True) + 1e-06)
            dg[pl.ds(k, 1), :] += jnp.sum(grad * val * factor, axis=0, keepdims=True)
            scaled = gains[pl.ds(k, 1), :] * grad
            back = factor * scaled - val * (factor * factor * factor * jnp.mean(scaled * val, axis=-1, keepdims=True))
            g[r, :] += back
            if k:
                dy[p.m, r, :] = g[r, :].astype(BF)

        each_rows(rows, body)

    load_dy.wait()
    load_h.wait()
    g[...] = dy[p.m].astype(F32)
    piece(dy, hid, 0, half)
    piece(dy, hid, half, half)
    load_w0.wait()
    load_v.wait()
    out_part = lambda j, k: mm_nt(hid[j], w0[cols(k, 512), :])
    sums[0].send(out_part)

    def result_own(k):
        at = cols(k, 512)
        da[:, at] = v[:, at] + out_part(p.m, k)

    each(width // 512, result_own)
    load_gate.wait()
    load_up.wait()

    def mix_back(j):
        dh = mm(dy[j], w0[...])
        value, slope = gelu_parts(gate[j].astype(F32))
        gate[j] = (dh * up[j].astype(F32) * slope).astype(BF)
        hid[j] = (dh * value).astype(BF)

    each(items, mix_back)
    load_w0 = local.go(gu_all.at[1], w0)
    gs.pump()
    sums[0].receive()

    def result_done(r):
        da[r, :] += sums[0].others(r)

    each_rows(rows, result_done)
    save_result = local.go(da, result)
    sums[0].sent()
    load_w1.wait()
    load_w0.wait()
    act_part = lambda j, k: mm_nt(gate[j], w1[cols(k, 512), :]) + mm_nt(hid[j], w0[cols(k, 512), :])
    sums[1].send(act_part)
    save_result.wait()

    def own_part(part):
        def body(k):
            da[:, cols(k, 512)] = part(p.m, k)

        each(width // 512, body)

    own_part(act_part)
    load_w0 = [local.go(co_all, w0.at[:, left]), local.go(cq_all, w0.at[:, right])]
    load_w1 = [local.go(ckv_all.at[0], w1.at[:, left]), local.go(ckv_all.at[1], w1.at[:, right])]
    load_s = [local.go(cqkv_i, qkv), local.go(cctx_i, ctx), local.go(clse_i, lse)]
    load_a.wait()
    piece(act_a, gate, 0, half)
    piece(act_a, gate, half, half)
    gs.pump()
    sums[1].receive()
    norm_back(2, sums[1], lambda r: v[r, :])
    gathers[0].start()
    sums[1].sent()
    load_v = local.go(x1_i, v)
    piece(act_a, hid, 0, half)
    piece(act_a, hid, half, half)
    load_a = local.go(pp_i, act_a)
    gs.pump()
    gathers[0].forward()
    gathers[0].finish()

    for copy in load_w0 + load_w1 + load_s:
        copy.wait()

    def ctx_back(j):
        dctx[j] = mm(dy[j], w0[:, left]).astype(BF)

    each(items, ctx_back)
    piece(dy, ctx, 0, c)

    def cross_back(j):
        ok = jnp.broadcast_to(cross_ok[j, pl.ds(0, 1), :], (rows, cross_ok.shape[2])) > 0.5
        attend_back(qkv.at[0], qkv.at[1], qkv.at[2], dctx, lse, dqkv.at[0], dqkv.at[1], dqkv.at[2], j, ok, heads)

    each(items, cross_back)
    query_part = lambda j, k: mm_nt(dqkv[0, j], w0[cols(k, 512), right])
    sums[2].send(query_part)
    gs.pump()
    own_part(query_part)
    load_w0 = [local.go(so_all, w0.at[:, left]), local.go(qkv_w.at[0], w0.at[:, right])]
    load_s = [local.go(qkv_i, qkv), local.go(ctx_i, ctx), local.go(lse_i, lse)]
    load_b.wait()
    piece(act_b, dqkv.at[0], 0, c)
    load_b = local.go(act1, act_b)
    load_a.wait()
    piece(act_a, dqkv.at[1], 0, c)
    load_v.wait()
    sums[2].receive()
    norm_back(1, sums[2], lambda r: v[r, :])
    gathers[1].start()
    sums[2].sent()
    piece(act_a, dqkv.at[2], 0, c)
    load_a = local.go(pat_all, act_a)
    gs.pump()
    gathers[1].forward()
    gathers[1].finish()

    proj_part = lambda j, k: mm_nt(dqkv[1, k], w1[cols(j, c), left]) + mm_nt(dqkv[2, k], w1[cols(j, c), right])
    sums[3].send(proj_part)

    def proj_own(k):
        dpp[k] = proj_part(p.m, k).astype(BF)

    each(items, proj_own)
    load_w1 = [local.go(qkv_w.at[1], w1.at[:, left]), local.go(qkv_w.at[2], w1.at[:, right])]

    for copy in load_w0 + load_s:
        copy.wait()
    each(items, ctx_back)
    piece(dy, ctx, 0, c)
    gs.pump()

    def self_back(j):
        ok = causal_ok(key_ok[j, pl.ds(0, 1), :], rows)
        attend_back(qkv.at[0], qkv.at[1], qkv.at[2], dctx, lse, dqkv.at[0], dqkv.at[1], dqkv.at[2], j, ok, heads)

    each(items, self_back)
    gs.pump()
    sums[3].receive()

    def proj_done(k):
        every = pl.ds(0, rows)
        dpp[k] = (dpp[k].astype(F32) + sums[3].others(every, cols(k, c))).astype(BF)

    each(items, proj_done)
    sums[3].sent()
    for copy in load_w1:
        copy.wait()
    self_part = lambda j, k: (
        mm_nt(dqkv[0, j], w0[cols(k, 512), right])
        + mm_nt(dqkv[1, j], w1[cols(k, 512), left])
        + mm_nt(dqkv[2, j], w1[cols(k, 512), right])
    )
    sums[4].send(self_part)
    own_part(self_part)
    gs.pump()
    load_b.wait()
    for k in range(3):
        piece(act_b, dqkv.at[k], 0, c)
    load_a.wait()
    piece(act_a, dpp, 0, c)
    gs.pump()
    sums[4].receive()
    norm_back(0, sums[4], lambda r: text[r, :].astype(F32))
    save_text = local.go(g, d_text)
    sums[4].sent()

    mod_g = [
        remote(dg, dgm.at[k], gain_send.at[k], gain_recv.at[k], batch=p.b, mod=j)
        for k, j in enumerate((p.core, p.far, p.farcore))
    ]
    for copy in mod_g:
        copy.start()
    gs.pump()
    for copy in mod_g:
        copy.wait()
    dg[...] += dgm[0] + dgm[1] + dgm[2]
    across = remote(dg, dgx, gx.at[0], gx.at[1], batch=p.x_peer, mod=p.m)
    across.start()
    gs.pump()
    across.wait()
    dg[...] += dgx[...]
    along = [
        remote(dg, dgz.at[s], gain_send.at[3 + s], gain_recv.at[3 + s], batch=p.z_peer(s), mod=p.m)
        for s in p.shifts
    ]
    for copy in along:
        copy.start()
    gs.pump()
    for copy in along:
        copy.wait()
    total = dg[...]
    for s in p.shifts:
        total = total + dgz[s]
    gain_out[...] = total
    gs.finish()
    save_text.wait()


def backward_call(n_batch, inputs, patch_rows):
    n_out = n_batch // 2
    dma = pltpu.SemaphoreType.DMA
    sds = jax.ShapeDtypeStruct
    items, rows, width = inputs[0].shape
    c, f = inputs[6].shape[2], inputs[11].shape[2]
    blk = width // n_batch
    any_ = pl.BlockSpec(memory_space=pl.ANY)
    vmem = pl.BlockSpec(memory_space=pltpu.VMEM)
    big = (items, rows, width)
    heads_shape = (items, rows, c)
    V = lambda shape, dtype=BF: pltpu.VMEM(shape, dtype)

    def bufs(count, r, w):
        lead = (count,) if count else ()
        return [sds(lead + (n_out, 2, r, w), BF), sds(lead + (n_out, r, w), BF), sds(lead + (n_out, r, w), BF)]

    return pl.pallas_call(
        functools.partial(backward_kernel, n_batch),
        out_shape=[sds((rows, width), F32), sds((rows, width), F32), sds((8, width), F32)]
        + bufs(6, blk, f // 2) + bufs(8, blk, c) + bufs(0, patch_rows, c),
        in_specs=[any_, vmem, any_, vmem, vmem, vmem] + [any_] * 22,
        out_specs=[any_, any_, vmem] + [any_] * 9,
        scratch_shapes=[V(big)] * 3
        + [V((items, rows, f))] * 3
        + [V((width, f))] * 2
        + [V((3,) + heads_shape)] * 2
        + [V(heads_shape)] * 3
        + [V((items, rows, 128), F32)]
        + [V((rows, width), F32)] * 3
        + [V((rows, width))] * 8
        + [V((n_out, 2, blk, f // 2)), V((n_out, blk, f // 2)), V((n_out, blk, f // 2))]
        + [V((8, width), F32), V((3, 8, width), F32), V((8, width), F32), V((n_out, 8, width), F32)]
        + GradSum.semaphores(n_out, 15)
        + [dma((2, 3)), dma((2, 3)), dma((5, 3)), dma((5, 3)), dma((3 + n_out,)), dma((3 + n_out,)), dma((2,)),
           dma((48,)), dma((3,))],
        compiler_params=pltpu.CompilerParams(collective_id=2, has_side_effects=True, vmem_limit_bytes=VMEM_LIMIT),
        cost_estimate=pl.CostEstimate(flops=75 * 10**9, bytes_accessed=800 * 10**6, transcendentals=0),
    )(*inputs)


def local(n_batch, n_mod, text, patches, text_lengths, patch_mask, cotangent, gains,
          w_qkv, w_so, w_cq, w_ckv, w_co, w_patch, w_gu, w_down):
    own_items, text_rows, width = text.shape
    mod = lax.axis_index("mod")
    nb = n_batch
    blk = width // nb
    positions = jnp.arange(text_rows)

    gw = blk // n_mod
    gain_tile = lax.dynamic_update_slice(jnp.zeros((16, blk), BF), gains, (0, mod * gw))
    col_w = width // n_mod
    pr = w_patch.shape[0]
    pr_pad = -(-pr // 16) * 16
    patch_tile = jnp.pad(w_patch, ((0, pr_pad - pr), (0, 0))).reshape(pr_pad, n_mod, col_w)
    patch_tile = jnp.transpose(patch_tile, (1, 0, 2))
    block, block_pad = n_mod * pr, -(-n_mod * pr // 16) * 16
    patch_in = jnp.pad(patches[0].reshape(-1, nb, block), ((0, 0), (0, 0), (0, blk - block))).reshape(-1, width)
    own_length = lax.dynamic_slice_in_dim(text_lengths, mod * own_items, own_items)
    valid = jnp.broadcast_to((positions[:, None] < own_length).astype(F32), (text_rows, 128))
    text_all, patch_all, gain_raw, patch_rows, self_qkv, dy_all, so_t, co_t, down_t = first_call(
        n_batch, text[0], patch_in, gain_tile, patch_tile, w_qkv, w_so, w_co, w_down, cotangent[0], valid
    )
    gain_all = jnp.transpose(gain_raw[:, :8], (1, 0, 2)).reshape(8, width).astype(F32)
    patch_own = patch_rows[:, :pr].reshape(block, col_w)
    patch_own = jnp.pad(patch_own, ((0, block_pad - block), (0, 0)))
    row_ok = (positions[None, :] < text_lengths[:, None]).astype(F32)
    key_ok = jnp.broadcast_to(row_ok[:, None, :], (n_mod, 8, text_rows))
    cross_ok = jnp.broadcast_to((patch_mask > 0).astype(F32)[:, None, :], (n_mod, 8, patch_mask.shape[1]))
    (so_all, _, ckv_all, cq_all, co_all, gu_all, down_all, act1, act2, act3, qkv, cqkv,
     ctx, cctx, lse, clse, pp, x1, x2, gate, up, hid) = forward_call(
        n_batch, text_all, patch_all, gain_all, patch_own, key_ok, cross_ok, self_qkv,
        so_t, w_ckv, w_cq, co_t, w_gu, down_t)
    outs = backward_call(
        n_batch,
        (dy_all, text[0], patch_all, gain_all, key_ok, cross_ok, self_qkv, so_all, ckv_all, cq_all, co_all, gu_all,
         down_all, act1, act2, act3, qkv, cqkv, ctx, cctx, lse, clse, pp, x1, x2, gate, up, hid),
        block_pad,
    )
    result, d_text, gain_sum = outs[:3]
    sum_f, sum_c, sum_p = outs[5], outs[8], outs[11]
    at = lax.axis_index("batch") * blk + mod * gw
    d_gains = lax.dynamic_slice(gain_sum, (0, at), (3, gw))

    def total(parts, axis=0):
        return jnp.sum(parts.astype(F32), axis=axis)

    def pair(k):
        return jnp.concatenate([total(sum_f[k]), total(sum_f[k + 1])], axis=1)

    grad_patch = total(sum_p)[:block].reshape(n_mod, pr, col_w)
    grad_patch = lax.all_to_all(grad_patch, "mod", 0, 0, tiled=True)
    grad_patch = jnp.transpose(grad_patch, (1, 0, 2)).reshape(pr, width)
    return (
        result[None],
        d_text[None],
        d_gains,
        total(sum_c[5:8], 1),
        total(sum_c[4]).T,
        total(sum_c[1]),
        total(sum_c[2:4], 1),
        total(sum_c[0]).T,
        grad_patch,
        jnp.stack([pair(2), pair(4)]),
        pair(0).T,
    )


def solution(mesh):
    placed = (
        P(("batch", "mod"), None, None),
        P(("batch", "mod"), None, None),
        P("batch"),
        P("batch", None),
        P(("batch", "mod"), None, None),
        P(None, ("batch", "mod")),
        P(None, "batch", "mod"),
        P("mod", "batch"),
        P("batch", "mod"),
        P(None, "batch", "mod"),
        P("mod", "batch"),
        P(("batch", "mod"), None),
        P(None, "batch", "mod"),
        P("mod", "batch"),
    )

    def run(*args):
        return local(mesh.shape["batch"], mesh.shape["mod"], *args)

    return jax.shard_map(
        run,
        mesh=mesh,
        in_specs=placed,
        out_specs=(
            P(("batch", "mod"), None, None),
            P(("batch", "mod"), None, None),
            P(None, ("batch", "mod")),
            P(None, "batch", "mod"),
            P("mod", "batch"),
            P("batch", "mod"),
            P(None, "batch", "mod"),
            P("mod", "batch"),
            P(("batch", "mod"), None),
            P(None, "batch", "mod"),
            P("mod", "batch"),
        ),
        check_vma=False,
    )
```

time: 1560 us -> 924 us (0.59)
  Pallas kernels: 445 us -> 865 us
  local copies, waits for them, and re-layouts: 385 us -> 21.6 us
  waiting for transfers between devices: 310 us -> 0.01 us
  matrix products: 172 us -> 0 us
  starting transfers between devices: 159 us -> 4.12 us
  other arithmetic: 52 us -> 22.8 us
    pallas_call x0 -> x1, Pallas kernels: none -> 440 us  [backward_call(): pl.pallas_call(functools.partial(backward_kernel, n_batch), out_shape=[sd...]
    ppermute x52 -> x0, waiting for transfers between devices: 308 us -> none  [the longest x13 189 us: along_x(): return lax.ppermute(value, 'batch', [(b, b ^ 1) for b in range(self.size)])]
    unnamed x327 -> x16, local copies, waits for them, and re-layouts: 209 us -> 9.65 us
    dot_general x42 -> x0, matrix products: 172 us -> none  [dot(): return jnp.einsum(spec, a, b, preferred_element_type=F32)]
    ppermute x52 -> x0, starting transfers between devices: 154 us -> none  [the longest x39 140 us: along_z(): return lax.ppermute(value, 'batch', pairs)]
    slice x14 -> x1, local copies, waits for them, and re-layouts: 64.6 us -> 0.95 us  [local(): patch_own = patch_rows[:, :pr].reshape(block, col_w)]
    reshape x8 -> x3, local copies, waits for them, and re-layouts: 38.2 us -> 2.96 us  [the longest x1 1.42 us: local(): jnp.pad(patches[0].reshape(-1, nb, block), ((0, 0), (0, 0), (0, blk - blo...]
    all_gather x3 -> x0, local copies, waits for them, and re-layouts: 18.6 us -> none  [mod_gather(): return lax.all_gather(value, 'mod', axis=axis, tiled=True)]
  transfers between devices with their start and end apart: 61 -> 1, of which waited for: 24 -> 0; matrix products, arithmetic and copies ran while one was open for 33% -> 2% of each run, Pallas kernels for 29% -> 0%
where the time goes in v3:
time: 924 us; the launch traced here: 915 us
  Pallas kernels  865 us (94%)
  other arithmetic  22.8 us (2%)
  local copies, waits for them, and re-layouts  21.6 us (2%)
    pallas_call x1, Pallas kernels, backward_call(): pl.pallas_call(functools.partial(backward_kernel, n_batch), out_shape=[sd...  440 us
    pallas_call x1, Pallas kernels, forward_call(): pl.pallas_call(functools.partial(forward_kernel, n_batch), out_shape=[sds...  333 us
    pallas_call x1, Pallas kernels, first_call(): pl.pallas_call(functools.partial(first_kernel, n_batch), out_shape=[jax.S...  92.1 us
  transfers between devices with their start and end apart: 1, of which 0 were waited for; matrix products, arithmetic and copies ran while one was open for 2% of the time, Pallas kernels for 0%

profile of v3, /device:TPU:0, one launch (start us, length us, event | category | flops | bytes accessed | tf_op | source)
XLA Modules:
  0.0 914.6 jit_solution(15785316161388919000)
XLA Ops:
  0.6 0.7 fusion
  1.4 1.2 dynamic_slice.6
  2.6 0.6 compare_convert_fusion.1
  3.3 0.7 compare_convert_fusion
  4.0 1.0 pad.9
  4.9 0.7 copy.43
  5.6 1.5 copy.32
  7.2 0.0 copy-start.3
  7.2 0.1 pad.8
  7.3 1.4 copy.39.patches
  8.7 0.0 copy-done.3
  8.7 0.3 dynamic_update_slice.3.gain_tile
  9.0 0.0 copy-start.2
  9.0 0.8 broadcast_in_dim.13.valid
  9.8 0.0 copy-done.2
  9.8 92.1 %shard_map.221 = (bf16[4,256,2048]{2,1,0:T(8,128)(2,1)}, bf16[4,256,2048]{2,1,0:T(8,128)(2,1)}, bf16[8,16,256]{2,1,0:T(8,128)(2,1)}, bf16[4,64,512]{2,1,0:T(8,12...) custom-call(bf16[256,2048]{1,0:T(8,128)(2,1)} %bitcast.38, ...), custom_call_target="tpu_custom_call" | custom-call | flops 1000000 | bytes 300000000 | tf_op jit(solution)/shard_map/pallas_call | solution.py:221
  101.9 1.4 slice_convert_fusion
  103.3 1.0 slice.40
  104.2 0.7 reshape.80.refs_3_
  104.9 0.6 broadcast_in_dim.14.refs_4_
  105.6 0.6 broadcast_in_dim.15.refs_5_
  106.2 333.0 %shard_map.222 = (bf16[2048,512]{1,0:T(8,128)(2,1)}, bf16[1664,512]{1,0:T(8,128)(2,1)}, bf16[2,2048,512]{2,1,0:T(8,128)(2,1)}, bf16[2048,512]{1,0:T(8,128)(2,1)}...) custom-call(bf16[4,256,2048]{2,1,0:T(8,128)(2,1)} %get-tuple-element, ...), custom_call_target="tpu_custom_call" | custom-call | flops 35000000512 | bytes 600000000 | tf_op jit(solution)/shard_map/pallas_call | solution.py:579
  439.2 439.9 %shard_map.223 = (f32[256,2048]{1,0:T(8,128)}, f32[256,2048]{1,0:T(8,128)}, f32[8,2048]{1,0:T(8,128)}, bf16[6,4,2,256,640]{4,3,2,1,0:T(8,128)(2,1)}, bf16[6,4,25...) custom-call(bf16[4,256,2048]{2,1,0:T(8,128)(2,1)} %get-tuple-element, ...), custom_call_target="tpu_custom_call" | custom-call | flops 74999996416 | bytes 800000000 | tf_op jit(solution)/shard_map/pallas_call | solution.py:981
  879.0 1.3 convert_reduce_fusion.11
  880.3 0.8 reshape.81
  881.2 4.1 all-to-all-start
  885.3 3.0 convert_reduce_fusion.1
  888.3 3.7 convert_reduce_fusion
  891.9 3.3 convert_reduce_fusion.8
  895.2 1.0 copy.37
  896.2 1.0 copy.36
  897.2 5.0 convert_reduce_fusion.3
  902.2 0.1 maximum_bitcast_fusion.2
  902.3 1.5 copy.38
  903.8 1.3 constant_dynamic-slice_fusion
  905.1 1.3 maximum_bitcast_fusion
  906.4 1.7 pad_maximum_fusion
  908.1 0.0 copy-start.1
  908.1 0.0 all-to-all-done
  908.1 1.4 copy.35
  909.5 0.1 pad.18
  909.6 0.9 copy.41
  910.5 0.0 copy-done.1
  910.5 0.0 copy-start
  910.5 1.3 copy.47
  911.8 1.0 copy-done
  912.9 1.3 copy.48
  (1 shorter events, 0.0 us)
Async XLA Ops:
  7.2 1.5 copy-start.3
  9.0 0.8 copy-start.2
  881.2 26.9 %all-to-all-start = ((f32[4,52,512]{2,1,0:T(8,128)}), f32[4,52,512]{2,1,0:T(8,128)}, u32[]{:S(2)}, u32[]{:S(2)}) async-start(f32[4,52,512]{2,1,0:T(8,128)} %reshape.81), calls=%async_computation | async-start | bytes 917504 | tf_op jit(solution)/shard_map/all_to_all | solution.py:1055
  908.1 2.5 copy-start.1
  910.5 2.3 copy-start

commit v4 on v3

--- a/solution.py
+++ b/solution.py
@@ -28,9 +28,15 @@
         self.far = (self.m + 2) % 4
         self.farcore = (self.core + 2) % 4
         self.x_peer = self.b + 1 - 2 * self.inner
-        self.shifts = []
-        for d in range(1, self.n_out // 2 + 1):
-            self.shifts += [d] if 2 * d == self.n_out else [d, self.n_out - d]
+        self.line = self.n_out == 4
+        self.shifts = [2, 1, 3] if self.line else list(range(1, self.n_out))
+        self.is_mid = (self.outer + 1) // 2 == 1
+        self.is_end = (self.outer + 1) // 2 != 1
+        self.inward = 1 + 2 * (self.outer // 2)
+        self.outward = 3 - 2 * (self.outer // 2)
+        self.end = 3 * (self.outer // 2)
+        self.relay = 2 - self.outer // 3
+        self.opposite = 3 - self.outer
 
     def z_peer(self, s):
         return (self.outer + s) % self.n_out * 2 + self.inner
@@ -56,13 +62,16 @@
 
 
 class BatchGather:
-    def __init__(self, place, tensors, sems):
+    def __init__(self, place, tensors, sems, wides=(), wide_sems=None):
         self.p = place
         self.tensors = tensors
         self.z_send, self.z_recv, self.x_send, self.x_recv, self.own = sems
         self.started = 0
         self.events = [(t, s) for t in range(len(tensors)) for s in [0] + place.shifts]
         self.at = 0
+        self.wides = wides
+        self.wide_sems = wide_sems
+        self.steps = [step for c in range(len(wides)) for step in ((self.wide_z, c), (self.wide_relay, c))]
 
     @staticmethod
     def semaphores(n_out, count):
@@ -73,6 +82,11 @@
         src, block = self.tensors[t]
         return remote(src, block(self.p.b), self.z_send.at[t, s], self.z_recv.at[t, s],
                       batch=self.p.z_peer(s), mod=self.p.m)
+
+    def z_relay(self, t):
+        where = self.tensors[t][1]((self.p.outer + 2) % 4 * 2 + self.p.inner)
+        return remote(where, where, self.z_send.at[t, 0], self.z_recv.at[t, self.p.inward],
+                      batch=self.p.end * 2 + self.p.inner, mod=self.p.m)
 
     def own_copy(self, t):
         src, block = self.tensors[t]
@@ -84,22 +98,44 @@
         return remote(src if s == 0 else where, where, self.x_send.at[t, s], self.x_recv.at[t, s],
                       batch=self.p.x_peer, mod=self.p.m)
 
+    def straight(self, copy, act):
+        p = self.p
+        if not p.line:
+            for s in p.shifts:
+                act(copy(s))
+            return
+        act(copy(2))
+        act(copy(p.inward))
+
+        @pl.when(p.is_mid)
+        def _():
+            act(copy(p.outward))
+
     def start(self, count=1):
         for t in range(self.started, min(self.started + count, len(self.tensors))):
-            for s in self.p.shifts:
-                self.z_copy(t, s).start()
+            self.straight(lambda s: self.z_copy(t, s), lambda c: c.start())
             self.own_copy(t).start()
             self.started = t + 1
 
     def pump(self, upto):
+        p = self.p
         while self.at < len(self.events) and self.events[self.at][0] <= upto:
             t, s = self.events[self.at]
             if s:
                 self.z_copy(t, s).wait_recv()
-                if s == self.p.shifts[-1]:
+                if p.line and s == 2:
+
+                    @pl.when(p.is_mid)
+                    def _():
+                        self.z_relay(t).start()
+
+                if s == p.shifts[-1]:
                     self.start()
             self.x_copy(t, s).start()
             self.at += 1
+            if s == p.shifts[-1] and self.steps:
+                step, c = self.steps.pop(0)
+                step(c)
 
     def arrived(self, t, ahead=1):
         self.pump(t + ahead)
@@ -107,12 +143,64 @@
         for s in [0] + self.p.shifts:
             self.x_copy(t, s).wait_recv()
 
+    def wide_own(self, c):
+        shard, block, _ = self.wides[c]
+        return pltpu.make_async_copy(shard, block(self.p.b), self.wide_sems[2].at[c])
+
+    def wide_x(self, c):
+        shard, block, _ = self.wides[c]
+        return remote(shard, block(self.p.b), self.wide_sems[0].at[c, 0], self.wide_sems[1].at[c, 0],
+                      batch=self.p.x_peer, mod=self.p.m)
+
+    def wide_copy(self, c, s):
+        pair = self.wides[c][2](self.p.outer)
+        return remote(pair, pair, self.wide_sems[0].at[c, s], self.wide_sems[1].at[c, s],
+                      batch=self.p.z_peer(s), mod=self.p.m)
+
+    def wide_on(self, c):
+        pair = self.wides[c][2]((self.p.outer + 2) % 4)
+        return remote(pair, pair, self.wide_sems[0].at[c, self.p.n_out], self.wide_sems[1].at[c, self.p.inward],
+                      batch=self.p.end * 2 + self.p.inner, mod=self.p.m)
+
+    def wide_start(self):
+        for c in range(len(self.wides)):
+            self.wide_own(c).start()
+            self.wide_x(c).start()
+
+    def wide_z(self, c):
+        self.wide_own(c).wait()
+        self.wide_x(c).wait_recv()
+        self.straight(lambda s: self.wide_copy(c, s), lambda d: d.start())
+
+    def wide_relay(self, c):
+        if self.p.line:
+            self.wide_copy(c, 2).wait_recv()
+
+            @pl.when(self.p.is_mid)
+            def _():
+                self.wide_on(c).start()
+
     def sent(self):
+        p = self.p
+        for step, c in self.steps:
+            step(c)
         for t in range(len(self.tensors)):
-            for s in self.p.shifts:
-                self.z_copy(t, s).wait_send()
-            for s in [0] + self.p.shifts:
+            self.straight(lambda s: self.z_copy(t, s), lambda c: c.wait_send())
+            for s in [0] + p.shifts:
                 self.x_copy(t, s).wait_send()
+        for c in range(len(self.wides)):
+            self.wide_x(c).wait_send()
+            self.straight(lambda s: self.wide_copy(c, s), lambda d: d.wait_send())
+            for s in p.shifts[1:] if p.line else p.shifts:
+                self.wide_copy(c, s).wait_recv()
+        if p.line:
+
+            @pl.when(p.is_mid)
+            def _():
+                for t in range(len(self.tensors)):
+                    self.z_relay(t).wait_send()
+                for c in range(len(self.wides)):
+                    self.wide_on(c).wait_send()
 
 
 class ModGather:
@@ -324,6 +412,10 @@
         self.to_near = remote(self.ns, self.cn, send.at[2], recv.at[2], batch=place.b, mod=place.core)
 
     def send(self, part):
+        self.send_core(part)
+        self.send_far(part)
+
+    def send_core(self, part):
         p, step = self.p, self.step
         n = self.fs.shape[1] // step
 
@@ -332,15 +424,20 @@
 
         def second(k):
             self.ns[:, cols(k, step)] = part(p.core, k).astype(BF)
-
-        def third(k):
-            at = cols(k, step)
-            self.fs[:, at] = (part(p.far, k) + self.cf[:, at].astype(F32)).astype(BF)
 
         each(n, first)
         self.to_core.start()
         each(n, second)
         self.to_near.start()
+
+    def send_far(self, part):
+        p, step = self.p, self.step
+        n = self.fs.shape[1] // step
+
+        def third(k):
+            at = cols(k, step)
+            self.fs[:, at] = (part(p.far, k) + self.cf[:, at].astype(F32)).astype(BF)
+
         self.to_core.wait()
         each(n, third)
         self.to_far.start()
@@ -364,6 +461,18 @@
         return (shard.at[pl.ds(k * half, half)], lambda q: whole.at[pl.ds(q * rows + k * half, half)])
 
     return [piece(0), piece(1)]
+
+
+STRIP = 256
+
+
+def strip(shard, whole, rows, k):
+    at = pl.ds(k * STRIP, STRIP)
+    return (
+        shard.at[:, at],
+        lambda q: whole.at[pl.ds(q * rows, rows), at],
+        lambda o: whole.at[pl.ds(o * 2 * rows, 2 * rows), at],
+    )
 
 
 def forward_kernel(n_batch, *refs):
@@ -372,7 +481,7 @@
     (so_all, patch_w, ckv_all, cq_all, co_all, gu_all, down_all, act1_o, act2_o, act3_o, qkv_o, cqkv_o,
      ctx_o, cctx_o, lse_o, clse_o, pp_o, x1_o, x2_o, gate_o, up_o, h_o) = refs[13:35]
     (act, x, wq, wo, wp, pat, pp, qkv, ctx, lse, fs, ns, cf, yr, cn, wg, gate, gate_b, up, hid,
-     z_send, z_recv, x_send, x_recv, own, mod_send, mod_recv, sum_send, sum_recv, loc) = refs[35:]
+     z_send, z_recv, x_send, x_recv, own, mod_send, mod_recv, sum_send, sum_recv, loc, wide_send, wide_recv, wide_own) = refs[35:]
     p = Place(n_batch)
     local = Local(loc)
     rows, width = x.shape
@@ -389,16 +498,18 @@
             (w_co, lambda q: co_all.at[pl.ds(q * cq_r, cq_r)]),
         ]
         + halves(w_gu.at[0], gu_all.at[0], cq_r)
-        + halves(w_gu.at[1], gu_all.at[1], cq_r)
-        + halves(w_down, down_all, cq_r),
+        + halves(w_gu.at[1], gu_all.at[1], cq_r),
         (z_send, z_recv, x_send, x_recv, own),
+        [strip(w_down, down_all, cq_r, k) for k in range(w_down.shape[1] // STRIP)],
+        (wide_send, wide_recv, wide_own),
     )
-    SO, PATCH, CK, CV, CQ, CO, GATE, GATE2, UP, UP2, DOWN, DOWN2 = range(12)
+    SO, PATCH, CK, CV, CQ, CO, GATE, GATE2, UP, UP2 = range(10)
     load_act = local.go(text_all, act)
     load_q = local.go(qkv_w, wq)
     load_pat = local.go(patch_all, pat)
     p.greet()
     g.start()
+    g.wide_start()
     bufs = (fs, ns, cf, yr, cn)
     one = BranchSum(p, bufs, sum_send.at[0], sum_recv.at[0])
     two = BranchSum(p, bufs, sum_send.at[1], sum_recv.at[1])
@@ -557,8 +668,6 @@
     each(4, up_one)
     save_up = local.go(up, up_o)
     save_h = local.go(hid, h_o)
-    g.arrived(DOWN)
-    g.arrived(DOWN2)
     g.sent()
     for c in (save_act, save_x, save_gate, save_up, save_h, save_ctx, save_lse, save_qkv, save_pp):
         c.wait()
@@ -598,44 +707,145 @@
         ]
         + [pltpu.VMEM((rows, width), BF)] * 5
         + [pltpu.VMEM((width, f), BF), pltpu.VMEM((items, rows, f), F32), pltpu.VMEM((items, rows, f), BF), pltpu.VMEM((items, rows, f), BF), pltpu.VMEM((items, rows, f), BF)]
-        + BatchGather.semaphores(n_out, 12)
-        + [dma((3, 3)), dma((3, 3)), dma((2, 3)), dma((2, 3)), dma((32 + n_batch,))],
+        + BatchGather.semaphores(n_out, 10)
+        + [dma((3, 3)), dma((3, 3)), dma((2, 3)), dma((2, 3)), dma((32 + n_batch,)),
+           dma((f // STRIP, n_out + 1)), dma((f // STRIP, n_out)), dma((f // STRIP,))],
         compiler_params=pltpu.CompilerParams(collective_id=1, has_side_effects=True, vmem_limit_bytes=VMEM_LIMIT),
         cost_estimate=pl.CostEstimate(flops=35 * 10**9, bytes_accessed=600 * 10**6, transcendentals=0),
     )(text_all, patch_all, gains, patch_own, key_ok, cross_ok, qkv_w, w_so, w_ckv, w_cq, w_co, w_gu, w_down)
 
 
-class GradSum:
+class Line:
+    def z_copy(self, t, s):
+        p = self.p
+        return remote(self.block(t, (p.outer + s) % p.n_out), self.slot(t, s), self.z_send.at[t, s],
+                      self.z_recv.at[t, s], batch=p.z_peer(s), mod=p.m)
+
+    def to_relay(self, t):
+        p = self.p
+        return remote(self.block(t, p.opposite), self.slot(t, p.n_out), self.z_send.at[t, 0], self.z_recv.at[t, 0],
+                      batch=p.relay * 2 + p.inner, mod=p.m)
+
+    def to_end(self, t):
+        p = self.p
+        return remote(self.block(t, p.end), self.slot(t, p.outward), self.z_send.at[t, 0],
+                      self.z_recv.at[t, p.outward], batch=p.end * 2 + p.inner, mod=p.m)
+
+    def z_start(self, t):
+        p = self.p
+        if not self.line:
+            for s in p.shifts:
+                self.z_copy(t, s).start()
+            return
+        self.z_copy(t, 2).start()
+        self.z_copy(t, p.inward).start()
+
+        @pl.when(p.is_end)
+        def _():
+            self.to_relay(t).start()
+
+    def z_relay(self, t):
+        p = self.p
+        if not self.line:
+            return
+
+        @pl.when(p.is_mid)
+        def _():
+            self.to_relay(t).wait_recv()
+            a, b = self.views(t)
+            self.fetch((self.block(t, p.end), a), (self.slot(t, p.n_out), b))
+            self.add(a, b)
+            self.fetch((a, self.block(t, p.end)))
+            self.to_end(t).start()
+
+    def fetch(self, *pairs):
+        copies = [pltpu.make_async_copy(a, b, self.loc.at[k]) for k, (a, b) in enumerate(pairs)]
+        for copy in copies:
+            copy.start()
+        for copy in copies:
+            copy.wait()
+
+    def add(self, a, *others):
+        lead, rows, width = a.shape
+        step = 16
+        while rows % (2 * step) == 0 and step * width < 16384:
+            step *= 2
+
+        def body(o):
+            def one(r):
+                total = a[o, r, :].astype(F32)
+                for b in others:
+                    total = total + b[o, r, :].astype(F32)
+                a[o, r, :] = total.astype(BF)
+
+            each_rows(rows, one, step)
+
+        each(lead, body)
+
+    def z_arrived(self, t):
+        p = self.p
+        if not self.line:
+            for s in p.shifts:
+                self.z_copy(t, s).wait_recv()
+            return
+        self.z_copy(t, 2).wait_recv()
+        self.z_copy(t, self.first_slot()).wait_recv()
+
+        @pl.when(p.is_mid)
+        def _():
+            self.z_copy(t, 3).wait_recv()
+
+    def first_slot(self):
+        return 3 - 2 * ((self.p.outer + 2) // 3)
+
+    def z_sent(self, t):
+        p = self.p
+        if not self.line:
+            for s in p.shifts:
+                self.z_copy(t, s).wait_send()
+            return
+        self.z_copy(t, 2).wait_send()
+        self.z_copy(t, p.inward).wait_send()
+        self.to_relay(t).wait_send()
+
+
+class GradSum(Line):
     def __init__(self, place, pieces, mine, got, sems, loc):
         self.p = place
         self.pieces = pieces
         self.mine, self.got = mine, got
         self.x_send, self.x_recv, self.z_send, self.z_recv = sems
         self.loc = loc
+        self.line = place.line
         self.ready = self.started = self.done = 0
-        self.window = 1
+        self.window = 2
 
     @staticmethod
     def semaphores(n_out, count):
         dma = pltpu.SemaphoreType.DMA
         return [dma((count,)), dma((count,)), dma((count, n_out)), dma((count, n_out))]
 
+    def block(self, t, o):
+        return self.pieces[t][1].at[pl.ds(o, 1)]
+
+    def slot(self, t, s):
+        return self.pieces[t][2].at[pl.ds(s, 1)]
+
+    def views(self, t):
+        _, rows, width = self.pieces[t][1].shape
+        return [v.at[pl.ds(0, 1), pl.ds(0, rows), pl.ds(0, width)] for v in (self.mine, self.got)]
+
     def x_copy(self, t):
         whole, from_x, _ = self.pieces[t]
         return remote(whole.at[:, 1 - self.p.inner], from_x, self.x_send.at[t], self.x_recv.at[t],
                       batch=self.p.x_peer, mod=self.p.m)
 
-    def z_copy(self, t, s):
-        _, from_x, from_z = self.pieces[t]
-        return remote(from_x.at[(self.p.outer + s) % self.p.n_out], from_z.at[s], self.z_send.at[t, s],
-                      self.z_recv.at[t, s], batch=self.p.z_peer(s), mod=self.p.m)
-
     def kick(self):
         while self.started < self.ready and self.started - self.done < self.window:
             self.x_copy(self.started).start()
             self.started += 1
 
-    def add(self):
+    def advance(self):
         self.ready += 1
         self.kick()
 
@@ -649,36 +859,21 @@
             self.kick()
             mine = self.mine.at[:, pl.ds(0, rows), pl.ds(0, width)]
             got = self.got.at[:, pl.ds(0, rows), pl.ds(0, width)]
-            one = pltpu.make_async_copy(whole.at[:, self.p.inner], mine, self.loc.at[0])
-            two = pltpu.make_async_copy(from_x, got, self.loc.at[1])
-            one.start()
-            two.start()
-            one.wait()
-            two.wait()
-            step = 16
-
-            def body(o):
-                def add(r):
-                    mine[o, r, :] = (mine[o, r, :].astype(F32) + got[o, r, :].astype(F32)).astype(BF)
-
-                each_rows(rows, add, step)
-
-            each(n_out, body)
-            one = pltpu.make_async_copy(mine, from_x, self.loc.at[0])
-            two = pltpu.make_async_copy(mine.at[self.p.outer], from_z.at[0], self.loc.at[1])
-            one.start()
-            two.start()
-            one.wait()
-            for s in self.p.shifts:
-                self.z_copy(t, s).start()
-            two.wait()
+            self.fetch((whole.at[:, self.p.inner], mine), (from_x, got))
+            self.add(mine, got)
+            self.fetch((mine, from_x), (mine.at[self.p.outer], from_z.at[0]))
+            self.z_start(t)
+            if t:
+                self.z_relay(t - 1)
 
     def finish(self):
+        last = len(self.pieces) - 1
         self.pump(len(self.pieces))
+        self.z_relay(last)
         for t in range(len(self.pieces)):
             self.x_copy(t).wait_send()
-            for s in self.p.shifts:
-                self.z_copy(t, s).wait()
+            self.z_arrived(t)
+            self.z_sent(t)
 
 
 def attend_back(q_ref, k_ref, v_ref, do_ref, lse_ref, dq_ref, dk_ref, dv_ref, j, allowed, heads):
@@ -718,7 +913,9 @@
     half = f // 2
     n_out, blk = p.n_out, width // n_batch
     heads = c // HD
-    pieces = [(whole_f.at[k], from_x_f.at[k], from_z_f.at[k]) for k in range(6)]
+    pieces = [
+        (whole_f.at[k], from_x_f.at[k], from_z_f.at[k // 2, :, :, pl.ds(k % 2 * half, half)]) for k in range(6)
+    ]
     pieces += [(whole_c.at[k], from_x_c.at[k], from_z_c.at[k]) for k in range(8)]
     pieces.append((whole_p, from_x_p, from_z_p))
     gs = GradSum(p, pieces, mine, got, (gx_send, gx_recv, gz_send, gz_recv), loc2)
@@ -760,7 +957,7 @@
         copy = pltpu.make_async_copy(st.at[:, :, pl.ds(0, used), pl.ds(0, count)], whole, loc2.at[2])
         copy.start()
         copy.wait()
-        gs.add()
+        gs.advance()
 
     def norm_back(k, total, v_rows):
         def body(r):
@@ -782,15 +979,6 @@
     piece(dy, hid, 0, half)
     piece(dy, hid, half, half)
     load_w0.wait()
-    load_v.wait()
-    out_part = lambda j, k: mm_nt(hid[j], w0[cols(k, 512), :])
-    sums[0].send(out_part)
-
-    def result_own(k):
-        at = cols(k, 512)
-        da[:, at] = v[:, at] + out_part(p.m, k)
-
-    each(width // 512, result_own)
     load_gate.wait()
     load_up.wait()
 
@@ -798,24 +986,15 @@
         dh = mm(dy[j], w0[...])
         value, slope = gelu_parts(gate[j].astype(F32))
         gate[j] = (dh * up[j].astype(F32) * slope).astype(BF)
-        hid[j] = (dh * value).astype(BF)
+        up[j] = (dh * value).astype(BF)
 
     each(items, mix_back)
     load_w0 = local.go(gu_all.at[1], w0)
-    gs.pump()
-    sums[0].receive()
-
-    def result_done(r):
-        da[r, :] += sums[0].others(r)
-
-    each_rows(rows, result_done)
-    save_result = local.go(da, result)
-    sums[0].sent()
     load_w1.wait()
     load_w0.wait()
-    act_part = lambda j, k: mm_nt(gate[j], w1[cols(k, 512), :]) + mm_nt(hid[j], w0[cols(k, 512), :])
+    act_part = lambda j, k: mm_nt(gate[j], w1[cols(k, 512), :]) + mm_nt(up[j], w0[cols(k, 512), :])
     sums[1].send(act_part)
-    save_result.wait()
+    gs.pump()
 
     def own_part(part):
         def body(k):
@@ -830,14 +1009,15 @@
     load_a.wait()
     piece(act_a, gate, 0, half)
     piece(act_a, gate, half, half)
+    piece(act_a, up, 0, half)
     gs.pump()
+    load_v.wait()
     sums[1].receive()
     norm_back(2, sums[1], lambda r: v[r, :])
     gathers[0].start()
     sums[1].sent()
     load_v = local.go(x1_i, v)
-    piece(act_a, hid, 0, half)
-    piece(act_a, hid, half, half)
+    piece(act_a, up, half, half)
     load_a = local.go(pp_i, act_a)
     gs.pump()
     gathers[0].forward()
@@ -868,24 +1048,25 @@
     load_b = local.go(act1, act_b)
     load_a.wait()
     piece(act_a, dqkv.at[1], 0, c)
+    piece(act_a, dqkv.at[2], 0, c)
+    load_a = local.go(pat_all, act_a)
     load_v.wait()
     sums[2].receive()
     norm_back(1, sums[2], lambda r: v[r, :])
     gathers[1].start()
     sums[2].sent()
-    piece(act_a, dqkv.at[2], 0, c)
-    load_a = local.go(pat_all, act_a)
+    load_v = local.go(x2_i, v)
     gs.pump()
+    proj_part = lambda j, k: mm_nt(dqkv[1, k], w1[cols(j, c), left]) + mm_nt(dqkv[2, k], w1[cols(j, c), right])
+    sums[3].send_core(proj_part)
+
+    def proj_own(k):
+        dpp[k] = proj_part(p.m, k).astype(BF)
+
+    each(items, proj_own)
     gathers[1].forward()
     gathers[1].finish()
-
-    proj_part = lambda j, k: mm_nt(dqkv[1, k], w1[cols(j, c), left]) + mm_nt(dqkv[2, k], w1[cols(j, c), right])
-    sums[3].send(proj_part)
-
-    def proj_own(k):
-        dpp[k] = proj_part(p.m, k).astype(BF)
-
-    each(items, proj_own)
+    sums[3].send_far(proj_part)
     load_w1 = [local.go(qkv_w.at[1], w1.at[:, left]), local.go(qkv_w.at[2], w1.at[:, right])]
 
     for copy in load_w0 + load_s:
@@ -899,6 +1080,9 @@
         attend_back(qkv.at[0], qkv.at[1], qkv.at[2], dctx, lse, dqkv.at[0], dqkv.at[1], dqkv.at[2], j, ok, heads)
 
     each(items, self_back)
+    load_b.wait()
+    for k in range(3):
+        piece(act_b, dqkv.at[k], 0, c)
     gs.pump()
     sums[3].receive()
 
@@ -917,10 +1101,8 @@
     )
     sums[4].send(self_part)
     own_part(self_part)
+    load_w0 = local.go(down_all, w0)
     gs.pump()
-    load_b.wait()
-    for k in range(3):
-        piece(act_b, dqkv.at[k], 0, c)
     load_a.wait()
     piece(act_a, dpp, 0, c)
     gs.pump()
@@ -935,13 +1117,31 @@
     ]
     for copy in mod_g:
         copy.start()
+    load_w0.wait()
+    out_part = lambda j, k: mm_nt(hid[j], w0[cols(k, 512), :])
+    sums[0].send(out_part)
     gs.pump()
+    load_v.wait()
+
+    def result_own(k):
+        at = cols(k, 512)
+        da[:, at] = v[:, at] + out_part(p.m, k)
+
+    each(width // 512, result_own)
     for copy in mod_g:
         copy.wait()
     dg[...] += dgm[0] + dgm[1] + dgm[2]
     across = remote(dg, dgx, gx.at[0], gx.at[1], batch=p.x_peer, mod=p.m)
     across.start()
     gs.pump()
+    sums[0].receive()
+
+    def result_done(r):
+        da[r, :] += sums[0].others(r)
+
+    each_rows(rows, result_done)
+    save_result = local.go(da, result)
+    sums[0].sent()
     across.wait()
     dg[...] += dgx[...]
     along = [
@@ -958,6 +1158,7 @@
         total = total + dgz[s]
     gain_out[...] = total
     gs.finish()
+    save_result.wait()
     save_text.wait()
 
 
@@ -976,12 +1177,12 @@
 
     def bufs(count, r, w):
         lead = (count,) if count else ()
-        return [sds(lead + (n_out, 2, r, w), BF), sds(lead + (n_out, r, w), BF), sds(lead + (n_out, r, w), BF)]
+        return [sds(lead + (n_out, 2, r, w), BF), sds(lead + (n_out, r, w), BF), sds(lead + (n_out + 1, r, w), BF)]
 
     return pl.pallas_call(
         functools.partial(backward_kernel, n_batch),
         out_shape=[sds((rows, width), F32), sds((rows, width), F32), sds((8, width), F32)]
-        + bufs(6, blk, f // 2) + bufs(8, blk, c) + bufs(0, patch_rows, c),
+        + bufs(6, blk, f // 2)[:2] + [sds((3, n_out + 1, blk, f), BF)] + bufs(8, blk, c) + bufs(0, patch_rows, c),
         in_specs=[any_, vmem, any_, vmem, vmem, vmem] + [any_] * 22,
         out_specs=[any_, any_, vmem] + [any_] * 9,
         scratch_shapes=[V(big)] * 3
@@ -996,7 +1197,7 @@
         + [V((8, width), F32), V((3, 8, width), F32), V((8, width), F32), V((n_out, 8, width), F32)]
         + GradSum.semaphores(n_out, 15)
         + [dma((2, 3)), dma((2, 3)), dma((5, 3)), dma((5, 3)), dma((3 + n_out,)), dma((3 + n_out,)), dma((2,)),
-           dma((48,)), dma((3,))],
+           dma((48,)), dma((4,))],
         compiler_params=pltpu.CompilerParams(collective_id=2, has_side_effects=True, vmem_limit_bytes=VMEM_LIMIT),
         cost_estimate=pl.CostEstimate(flops=75 * 10**9, bytes_accessed=800 * 10**6, transcendentals=0),
     )(*inputs)
@@ -1045,11 +1246,15 @@
     at = lax.axis_index("batch") * blk + mod * gw
     d_gains = lax.dynamic_slice(gain_sum, (0, at), (3, gw))
 
+    n_out = nb // 2
+    outer = lax.axis_index("batch") // 2
+    slots = jnp.arange(n_out)
+    missing = (((outer == 0) & (slots == 1)) | ((outer == 3) & (slots == 3))) & (n_out == 4)
+
     def total(parts, axis=0):
-        return jnp.sum(parts.astype(F32), axis=axis)
-
-    def pair(k):
-        return jnp.concatenate([total(sum_f[k]), total(sum_f[k + 1])], axis=1)
+        parts = lax.slice_in_dim(parts, 0, n_out, axis=axis)
+        gone = missing.reshape((1,) * axis + (n_out,) + (1,) * (parts.ndim - axis - 1))
+        return jnp.sum(jnp.where(gone, 0.0, parts.astype(F32)), axis=axis)
 
     grad_patch = total(sum_p)[:block].reshape(n_mod, pr, col_w)
     grad_patch = lax.all_to_all(grad_patch, "mod", 0, 0, tiled=True)
@@ -1064,8 +1269,8 @@
         total(sum_c[2:4], 1),
         total(sum_c[0]).T,
         grad_patch,
-        jnp.stack([pair(2), pair(4)]),
-        pair(0).T,
+        total(sum_f[1:], 1),
+        total(sum_f[0]).T,
     )
 
 

time: 924 us -> 873 us (0.945)
  Pallas kernels: 865 us -> 814 us
    pallas_call x1, Pallas kernels: 333 us -> 297 us  [forward_call(): pl.pallas_call(functools.partial(forward_kernel, n_batch), out_shape=[sds...]
    pallas_call x1, Pallas kernels: 440 us -> 425 us  [backward_call(): pl.pallas_call(functools.partial(backward_kernel, n_batch), out_shape=[sd...]
where the time goes in v4:
time: 873 us; the launch traced here: 861 us
  Pallas kernels  814 us (93%)
  other arithmetic  20.3 us (2%)
  local copies, waits for them, and re-layouts  19.4 us (2%)
    pallas_call x1, Pallas kernels, backward_call(): pl.pallas_call(functools.partial(backward_kernel, n_batch), out_shape=[sd...  425 us
    pallas_call x1, Pallas kernels, forward_call(): pl.pallas_call(functools.partial(forward_kernel, n_batch), out_shape=[sds...  297 us
    pallas_call x1, Pallas kernels, first_call(): pl.pallas_call(functools.partial(first_kernel, n_batch), out_shape=[jax.S...  92.4 us
  transfers between devices with their start and end apart: 1, of which 0 were waited for; matrix products, arithmetic and copies ran while one was open for 2% of the time, Pallas kernels for 0%

profile of v4, /device:TPU:0, one launch (start us, length us, event | category | flops | bytes accessed | tf_op | source)
XLA Modules:
  0.0 860.9 jit_solution(16639065286324663659)
XLA Ops:
  0.7 0.7 fusion.4
  1.4 1.2 dynamic_slice.6
  2.6 0.6 compare_convert_fusion.1
  3.3 0.7 compare_convert_fusion
  4.0 1.0 pad.9
  4.9 0.7 copy.43
  5.7 0.0 copy-start.4
  5.7 1.5 copy.32
  7.2 0.1 pad.8
  7.3 1.4 copy.39.patches
  8.7 0.0 copy-done.4
  8.7 0.3 dynamic_update_slice.3.gain_tile
  9.0 0.0 copy-start.3
  9.0 0.8 broadcast_in_dim.111.valid
  9.8 0.0 copy-done.3
  9.8 92.4 %shard_map.221 = (bf16[4,256,2048]{2,1,0:T(8,128)(2,1)}, bf16[4,256,2048]{2,1,0:T(8,128)(2,1)}, bf16[8,16,256]{2,1,0:T(8,128)(2,1)}, bf16[4,64,512]{2,1,0:T(8,12...) custom-call(bf16[256,2048]{1,0:T(8,128)(2,1)} %bitcast.47, ...), custom_call_target="tpu_custom_call" | custom-call | flops 1000000 | bytes 300000000 | tf_op jit(solution)/shard_map/pallas_call | solution.py:309
  102.2 1.4 slice_convert_fusion
  103.6 1.0 slice.49
  104.6 0.7 reshape.109.refs_3_
  105.3 0.6 broadcast_in_dim.112.refs_4_
  105.9 0.6 broadcast_in_dim.113.refs_5_
  106.6 296.7 %shard_map.222 = (bf16[2048,512]{1,0:T(8,128)(2,1)}, bf16[1664,512]{1,0:T(8,128)(2,1)}, bf16[2,2048,512]{2,1,0:T(8,128)(2,1)}, bf16[2048,512]{1,0:T(8,128)(2,1)}...) custom-call(bf16[4,256,2048]{2,1,0:T(8,128)(2,1)} %get-tuple-element, ...), custom_call_target="tpu_custom_call" | custom-call | flops 35000000512 | bytes 600000000 | tf_op jit(solution)/shard_map/pallas_call | solution.py:688
  403.3 425.3 %shard_map.223 = (f32[256,2048]{1,0:T(8,128)}, f32[256,2048]{1,0:T(8,128)}, f32[8,2048]{1,0:T(8,128)}, bf16[6,4,2,256,640]{4,3,2,1,0:T(8,128)(2,1)}, bf16[6,4,25...) custom-call(bf16[4,256,2048]{2,1,0:T(8,128)(2,1)} %get-tuple-element, ...), custom_call_target="tpu_custom_call" | custom-call | flops 74999996416 | bytes 800000000 | tf_op jit(solution)/shard_map/pallas_call | solution.py:1182
  828.5 1.4 select_reduce_fusion.3
  830.0 0.8 reshape.110
  830.8 5.5 all-to-all-start
  836.3 0.0 copy-start
  836.4 2.6 fusion
  839.0 6.0 select_reduce_fusion
  845.0 0.0 copy-done
  845.0 1.9 select_reduce_fusion.1
  846.9 1.5 fusion.1
  848.4 1.3 constant_dynamic-slice_fusion
  849.8 1.5 copy.38
  851.2 1.0 copy.37
  852.2 1.0 copy.36
  853.2 0.0 copy-start.2
  853.2 3.3 select_reduce_fusion.2
  856.5 0.0 all-to-all-done
  856.5 0.3 copy.35
  856.8 0.1 pad.10
  856.9 0.0 copy-start.1
  856.9 0.9 copy.41
  857.8 0.0 copy-done.2
  857.8 1.3 copy.47
  859.1 0.0 copy-done.1
  859.1 1.3 copy.48
  (2 shorter events, 0.0 us)
Async XLA Ops:
  5.7 3.1 copy-start.4
  9.0 0.8 copy-start.3
  830.8 25.7 %all-to-all-start = ((f32[4,52,512]{2,1,0:T(8,128)}), f32[4,52,512]{2,1,0:T(8,128)S(1)}, u32[]{:S(2)}, u32[]{:S(2)}) async-start(f32[4,52,512]{2,1,0:T(8,128)} %reshape.110), calls=%async_computation | async-start | bytes 917504 | tf_op jit(solution)/shard_map/all_to_all | solution.py:1260
  836.3 8.7 %copy-start = (bf16[8,5,256,512]{3,2,1,0:T(8,128)(2,1)S(1)}, bf16[8,5,256,512]{3,2,1,0:T(8,128)(2,1)}, u32[]{:S(2)}) copy-start(bf16[8,5,256,512]{3,2,1,0:T(8,128)(2,1)} %get-tuple-element.80) | copy-start | bytes 31457284
  853.2 4.6 copy-start.2
  856.9 2.2 copy-start.1

commit v5 on v4

--- a/solution.py
+++ b/solution.py
@@ -62,12 +62,13 @@
 
 
 class BatchGather:
-    def __init__(self, place, tensors, sems, wides=(), wide_sems=None):
+    def __init__(self, place, tensors, sems, wides=(), wide_sems=None, early=()):
         self.p = place
         self.tensors = tensors
         self.z_send, self.z_recv, self.x_send, self.x_recv, self.own = sems
         self.started = 0
-        self.events = [(t, s) for t in range(len(tensors)) for s in [0] + place.shifts]
+        self.early = early
+        self.events = [(t, s) for t in range(len(tensors)) for s in [0] + place.shifts if s or t not in early]
         self.at = 0
         self.wides = wides
         self.wide_sems = wide_sems
@@ -161,6 +162,10 @@
         pair = self.wides[c][2]((self.p.outer + 2) % 4)
         return remote(pair, pair, self.wide_sems[0].at[c, self.p.n_out], self.wide_sems[1].at[c, self.p.inward],
                       batch=self.p.end * 2 + self.p.inner, mod=self.p.m)
+
+    def early_start(self):
+        for t in self.early:
+            self.x_copy(t, 0).start()
 
     def wide_start(self):
         for c in range(len(self.wides)):
@@ -240,7 +245,7 @@
         (gain_sum, lambda q: gain_all.at[q]),
         (w_qkv.at[2], lambda q: qkv_all.at[2, pl.ds(q * rows, rows)]),
     ]
-    g = BatchGather(p, tensors, (z_send, z_recv, x_send, x_recv, own))
+    g = BatchGather(p, tensors, (z_send, z_recv, x_send, x_recv, own), early=(0, 1, 3))
     copies = [
         pltpu.make_async_copy(text, text_all.at[p.m], misc.at[0]),
         pltpu.make_async_copy(patches, patch_all.at[p.m], misc.at[1]),
@@ -263,6 +268,7 @@
     for c in gains:
         c.start()
     g.start()
+    g.early_start()
     for c in copies:
         c.wait()
     text_g = ModGather(p, lambda j: text_all.at[j], mod_send.at[0], mod_recv.at[0])
@@ -282,12 +288,10 @@
     so_t[...] = w_so[...].T
     co_t[...] = w_co[...].T
     down_t[...] = w_down[...].T
-    g.pump(0)
+    dy_g.start()
+    g.pump(3)
     text_g.forward()
-    dy_g.start()
-    g.pump(1)
     patch_g.forward()
-    g.pump(3)
     dy_g.forward()
     for t in range(4):
         g.arrived(t)
@@ -455,10 +459,11 @@
 
 
 def halves(shard, whole, rows):
-    half = rows // 2
+    half = shard.shape[1] // 2
 
     def piece(k):
-        return (shard.at[pl.ds(k * half, half)], lambda q: whole.at[pl.ds(q * rows + k * half, half)])
+        at = pl.ds(k * half, half)
+        return (shard.at[:, at], lambda q: whole.at[pl.ds(q * rows, rows), at])
 
     return [piece(0), piece(1)]
 
@@ -644,28 +649,33 @@
     a3_g.finish()
     save_act = local.go(act, act3_o)
 
-    g.arrived(GATE)
-    g.arrived(GATE2)
-    load_g = local.go(gu_all.at[0], wg)
-    load_g.wait()
-
-    def gate_one(j):
-        gate[j] = mm(act[j], wg[...])
-        gate_b[j] = gate[j].astype(BF)
-
-    each(4, gate_one)
+    half = wg.shape[1] // 2
+    low, high = pl.ds(0, half), pl.ds(half, half)
+
+    def gate_half(at):
+        def body(j):
+            value = mm(act[j], wg[:, at])
+            gate[j, :, at] = value
+            gate_b[j, :, at] = value.astype(BF)
+
+        each(4, body)
+
+    def up_half(at):
+        def body(j):
+            u = mm(act[j], wg[:, at])
+            up[j, :, at] = u.astype(BF)
+            hid[j, :, at] = (jax.nn.gelu(gate[j, :, at], approximate=True) * u).astype(BF)
+
+        each(4, body)
+
+    for t, k, at, compute in (
+        (GATE, 0, low, gate_half), (GATE2, 0, high, gate_half), (UP, 1, low, up_half), (UP2, 1, high, up_half)
+    ):
+        g.arrived(t)
+        load_g = local.go(gu_all.at[k, :, at], wg.at[:, at])
+        load_g.wait()
+        compute(at)
     save_gate = local.go(gate_b, gate_o)
-    g.arrived(UP)
-    g.arrived(UP2)
-    load_g = local.go(gu_all.at[1], wg)
-    load_g.wait()
-
-    def up_one(j):
-        u = mm(act[j], wg[...])
-        up[j] = u.astype(BF)
-        hid[j] = (jax.nn.gelu(gate[j], approximate=True) * u).astype(BF)
-
-    each(4, up_one)
     save_up = local.go(up, up_o)
     save_h = local.go(hid, h_o)
     g.sent()

time: 873 us -> 866 us (level)
  no operation moved by 1% of the time
where the time goes in v5:
time: 866 us; the launch traced here: 854 us
  Pallas kernels  809 us (93%)
  other arithmetic  20.3 us (2%)
  local copies, waits for them, and re-layouts  19.4 us (2%)
    pallas_call x1, Pallas kernels, backward_call(): pl.pallas_call(functools.partial(backward_kernel, n_batch), out_shape=[sd...  421 us
    pallas_call x1, Pallas kernels, forward_call(): pl.pallas_call(functools.partial(forward_kernel, n_batch), out_shape=[sds...  303 us
    pallas_call x1, Pallas kernels, first_call(): pl.pallas_call(functools.partial(first_kernel, n_batch), out_shape=[jax.S...  85.8 us
  transfers between devices with their start and end apart: 1, of which 0 were waited for; matrix products, arithmetic and copies ran while one was open for 2% of the time, Pallas kernels for 0%

profile of v5, /device:TPU:0, one launch (start us, length us, event | category | flops | bytes accessed | tf_op | source)
XLA Modules:
  0.0 853.7 jit_solution(13301385992399216293)
XLA Ops:
  0.7 0.7 fusion.4
  1.4 1.2 dynamic_slice.6
  2.6 0.6 compare_convert_fusion.1
  3.3 0.7 compare_convert_fusion
  4.0 1.0 pad.9
  4.9 0.7 copy.43
  5.7 0.0 copy-start.4
  5.7 1.5 copy.32
  7.2 0.1 pad.8
  7.3 1.4 copy.39.patches
  8.7 0.0 copy-done.4
  8.7 0.3 dynamic_update_slice.3.gain_tile
  9.0 0.0 copy-start.3
  9.0 0.8 broadcast_in_dim.111.valid
  9.8 0.0 copy-done.3
  9.8 85.8 %shard_map.221 = (bf16[4,256,2048]{2,1,0:T(8,128)(2,1)}, bf16[4,256,2048]{2,1,0:T(8,128)(2,1)}, bf16[8,16,256]{2,1,0:T(8,128)(2,1)}, bf16[4,64,512]{2,1,0:T(8,12...) custom-call(bf16[256,2048]{1,0:T(8,128)(2,1)} %bitcast.47, ...), custom_call_target="tpu_custom_call" | custom-call | flops 1000000 | bytes 300000000 | tf_op jit(solution)/shard_map/pallas_call | solution.py:313
  95.5 1.4 slice_convert_fusion
  96.9 1.0 slice.49
  97.9 0.7 reshape.109.refs_3_
  98.6 0.6 broadcast_in_dim.112.refs_4_
  99.3 0.6 broadcast_in_dim.113.refs_5_
  99.9 302.7 %shard_map.222 = (bf16[2048,512]{1,0:T(8,128)(2,1)}, bf16[1664,512]{1,0:T(8,128)(2,1)}, bf16[2,2048,512]{2,1,0:T(8,128)(2,1)}, bf16[2048,512]{1,0:T(8,128)(2,1)}...) custom-call(bf16[4,256,2048]{2,1,0:T(8,128)(2,1)} %get-tuple-element, ...), custom_call_target="tpu_custom_call" | custom-call | flops 35000000512 | bytes 600000000 | tf_op jit(solution)/shard_map/pallas_call | solution.py:698
  402.5 420.9 %shard_map.223 = (f32[256,2048]{1,0:T(8,128)}, f32[256,2048]{1,0:T(8,128)}, f32[8,2048]{1,0:T(8,128)}, bf16[6,4,2,256,640]{4,3,2,1,0:T(8,128)(2,1)}, bf16[6,4,25...) custom-call(bf16[4,256,2048]{2,1,0:T(8,128)(2,1)} %get-tuple-element, ...), custom_call_target="tpu_custom_call" | custom-call | flops 74999996416 | bytes 800000000 | tf_op jit(solution)/shard_map/pallas_call | solution.py:1192
  823.4 1.4 select_reduce_fusion.3
  824.9 0.8 reshape.110
  825.7 3.5 all-to-all-start
  829.2 0.0 copy-start
  829.2 2.6 fusion
  831.8 6.0 select_reduce_fusion
  837.8 0.0 copy-done
  837.8 1.9 select_reduce_fusion.1
  839.7 1.5 fusion.1
  841.3 1.3 constant_dynamic-slice_fusion
  842.6 1.5 copy.38
  844.1 1.0 copy.37
  845.1 1.0 copy.36
  846.0 0.0 copy-start.2
  846.0 3.3 select_reduce_fusion.2
  849.4 0.0 all-to-all-done
  849.4 0.3 copy.35
  849.6 0.1 pad.10
  849.7 0.0 copy-start.1
  849.7 0.9 copy.41
  850.6 0.0 copy-done.2
  850.6 1.3 copy.47
  852.0 0.0 copy-done.1
  852.0 1.3 copy.48
  (2 shorter events, 0.0 us)
Async XLA Ops:
  5.7 3.1 copy-start.4
  9.0 0.8 copy-start.3
  825.7 23.7 %all-to-all-start = ((f32[4,52,512]{2,1,0:T(8,128)}), f32[4,52,512]{2,1,0:T(8,128)S(1)}, u32[]{:S(2)}, u32[]{:S(2)}) async-start(f32[4,52,512]{2,1,0:T(8,128)} %reshape.110), calls=%async_computation | async-start | bytes 917504 | tf_op jit(solution)/shard_map/all_to_all | solution.py:1270
  829.2 8.7 %copy-start = (bf16[8,5,256,512]{3,2,1,0:T(8,128)(2,1)S(1)}, bf16[8,5,256,512]{3,2,1,0:T(8,128)(2,1)}, u32[]{:S(2)}) copy-start(bf16[8,5,256,512]{3,2,1,0:T(8,128)(2,1)} %get-tuple-element.80) | copy-start | bytes 31457284
  846.0 4.6 copy-start.2
  849.7 2.2 copy-start.1

commit v6 on v5

--- a/solution.py
+++ b/solution.py
@@ -934,13 +934,6 @@
 
     load_dy = local.go(dy_all, dy)
     load_h = local.go(h_i, hid)
-    load_w0 = local.go(down_all, w0)
-    load_v = local.go(x2_i, v)
-    load_gate = local.go(gate_i, gate)
-    load_up = local.go(up_i, up)
-    load_w1 = local.go(gu_all.at[0], w1)
-    load_a = local.go(act3, act_a)
-    load_b = local.go(act2, act_b)
     p.greet()
     set_a = (fs, ns, cf, yr, cn)
     set_b = (fs, ns, cf2, yr2, cn2)
@@ -985,8 +978,15 @@
 
     load_dy.wait()
     load_h.wait()
+    load_w0 = local.go(down_all, w0)
+    load_v = local.go(x2_i, v)
+    load_gate = local.go(gate_i, gate)
+    load_up = local.go(up_i, up)
+    load_w1 = local.go(gu_all.at[0], w1)
+    load_a = local.go(act3, act_a)
+    load_b = local.go(act2, act_b)
+    piece(dy, hid, 0, half)
     g[...] = dy[p.m].astype(F32)
-    piece(dy, hid, 0, half)
     piece(dy, hid, half, half)
     load_w0.wait()
     load_gate.wait()

time: 866 us -> 866 us (level)
  no operation moved by 1% of the time
where the time goes in v6:
time: 866 us; the launch traced here: 854 us
  Pallas kernels  809 us (93%)
  other arithmetic  20.3 us (2%)
  local copies, waits for them, and re-layouts  19.4 us (2%)
    pallas_call x1, Pallas kernels, backward_call(): pl.pallas_call(functools.partial(backward_kernel, n_batch), out_shape=[sd...  421 us
    pallas_call x1, Pallas kernels, forward_call(): pl.pallas_call(functools.partial(forward_kernel, n_batch), out_shape=[sds...  303 us
    pallas_call x1, Pallas kernels, first_call(): pl.pallas_call(functools.partial(first_kernel, n_batch), out_shape=[jax.S...  85.8 us
  transfers between devices with their start and end apart: 1, of which 0 were waited for; matrix products, arithmetic and copies ran while one was open for 2% of the time, Pallas kernels for 0%

profile of v6, /device:TPU:0, one launch (start us, length us, event | category | flops | bytes accessed | tf_op | source)
XLA Modules:
  0.0 853.6 jit_solution(14285075352001894817)
XLA Ops:
  0.7 0.7 fusion.4
  1.4 1.2 dynamic_slice.6
  2.6 0.6 compare_convert_fusion.1
  3.3 0.7 compare_convert_fusion
  4.0 1.0 pad.9
  4.9 0.7 copy.43
  5.7 0.0 copy-start.4
  5.7 1.5 copy.32
  7.2 0.1 pad.8
  7.3 1.4 copy.39.patches
  8.7 0.0 copy-done.4
  8.7 0.3 dynamic_update_slice.3.gain_tile
  9.0 0.0 copy-start.3
  9.0 0.8 broadcast_in_dim.111.valid
  9.8 0.0 copy-done.3
  9.8 85.8 %shard_map.221 = (bf16[4,256,2048]{2,1,0:T(8,128)(2,1)}, bf16[4,256,2048]{2,1,0:T(8,128)(2,1)}, bf16[8,16,256]{2,1,0:T(8,128)(2,1)}, bf16[4,64,512]{2,1,0:T(8,12...) custom-call(bf16[256,2048]{1,0:T(8,128)(2,1)} %bitcast.47, ...), custom_call_target="tpu_custom_call" | custom-call | flops 1000000 | bytes 300000000 | tf_op jit(solution)/shard_map/pallas_call | solution.py:313
  95.5 1.4 slice_convert_fusion
  96.9 1.0 slice.49
  97.9 0.7 reshape.109.refs_3_
  98.6 0.6 broadcast_in_dim.112.refs_4_
  99.3 0.6 broadcast_in_dim.113.refs_5_
  99.9 302.7 %shard_map.222 = (bf16[2048,512]{1,0:T(8,128)(2,1)}, bf16[1664,512]{1,0:T(8,128)(2,1)}, bf16[2,2048,512]{2,1,0:T(8,128)(2,1)}, bf16[2048,512]{1,0:T(8,128)(2,1)}...) custom-call(bf16[4,256,2048]{2,1,0:T(8,128)(2,1)} %get-tuple-element, ...), custom_call_target="tpu_custom_call" | custom-call | flops 35000000512 | bytes 600000000 | tf_op jit(solution)/shard_map/pallas_call | solution.py:698
  402.5 420.8 %shard_map.223 = (f32[256,2048]{1,0:T(8,128)}, f32[256,2048]{1,0:T(8,128)}, f32[8,2048]{1,0:T(8,128)}, bf16[6,4,2,256,640]{4,3,2,1,0:T(8,128)(2,1)}, bf16[6,4,25...) custom-call(bf16[4,256,2048]{2,1,0:T(8,128)(2,1)} %get-tuple-element, ...), custom_call_target="tpu_custom_call" | custom-call | flops 74999996416 | bytes 800000000 | tf_op jit(solution)/shard_map/pallas_call | solution.py:1192
  823.3 1.4 select_reduce_fusion.3
  824.8 0.8 reshape.110
  825.6 3.5 all-to-all-start
  829.1 0.0 copy-start
  829.1 2.6 fusion
  831.7 6.0 select_reduce_fusion
  837.7 0.0 copy-done
  837.7 1.9 select_reduce_fusion.1
  839.6 1.5 fusion.1
  841.1 1.3 constant_dynamic-slice_fusion
  842.5 1.5 copy.38
  843.9 1.0 copy.37
  844.9 1.0 copy.36
  845.9 0.0 copy-start.2
  845.9 3.3 select_reduce_fusion.2
  849.2 0.0 all-to-all-done
  849.2 0.3 copy.35
  849.5 0.1 pad.10
  849.6 0.0 copy-start.1
  849.6 0.9 copy.41
  850.5 0.0 copy-done.2
  850.5 1.3 copy.47
  851.8 0.0 copy-done.1
  851.8 1.3 copy.48
  (2 shorter events, 0.0 us)
Async XLA Ops:
  5.7 3.1 copy-start.4
  9.0 0.8 copy-start.3
  825.6 23.7 %all-to-all-start = ((f32[4,52,512]{2,1,0:T(8,128)}), f32[4,52,512]{2,1,0:T(8,128)S(1)}, u32[]{:S(2)}, u32[]{:S(2)}) async-start(f32[4,52,512]{2,1,0:T(8,128)} %reshape.110), calls=%async_computation | async-start | bytes 917504 | tf_op jit(solution)/shard_map/all_to_all | solution.py:1270
  829.1 8.7 %copy-start = (bf16[8,5,256,512]{3,2,1,0:T(8,128)(2,1)S(1)}, bf16[8,5,256,512]{3,2,1,0:T(8,128)(2,1)}, u32[]{:S(2)}) copy-start(bf16[8,5,256,512]{3,2,1,0:T(8,128)(2,1)} %get-tuple-element.80) | copy-start | bytes 31457284
  845.9 4.6 copy-start.2
  849.6 2.2 copy-start.1
